TPU v7x, 256 devices: a whole 4x4x8 slice. The times are simulated.
256 devices in a mesh: row: 16 (over z, x_lo), col: 16 (over y, x_hi, core).
Axes of the slice: x: 4 (x_hi: 2, x_lo: 2; x = x_hi * 2 + x_lo), y: 4, z: 8, core: 2. Of those that a mesh axis runs over, the one named last changes fastest.
Arguments:
- fraction: float32 [128, 128, 2048], P('row', 'col'), may hold values from 0 to 1
- flow_x: float32 [128, 128, 2048], P('row', 'col'), may hold values from -0.4 to 0.4
- flow_y: float32 [128, 128, 2048], P('row', 'col'), may hold values from -0.4 to 0.4
- flow_z: float32 [128, 128, 2048], P('row', 'col'), may hold values from -0.4 to 0.4
Outputs:
- advected: float32 [128, 128, 2048], P('row', 'col')
All inputs are finite; a program needn't handle non-finite values.
Results may differ from a plain program's by a relative error of at most 0.0003.
Values sent between devices are 32-bit elements; how exact they have to be, the bound alone decides.
No kernel may reach another device: no remote copies, remote signals or barrier semaphores. Data moves between devices by JAX's collectives and lax.ppermute only.
A program may use at most 64 MiB of HBM per device.

v0:
```python
import jax
import jax.numpy as jnp
from jax import lax
from jax.sharding import PartitionSpec as P


def face_flux(field, courant, direction):
    normal = jnp.roll(field, -1, direction) - jnp.roll(field, 1, direction)
    field_below = jnp.roll(field, 1, direction)
    normal_below = jnp.roll(normal, 1, direction)
    forward = courant >= 0.0
    donor_value = jnp.where(forward, field_below, field)
    slope_side = jnp.where(forward, normal_below, -normal)
    reach = jnp.abs(courant)
    weight = jax.nn.sigmoid(20.0 * slope_side)
    volume = weight * jnp.minimum(donor_value, reach) + (1.0 - weight) * jnp.maximum(
        0.0, reach - 1.0 + donor_value
    )
    return jnp.where(forward, volume, -volume)


def advance(field, courant, indicator, direction):
    flux = face_flux(field, courant, direction)
    outflow = jnp.roll(flux, -1, direction) - flux
    spread = jnp.roll(courant, -1, direction) - courant
    return field - outflow + indicator * spread


def marked(start_field):
    return jnp.where(start_field > 0.5, 1.0, 0.0).astype(start_field.dtype)


def per_device(fraction, flow_x, flow_y, flow_z):
    first = advance(fraction, flow_x, marked(fraction), 2)
    row_first, row_start, row_flow_y, row_flow_z = (
        lax.all_to_all(first, "row", split_axis=2, concat_axis=0, tiled=True),
        lax.all_to_all(fraction, "row", split_axis=2, concat_axis=0, tiled=True),
        lax.all_to_all(flow_y, "row", split_axis=2, concat_axis=0, tiled=True),
        lax.all_to_all(flow_z, "row", split_axis=2, concat_axis=0, tiled=True),
    )
    second = advance(row_first, row_flow_y, marked(row_start), 0)
    col_second, col_start, col_flow_z = (
        lax.all_to_all(second, "col", split_axis=0, concat_axis=1, tiled=True),
        lax.all_to_all(row_start, "col", split_axis=0, concat_axis=1, tiled=True),
        lax.all_to_all(row_flow_z, "col", split_axis=0, concat_axis=1, tiled=True),
    )
    third = advance(col_second, col_flow_z, marked(col_start), 1)
    partway = lax.all_to_all(third, "col", split_axis=1, concat_axis=0, tiled=True)
    return lax.all_to_all(partway, "row", split_axis=0, concat_axis=2, tiled=True)


def solution(mesh):
    in_specs = (
        P("row", "col", None),
        P("row", "col", None),
        P("row", "col", None),
        P("row", "col", None),
    )
    out_specs = P("row", "col", None)
    return jax.shard_map(
        per_device, mesh=mesh, in_specs=in_specs, out_specs=out_specs, check_vma=False
    )
```

profile of v0, /device:TPU:2, one launch (start us, length us, event | category | flops | bytes accessed | tf_op | source)
XLA Modules:
  0.0 233.0 jit_solution(5897233541763343166)
XLA Ops:
  0.0 1.5 fusion.29
  1.5 0.9 fusion.28
  2.4 0.2 maximum_subtract_fusion
  2.6 0.1 slice.138
  2.6 1.7 negate_select_fusion.2
  4.3 0.2 slice.140
  4.5 0.2 slice.116
  4.7 0.0 copy-done
  4.8 0.2 fusion.6
  5.0 0.0 copy-start.5
  5.0 4.6 %copy.125 = f32[8,8,2048]{1,0,2:T(8,128)} copy(f32[8,8,2048]{2,1,0:T(8,128)S(1)} %fusion.6) | data formatting | bytes 1048576 | tf_op jit(solution)/shard_map/add | solution.py:26
  9.6 7.3 %reshape.10 = f32[16,1,8192]{2,1,0:T(1,128)} reshape(f32[2048,8,8]{2,1,0:T(8,128)} %bitcast.71) | data formatting | bytes 1048576
  16.9 9.9 %all-to-all-start = ((f32[16,1,8192]{2,1,0:T(1,128)}), f32[16,1,8192]{2,1,0:T(1,128)S(1)}, u32[]{:S(2)}, u32[]{:S(2)}) async-start(f32[16,1,8192]{2,1,0:T(1,128)} %reshape.10), calls=%async_computation | async-start | bytes 1048576 | tf_op jit(solution)/shard_map/all_to_all | solution.py:36
  26.9 4.6 %copy.128 = f32[8,8,2048]{1,0,2:T(8,128)} copy(f32[8,8,2048]{2,1,0:T(8,128)S(1)} %copy-done.5) | data formatting | bytes 1048576 | tf_op args[2]
  31.5 7.3 %reshape.12 = f32[16,1,8192]{2,1,0:T(1,128)} reshape(f32[2048,8,8]{2,1,0:T(8,128)} %bitcast.76) | data formatting | bytes 1048576
  38.8 3.4 %all-to-all-done = f32[16,1,8192]{2,1,0:T(1,128)S(1)} async-done(((f32[16,1,8192]{2,1,0:T(1,128)}), f32[16,1,8192]{2,1,0:T(1,128)S(1)}, u32[]{:S(2)}, u32[]{:S(2)}) %all-to-all-start) | async-done | bytes 524320 | tf_op jit(solution)/shard_map/all_to_all | solution.py:36
  42.2 5.3 %all-to-all-start.1 = ((f32[16,1,8192]{2,1,0:T(1,128)}), f32[16,1,8192]{2,1,0:T(1,128)S(1)}, u32[]{:S(2)}, u32[]{:S(2)}) async-start(f32[16,1,8192]{2,1,0:T(1,128)} %reshape.12), calls=%async_computation.1 | async-start | bytes 1048576 | tf_op jit(solution)/shard_map/all_to_all | solution.py:38
  47.5 4.6 %copy.131 = f32[8,8,2048]{1,0,2:T(8,128)} copy(f32[8,8,2048]{2,1,0:T(8,128)S(1)} %copy-done) | data formatting | bytes 1048576 | tf_op args[0]
  52.1 7.3 %reshape.14 = f32[16,1,8192]{2,1,0:T(1,128)} reshape(f32[2048,8,8]{2,1,0:T(8,128)} %bitcast.77) | data formatting | bytes 1048576
  59.4 3.4 %all-to-all-done.1 = f32[16,1,8192]{2,1,0:T(1,128)S(1)} async-done(((f32[16,1,8192]{2,1,0:T(1,128)}), f32[16,1,8192]{2,1,0:T(1,128)S(1)}, u32[]{:S(2)}, u32[]{:S(2)}) %all-to-all-start.1) | async-done | bytes 524320 | tf_op jit(solution)/shard_map/all_to_all | solution.py:38
  62.8 5.1 %all-to-all-start.2 = ((f32[16,1,8192]{2,1,0:T(1,128)}), f32[16,1,8192]{2,1,0:T(1,128)S(1)}, u32[]{:S(2)}, u32[]{:S(2)}) async-start(f32[16,1,8192]{2,1,0:T(1,128)} %reshape.14), calls=%async_computation.2 | async-start | bytes 1048576 | tf_op jit(solution)/shard_map/all_to_all | solution.py:37
  67.9 4.6 %copy.135 = f32[8,8,2048]{1,0,2:T(8,128)} copy(f32[8,8,2048]{2,1,0:T(8,128)S(1)} %copy-done.6) | data formatting | bytes 1048576 | tf_op args[3]
  72.5 7.3 %reshape.16 = f32[16,1,8192]{2,1,0:T(1,128)} reshape(f32[2048,8,8]{2,1,0:T(8,128)} %bitcast.78) | data formatting | bytes 1048576
  79.8 0.5 broadcast.69
  80.4 1.9 reduce
  82.2 6.6 %reshape.11 = f32[2048,8,8]{2,1,0:T(8,128)} reshape(f32[16,8192]{1,0:T(8,128)S(1)} %reduce) | data formatting | bytes 1048576
  88.9 5.1 %copy.127 = f32[16,8,8,128]{3,2,1,0:T(8,128)S(1)} copy(f32[16,8,8,128]{2,1,3,0:T(8,128)} %bitcast.72) | data formatting | bytes 1048576 | tf_op jit(solution)/shard_map/all_to_all | solution.py:36
  94.0 0.0 all-to-all-done.2
  94.0 0.0 copy-start.2
  94.0 8.2 %all-to-all-start.4 = ((f32[16,1,8192]{2,1,0:T(1,128)}), f32[16,1,8192]{2,1,0:T(1,128)S(1)}, u32[]{:S(2)}, u32[]{:S(2)}) async-start(f32[16,1,8192]{2,1,0:T(1,128)} %reshape.16), calls=%async_computation.4 | async-start | bytes 1048576 | tf_op jit(solution)/shard_map/all_to_all | solution.py:39
  102.2 0.1 fusion.27
  102.3 0.0 copy-done.2
  102.3 0.1 maximum_subtract_fusion.3
  102.4 0.8 slice.147
  103.2 1.9 reduce.1
  105.1 6.6 %reshape.13 = f32[2048,8,8]{2,1,0:T(8,128)} reshape(f32[16,8192]{1,0:T(8,128)S(1)} %reduce.1) | data formatting | bytes 1048576
  111.7 5.1 %copy.130 = f32[16,8,8,128]{3,2,1,0:T(8,128)S(1)} copy(f32[16,8,8,128]{2,1,3,0:T(8,128)} %bitcast.73) | data formatting | bytes 1048576 | tf_op jit(solution)/shard_map/all_to_all | solution.py:38
  116.8 1.4 negate_select_fusion.1
  118.3 0.8 slice.148
  119.1 0.8 slice.150
  120.0 2.9 %reduce.2 = f32[16,8192]{1,0:T(8,128)S(1)} reduce(f32[16,1,8192]{2,1,0:T(1,128)} %copy-done.2, f32[]{:T(128)} %broadcast.69), dimensions={1}, to_apply=%all_to_all.119.reduce_sub_computation | reduce | bytes 1048580 | tf_op jit(solution)/shard_map/all_to_all | solution.py:37
  122.9 6.6 %reshape.15 = f32[2048,8,8]{2,1,0:T(8,128)} reshape(f32[16,8192]{1,0:T(8,128)S(1)} %reduce.2) | data formatting | bytes 1048576
  129.5 5.9 %copy.133 = f32[16,8,8,128]{3,2,1,0:T(8,128)} copy(f32[16,8,8,128]{2,1,3,0:T(8,128)} %bitcast.74) | data formatting | bytes 1048576 | tf_op jit(solution)/shard_map/all_to_all | solution.py:37
  135.5 0.0 copy-done.4
  135.5 2.0 fusion.14
  137.5 0.0 all-to-all-done.4
  137.5 6.1 %all-to-all-start.3 = ((f32[128,8,128]{2,1,0:T(8,128)}), f32[128,8,128]{2,1,0:T(8,128)S(1)}, u32[]{:S(2)}, u32[]{:S(2)}) async-start(f32[128,8,128]{2,1,0:T(8,128)} %fusion.14), calls=%async_computation.3 | async-start | bytes 1048576 | tf_op jit(solution)/shard_map/all_to_all | solution.py:43
  143.7 1.9 reduce.3
  145.5 6.6 %reshape.17 = f32[2048,8,8]{2,1,0:T(8,128)} reshape(f32[16,8192]{1,0:T(8,128)S(1)} %reduce.3) | data formatting | bytes 1048576
  152.2 5.8 %copy.137 = f32[16,8,8,128]{3,2,1,0:T(8,128)} copy(f32[16,8,8,128]{2,1,3,0:T(8,128)} %bitcast.75) | data formatting | bytes 1048576 | tf_op jit(solution)/shard_map/all_to_all | solution.py:39
  158.0 0.0 all-to-all-done.3
  158.0 7.2 %all-to-all-start.5 = ((f32[128,8,128]{2,1,0:T(8,128)}), f32[128,8,128]{2,1,0:T(8,128)S(1)}, u32[]{:S(2)}, u32[]{:S(2)}) async-start(f32[128,8,128]{2,1,0:T(8,128)} %bitcast.20), calls=%async_computation.5 | async-start | bytes 1048576 | tf_op jit(solution)/shard_map/all_to_all | solution.py:45
  165.3 0.1 fusion.25
  165.4 12.2 %all-to-all-done.5 = f32[128,8,128]{2,1,0:T(8,128)S(1)} async-done(((f32[128,8,128]{2,1,0:T(8,128)}), f32[128,8,128]{2,1,0:T(8,128)S(1)}, u32[]{:S(2)}, u32[]{:S(2)}) %all-to-all-start.5) | async-done | bytes 524320 | tf_op jit(solution)/shard_map/all_to_all | solution.py:45
  177.6 3.6 %all-to-all-start.6 = ((f32[128,8,128]{2,1,0:T(8,128)}), f32[128,8,128]{2,1,0:T(8,128)S(1)}, u32[]{:S(2)}, u32[]{:S(2)}) async-start(f32[128,8,128]{2,1,0:T(8,128)} %bitcast.13), calls=%async_computation.6 | async-start | bytes 1048576 | tf_op jit(solution)/shard_map/all_to_all | solution.py:44
  181.2 0.1 maximum_subtract_fusion.6
  181.3 0.4 negate_select_fusion
  181.9 11.6 %all-to-all-done.6 = f32[128,8,128]{2,1,0:T(8,128)S(1)} async-done(((f32[128,8,128]{2,1,0:T(8,128)}), f32[128,8,128]{2,1,0:T(8,128)S(1)}, u32[]{:S(2)}, u32[]{:S(2)}) %all-to-all-start.6) | async-done | bytes 524320 | tf_op jit(solution)/shard_map/all_to_all | solution.py:44
  193.6 0.2 fusion.22
  193.8 0.3 copy.140
  194.1 15.0 %all_to_all.153 = f32[8,128,128]{2,0,1:T(8,128)S(1)} all-to-all(f32[8,128,128]{2,0,1:T(8,128)S(1)} %copy.140), channel_id=1, replica_groups=mesh['row'=16,'col'=16] {'col'}, dimensions={1} | all-to-all | bytes 1048576 | tf_op jit(solution)/shard_map/all_to_all | solution.py:48
  209.1 0.1 copy.142
  209.2 23.0 %all_to_all.154 = f32[128,8,128]{2,1,0:T(8,128)S(1)} all-to-all(f32[128,8,128]{2,1,0:T(8,128)S(1)} %bitcast.97), channel_id=1, replica_groups=mesh['row'=16,'col'=16] {'row'}, dimensions={0} | all-to-all | bytes 1048576 | tf_op jit(solution)/shard_map/all_to_all | solution.py:49
  232.2 0.8 copy.166
  (25 shorter events, 0.3 us)
Async XLA Ops:
  0.0 4.7 %copy-start = (f32[8,8,2048]{2,1,0:T(8,128)S(1)}, f32[8,8,2048]{2,1,0:T(8,128)}, u32[]{:S(2)}) copy-start(f32[8,8,2048]{2,1,0:T(8,128)} %param.4) | copy-start | bytes 1572868
  0.0 4.5 %copy-start.1 = (f32[8,8,2048]{2,1,0:T(8,128)S(1)}, f32[8,8,2048]{2,1,0:T(8,128)}, u32[]{:S(2)}) copy-start(f32[8,8,2048]{2,1,0:T(8,128)} %param.5) | copy-start | bytes 1572868
  0.0 4.7 %slice-start = ((f32[8,8,2048]{2,1,0:T(8,128)}), f32[8,8,1]{2,1,0:T(8,128)S(1)}, s32[]{:S(2)}) async-start(f32[8,8,2048]{2,1,0:T(8,128)} %param.5), calls=%async_computation.9 | async-start | bytes 65536 | tf_op jit(solution)/shard_map/jit(_roll_static)/slice | solution.py:25
  5.0 21.9 %copy-start.5 = (f32[8,8,2048]{2,1,0:T(8,128)S(1)}, f32[8,8,2048]{2,1,0:T(8,128)}, u32[]{:S(2)}) copy-start(f32[8,8,2048]{2,1,0:T(8,128)} %param.6) | copy-start | bytes 1572868
  16.9 25.3 %all-to-all-start = ((f32[16,1,8192]{2,1,0:T(1,128)}), f32[16,1,8192]{2,1,0:T(1,128)S(1)}, u32[]{:S(2)}, u32[]{:S(2)}) async-start(f32[16,1,8192]{2,1,0:T(1,128)} %reshape.10), calls=%async_computation | async-start | bytes 1048576 | tf_op jit(solution)/shard_map/all_to_all | solution.py:36
  42.2 20.6 %all-to-all-start.1 = ((f32[16,1,8192]{2,1,0:T(1,128)}), f32[16,1,8192]{2,1,0:T(1,128)S(1)}, u32[]{:S(2)}, u32[]{:S(2)}) async-start(f32[16,1,8192]{2,1,0:T(1,128)} %reshape.12), calls=%async_computation.1 | async-start | bytes 1048576 | tf_op jit(solution)/shard_map/all_to_all | solution.py:38
  47.5 20.5 %copy-start.6 = (f32[8,8,2048]{2,1,0:T(8,128)S(1)}, f32[8,8,2048]{2,1,0:T(8,128)}, u32[]{:S(2)}) copy-start(f32[8,8,2048]{2,1,0:T(8,128)} %param.7) | copy-start | bytes 1572868
  62.8 31.2 %all-to-all-start.2 = ((f32[16,1,8192]{2,1,0:T(1,128)}), f32[16,1,8192]{2,1,0:T(1,128)S(1)}, u32[]{:S(2)}, u32[]{:S(2)}) async-start(f32[16,1,8192]{2,1,0:T(1,128)} %reshape.14), calls=%async_computation.2 | async-start | bytes 1048576 | tf_op jit(solution)/shard_map/all_to_all | solution.py:37
  94.0 8.3 %copy-start.2 = (f32[16,1,8192]{2,1,0:T(1,128)}, f32[16,1,8192]{2,1,0:T(1,128)S(1)}, u32[]{:S(2)}) copy-start(f32[16,1,8192]{2,1,0:T(1,128)S(1)} %all-to-all-done.2) | copy-start | bytes 1572868
  94.0 43.5 %all-to-all-start.4 = ((f32[16,1,8192]{2,1,0:T(1,128)}), f32[16,1,8192]{2,1,0:T(1,128)S(1)}, u32[]{:S(2)}, u32[]{:S(2)}) async-start(f32[16,1,8192]{2,1,0:T(1,128)} %reshape.16), calls=%async_computation.4 | async-start | bytes 1048576 | tf_op jit(solution)/shard_map/all_to_all | solution.py:39
  129.5 5.9 %copy-start.3 = (f32[127,8,128]{2,1,0:T(8,128)S(1)}, f32[127,8,128]{2,1,0:T(8,128)}, u32[]{:S(2)}) copy-start(f32[127,8,128]{2,1,0:T(8,128)} %slice.148) | copy-start | bytes 1560580
  129.5 5.9 %copy-start.4 = (f32[127,8,128]{2,1,0:T(8,128)S(1)}, f32[127,8,128]{2,1,0:T(8,128)}, u32[]{:S(2)}) copy-start(f32[127,8,128]{2,1,0:T(8,128)} %slice.150) | copy-start | bytes 1560580
  137.5 20.5 %all-to-all-start.3 = ((f32[128,8,128]{2,1,0:T(8,128)}), f32[128,8,128]{2,1,0:T(8,128)S(1)}, u32[]{:S(2)}, u32[]{:S(2)}) async-start(f32[128,8,128]{2,1,0:T(8,128)} %fusion.14), calls=%async_computation.3 | async-start | bytes 1048576 | tf_op jit(solution)/shard_map/all_to_all | solution.py:43
  158.0 19.6 %all-to-all-start.5 = ((f32[128,8,128]{2,1,0:T(8,128)}), f32[128,8,128]{2,1,0:T(8,128)S(1)}, u32[]{:S(2)}, u32[]{:S(2)}) async-start(f32[128,8,128]{2,1,0:T(8,128)} %bitcast.20), calls=%async_computation.5 | async-start | bytes 1048576 | tf_op jit(solution)/shard_map/all_to_all | solution.py:45
  177.6 15.9 %all-to-all-start.6 = ((f32[128,8,128]{2,1,0:T(8,128)}), f32[128,8,128]{2,1,0:T(8,128)S(1)}, u32[]{:S(2)}, u32[]{:S(2)}) async-start(f32[128,8,128]{2,1,0:T(8,128)} %bitcast.13), calls=%async_computation.6 | async-start | bytes 1048576 | tf_op jit(solution)/shard_map/all_to_all | solution.py:44
where the time goes:
time: 235 us; the launch traced here: 233 us
  local copies, waits for them, and re-layouts  104 us (44%)
  starting transfers between devices  45.5 us (19%)
  blocking collectives  38 us (16%)
  waiting for transfers between devices  30.7 us (13%)
  other arithmetic  15 us (6%)
    unnamed x25, local copies, waits for them, and re-layouts  69.5 us
    all_to_all x1, blocking collectives, per_device(): lax.all_to_all(partway, 'row', split_axis=0, concat_axis=2, tiled=True)  23 us
    all_to_all x1, blocking collectives, per_device(): lax.all_to_all(third, 'col', split_axis=1, concat_axis=0, tiled=True)  15 us
    all_to_all x1, waiting for transfers between devices, per_device(): lax.all_to_all(row_flow_z, 'col', split_axis=0, concat_axis=1, tiled=True)  12.2 us
    all_to_all x1, waiting for transfers between devices, per_device(): lax.all_to_all(row_start, 'col', split_axis=0, concat_axis=1, tiled=True)  11.6 us
    all_to_all x1, starting transfers between devices, per_device(): lax.all_to_all(first, 'row', split_axis=2, concat_axis=0, tiled=True)  9.94 us
    all_to_all x1, starting transfers between devices, per_device(): lax.all_to_all(flow_z, 'row', split_axis=2, concat_axis=0, tiled=True)  8.19 us
    all_to_all x1, starting transfers between devices, per_device(): lax.all_to_all(row_flow_z, 'col', split_axis=0, concat_axis=1, tiled=True)  7.22 us
  transfers between devices with their start and end apart: 7, of which 4 were waited for; matrix products, arithmetic and copies ran while one was open for 43% of the time, Pallas kernels for 0%

commit v1 on v0

v1 whole, which is shorter than its diff:
```python
import jax
import jax.numpy as jnp
from jax import lax
from jax.experimental import pallas as pl
from jax.experimental.pallas import tpu as pltpu
from jax.sharding import PartitionSpec as P


def face_flux(two_below, below, here, above, courant):
    forward = courant >= 0.0
    donor = jnp.where(forward, below, here)
    slope = jnp.where(forward, here - two_below, below - above)
    reach = jnp.abs(courant)
    least = jnp.minimum(donor, reach)
    most = jnp.maximum(0.0, reach - 1.0 + donor)
    tilt = jnp.tanh(10.0 * slope)
    volume = 0.5 * ((least + most) + tilt * (least - most))
    return jnp.where(forward, volume, -volume)


def updated(here, flux, next_flux, courant, next_courant, start):
    spread = jnp.where(start > 0.5, next_courant - courant, 0.0)
    return here - (next_flux - flux) + spread


def x_sweep(fraction, flow_x, flow_y, first, upward, downward):
    rows, _, length = fraction.shape

    def row(i, _):
        here = fraction[i]
        courant = flow_x[i]
        below = pltpu.roll(here, 1, 1)
        two_below = pltpu.roll(here, 2, 1)
        above = pltpu.roll(here, length - 1, 1)
        flux = face_flux(two_below, below, here, above, courant)
        first[i] = updated(
            here,
            flux,
            pltpu.roll(flux, length - 1, 1),
            courant,
            pltpu.roll(courant, length - 1, 1),
            here,
        )
        return _

    lax.fori_loop(0, rows, row, None)
    upward[...] = first[rows - 2 :]
    downward[:2] = first[:2]
    downward[2] = flow_y[0]


def y_sweep(first, flow_y, fraction, flow_z, lower, upper, second, upward, downward):
    rows, columns, length = first.shape

    def tile(t, _):
        at = pl.ds(pl.multiple_of(t * 128, 128), 128)
        cells = (
            [lower[0, :, at], lower[1, :, at]]
            + [first[i, :, at] for i in range(rows)]
            + [upper[0, :, at], upper[1, :, at]]
        )
        flows = [flow_y[i, :, at] for i in range(rows)] + [upper[2, :, at]]
        flux = face_flux(*cells[:4], flows[0])
        for i in range(rows):
            next_flux = face_flux(*cells[i + 1 : i + 5], flows[i + 1])
            result = updated(
                cells[i + 2], flux, next_flux, flows[i], flows[i + 1], fraction[i, :, at]
            )
            flux = next_flux
            second[i, :, at] = result
            upward[0, i : i + 1, at] = result[columns - 2 : columns - 1]
            upward[1, i : i + 1, at] = result[columns - 1 :]
            downward[0, i : i + 1, at] = result[:1]
            downward[1, i : i + 1, at] = result[1:2]
            downward[2, i : i + 1, at] = flow_z[i, :1, at]
        return _

    lax.fori_loop(0, length // 128, tile, None)


def z_sweep(second, flow_z, fraction, own, lower, upper, out, last_flux):
    rows, columns, length = second.shape
    chunk = 512
    place = lax.broadcasted_iota(jnp.int32, (columns, chunk), 0)
    bottom = place == 0
    top = place == columns - 1

    for k in range(length // chunk):
        at = slice(k * chunk, (k + 1) * chunk)
        last_flux[:, at] = face_flux(
            own[0, :, at], own[1, :, at], upper[0, :, at], upper[1, :, at], upper[2, :, at]
        )

    for k in range(length // chunk):
        at = slice(k * chunk, (k + 1) * chunk)
        for i in range(rows):
            here = second[i, :, at]
            courant = flow_z[i, :, at]
            below = jnp.where(bottom, lower[1, i : i + 1, at], pltpu.roll(here, 1, 0))
            two_below = jnp.where(bottom, lower[0, i : i + 1, at], pltpu.roll(below, 1, 0))
            above = jnp.where(top, upper[0, i : i + 1, at], pltpu.roll(here, columns - 1, 0))
            flux = face_flux(two_below, below, here, above, courant)
            next_flux = jnp.where(top, last_flux[i : i + 1, at], pltpu.roll(flux, columns - 1, 0))
            next_courant = jnp.where(
                top, upper[2, i : i + 1, at], pltpu.roll(courant, columns - 1, 0)
            )
            out[i, :, at] = updated(
                here, flux, next_flux, courant, next_courant, fraction[i, :, at]
            )


def in_vmem(n):
    return [pl.BlockSpec(memory_space=pltpu.VMEM)] * n


def per_device(n_row, n_col, fraction, flow_x, flow_y, flow_z):
    block, dtype = fraction.shape, fraction.dtype
    rows, columns, length = block
    whole = jax.ShapeDtypeStruct(block, dtype)
    params = pltpu.CompilerParams(vmem_limit_bytes=32 * 1024 * 1024)

    def slabs(n, width):
        return jax.ShapeDtypeStruct((n, width, length), dtype)

    up = lambda n: [(i, (i + 1) % n) for i in range(n)]
    down = lambda n: [(i, (i - 1) % n) for i in range(n)]

    first, upward, downward = pl.pallas_call(
        x_sweep,
        out_shape=(whole, slabs(2, columns), slabs(3, columns)),
        in_specs=in_vmem(3),
        out_specs=in_vmem(3),
        compiler_params=params,
    )(fraction, flow_x, flow_y)
    lower = lax.ppermute(upward, "row", up(n_row))
    upper = lax.ppermute(downward, "row", down(n_row))
    second, upward, downward = pl.pallas_call(
        y_sweep,
        out_shape=(whole, slabs(2, rows), slabs(3, rows)),
        in_specs=in_vmem(6),
        out_specs=in_vmem(3),
        compiler_params=params,
    )(first, flow_y, fraction, flow_z, lower, upper)
    lower = lax.ppermute(upward, "col", up(n_col))
    upper = lax.ppermute(downward, "col", down(n_col))
    return pl.pallas_call(
        z_sweep,
        out_shape=whole,
        in_specs=in_vmem(6),
        out_specs=pl.BlockSpec(memory_space=pltpu.VMEM),
        scratch_shapes=[pltpu.VMEM((rows, length), dtype)],
        compiler_params=params,
    )(second, flow_z, fraction, upward, lower, upper)


def solution(mesh):
    spec = P("row", "col", None)

    def step(fraction, flow_x, flow_y, flow_z):
        return per_device(
            mesh.shape["row"], mesh.shape["col"], fraction, flow_x, flow_y, flow_z
        )

    return jax.shard_map(
        step, mesh=mesh, in_specs=(spec,) * 4, out_specs=spec, check_vma=False
    )
```

time: 235 us -> 30.7 us (0.13)
  the two profiles are of different devices: /device:TPU:2 before, /device:TPU:0 now
where the time goes in v1:
time: 30.7 us; the launch traced here: 30.5 us
  waiting for transfers between devices  15.1 us (49%)
  starting transfers between devices  8.4 us (27%)
  Pallas kernels  3.86 us (13%)
  local copies, waits for them, and re-layouts  3.13 us (10%)
    ppermute x1, waiting for transfers between devices, per_device(): lower = lax.ppermute(upward, 'col', up(n_col))  8 us
    ppermute x1, waiting for transfers between devices, per_device(): lower = lax.ppermute(upward, 'row', up(n_row))  7.07 us
    ppermute x1, starting transfers between devices, per_device(): upper = lax.ppermute(downward, 'row', down(n_row))  5.12 us
    ppermute x1, starting transfers between devices, per_device(): upper = lax.ppermute(downward, 'col', down(n_col))  3.27 us
    unnamed x10, local copies, waits for them, and re-layouts  3.13 us
    pallas_call x1, Pallas kernels, per_device(): pl.pallas_call(x_sweep, out_shape=(whole, slabs(2, columns), slabs(3, col...  1.7 us
    pallas_call x1, Pallas kernels, per_device(): pl.pallas_call(z_sweep, out_shape=whole, in_specs=in_vmem(6), out_specs=p...  1.43 us
    pallas_call x1, Pallas kernels, per_device(): pl.pallas_call(y_sweep, out_shape=(whole, slabs(2, rows), slabs(3, rows))...  0.73 us
  transfers between devices with their start and end apart: 4, of which 2 were waited for; matrix products, arithmetic and copies ran while one was open for 0% of the time, Pallas kernels for 0%

profile of v1, /device:TPU:0, one launch (start us, length us, event | category | flops | bytes accessed | tf_op | source)
XLA Modules:
  0.0 30.5 jit_solution(14295732895221791572)
XLA Ops:
  0.0 0.0 copy-start
  0.0 1.0 %copy-done = f32[8,8,2048]{2,1,0:T(8,128)S(1)} copy-done((f32[8,8,2048]{2,1,0:T(8,128)S(1)}, f32[8,8,2048]{2,1,0:T(8,128)}, u32[]{:S(2)}) %copy-start) | copy-done | bytes 524312
  1.0 0.0 copy-start.1
  1.0 1.0 %copy-done.1 = f32[8,8,2048]{2,1,0:T(8,128)S(1)} copy-done((f32[8,8,2048]{2,1,0:T(8,128)S(1)}, f32[8,8,2048]{2,1,0:T(8,128)}, u32[]{:S(2)}) %copy-start.1) | copy-done | bytes 524312
  2.1 0.0 copy-start.4
  2.1 1.0 %copy-done.4 = f32[8,8,2048]{2,1,0:T(8,128)S(1)} copy-done((f32[8,8,2048]{2,1,0:T(8,128)S(1)}, f32[8,8,2048]{2,1,0:T(8,128)}, u32[]{:S(2)}) %copy-start.4) | copy-done | bytes 524312
  3.1 0.0 copy-start.2
  3.1 0.0 copy-start.3
  3.1 1.7 %shard_map.46 = (f32[8,8,2048]{2,1,0:T(8,128)S(1)}, f32[2,8,2048]{2,1,0:T(8,128)S(1)}, f32[3,8,2048]{2,1,0:T(8,128)S(1)}) custom-call(f32[8,8,2048]{2,1,0:T(8,128)S(1)} %copy-done, f32[8,8,2048]{2,1,0:T(8,128)S(1)} %copy-done.4, f32[8,8,2048]{2,1,0:T(8,128)S(1)} %copy-done.1), custom_call_target="tpu_custom_call" | custom-call | tf_op jit(solution)/shard_map/pallas_call | solution.py:128
  4.8 5.1 %collective-permute-start.1 = (f32[3,8,2048]{2,1,0:T(8,128)S(1)}, f32[3,8,2048]{2,1,0:T(8,128)S(1)}, u32[]{:S(2)}, u32[]{:S(2)}) collective-permute-start(f32[3,8,2048]{2,1,0:T(8,128)S(1)} %get-tuple-element.13), channel_id=1, source_target_pairs={{0,240},{16,0},{32,16},{48,32},{64,48},{80,64},{96,80},{112,96},{1... | collective-permute-start | bytes 589832 | tf_op jit(solution)/shard_map/ppermute | solution.py:136
  10.0 0.0 collective-permute-start
  10.0 7.1 %collective-permute-done.lower = f32[2,8,2048]{2,1,0:T(8,128)S(1)} collective-permute-done((f32[2,8,2048]{2,1,0:T(8,128)S(1)}, f32[2,8,2048]{2,1,0:T(8,128)S(1)}, u32[]{:S(2)}, u32[]{:S(2)}) %collective-permute-start) | collective-permute-done | bytes 131104 | tf_op jit(solution)/shard_map/ppermute | solution.py:135
  17.0 0.0 collective-permute-done.1.upper
  17.0 0.0 copy-done.2
  17.0 0.0 copy-done.3
  17.1 0.7 %shard_map.47 = (f32[8,8,2048]{2,1,0:T(8,128)S(1)}, f32[2,8,2048]{2,1,0:T(8,128)S(1)}, f32[3,8,2048]{2,1,0:T(8,128)S(1)}) custom-call(f32[8,8,2048]{2,1,0:T(8,128)S(1)} %get-tuple-element.11.first, f32[8,8,2048]{2,1,0:T(8,128)S(1)} %copy-done.2, f32[8,8,2048]{2,1,0:T(8,128)S(1)} %copy-done, f32[8,8,2048]{2,1,0:T(8,128)S(1)} %copy-done.3, ...), custom_call_target="tpu_custom_call" | custom-call | tf_op jit(solution)/shard_map/pallas_call | solution.py:137
  17.8 3.3 %collective-permute-start.3 = (f32[3,8,2048]{2,1,0:T(8,128)S(1)}, f32[3,8,2048]{2,1,0:T(8,128)S(1)}, u32[]{:S(2)}, u32[]{:S(2)}) collective-permute-start(f32[3,8,2048]{2,1,0:T(8,128)S(1)} %get-tuple-element.16), channel_id=1, source_target_pairs={{0,15},{1,0},{2,1},{3,2},{4,3},{5,4},{6,5},{7,6},{8,7},{9,8},{10,9... | collective-permute-start | bytes 589832 | tf_op jit(solution)/shard_map/ppermute | solution.py:145
  21.1 0.0 collective-permute-start.2
  21.1 8.0 %collective-permute-done.2.lower = f32[2,8,2048]{2,1,0:T(8,128)S(1)} collective-permute-done((f32[2,8,2048]{2,1,0:T(8,128)S(1)}, f32[2,8,2048]{2,1,0:T(8,128)S(1)}, u32[]{:S(2)}, u32[]{:S(2)}) %collective-permute-start.2) | collective-permute-done | bytes 131104 | tf_op jit(solution)/shard_map/ppermute | solution.py:144
  29.1 0.0 collective-permute-done.3.upper
  29.1 1.4 %shard_map.48 = f32[8,8,2048]{2,1,0:T(8,128)} custom-call(f32[8,8,2048]{2,1,0:T(8,128)S(1)} %get-tuple-element.14.second, f32[8,8,2048]{2,1,0:T(8,128)S(1)} %copy-done.3, f32[8,8,2048]{2,1,0:T(8,128)S(1)} %copy-done, f32[2,8,2048]{2,1,0:T(8,128)S(1)} %get-tuple-element.15.own, f32[2,8,2048]{2,1,0:T(8,128)S(1)} %collective-permute-done.2.lower, ...), custom_call_target="tpu_custom_call" | custom-call | tf_op jit(solution)/shard_map/pallas_call | solution.py:146
Async XLA Ops:
  0.0 1.0 %copy-start = (f32[8,8,2048]{2,1,0:T(8,128)S(1)}, f32[8,8,2048]{2,1,0:T(8,128)}, u32[]{:S(2)}) copy-start(f32[8,8,2048]{2,1,0:T(8,128)} %fraction.5) | copy-start | bytes 1572868
  1.0 1.0 %copy-start.1 = (f32[8,8,2048]{2,1,0:T(8,128)S(1)}, f32[8,8,2048]{2,1,0:T(8,128)}, u32[]{:S(2)}) copy-start(f32[8,8,2048]{2,1,0:T(8,128)} %flow_y.3) | copy-start | bytes 1572868
  2.1 1.0 %copy-start.4 = (f32[8,8,2048]{2,1,0:T(8,128)S(1)}, f32[8,8,2048]{2,1,0:T(8,128)}, u32[]{:S(2)}) copy-start(f32[8,8,2048]{2,1,0:T(8,128)} %flow_x.1) | copy-start | bytes 1572868
  3.1 13.9 %copy-start.2 = (f32[8,8,2048]{2,1,0:T(8,128)S(1)}, f32[8,8,2048]{2,1,0:T(8,128)}, u32[]{:S(2)}) copy-start(f32[8,8,2048]{2,1,0:T(8,128)} %flow_y.3) | copy-start | bytes 1572868
  3.1 13.9 %copy-start.3 = (f32[8,8,2048]{2,1,0:T(8,128)S(1)}, f32[8,8,2048]{2,1,0:T(8,128)}, u32[]{:S(2)}) copy-start(f32[8,8,2048]{2,1,0:T(8,128)} %flow_z.3) | copy-start | bytes 1572868
  4.8 12.2 %collective-permute-start.1 = (f32[3,8,2048]{2,1,0:T(8,128)S(1)}, f32[3,8,2048]{2,1,0:T(8,128)S(1)}, u32[]{:S(2)}, u32[]{:S(2)}) collective-permute-start(f32[3,8,2048]{2,1,0:T(8,128)S(1)} %get-tuple-element.13), channel_id=1, source_target_pairs={{0,240},{16,0},{32,16},{48,32},{64,48},{80,64},{96,80},{112,96},{1... | collective-permute-start | bytes 589832 | tf_op jit(solution)/shard_map/ppermute | solution.py:136
  10.0 7.1 %collective-permute-start = (f32[2,8,2048]{2,1,0:T(8,128)S(1)}, f32[2,8,2048]{2,1,0:T(8,128)S(1)}, u32[]{:S(2)}, u32[]{:S(2)}) collective-permute-start(f32[2,8,2048]{2,1,0:T(8,128)S(1)} %get-tuple-element.12), channel_id=1, source_target_pairs={{0,16},{16,32},{32,48},{48,64},{64,80},{80,96},{96,112},{112,128},... | collective-permute-start | bytes 393224 | tf_op jit(solution)/shard_map/ppermute | solution.py:135
  17.8 11.3 %collective-permute-start.3 = (f32[3,8,2048]{2,1,0:T(8,128)S(1)}, f32[3,8,2048]{2,1,0:T(8,128)S(1)}, u32[]{:S(2)}, u32[]{:S(2)}) collective-permute-start(f32[3,8,2048]{2,1,0:T(8,128)S(1)} %get-tuple-element.16), channel_id=1, source_target_pairs={{0,15},{1,0},{2,1},{3,2},{4,3},{5,4},{6,5},{7,6},{8,7},{9,8},{10,9... | collective-permute-start | bytes 589832 | tf_op jit(solution)/shard_map/ppermute | solution.py:145
  21.1 8.0 %collective-permute-start.2 = (f32[2,8,2048]{2,1,0:T(8,128)S(1)}, f32[2,8,2048]{2,1,0:T(8,128)S(1)}, u32[]{:S(2)}, u32[]{:S(2)}) collective-permute-start(f32[2,8,2048]{2,1,0:T(8,128)S(1)} %get-tuple-element.15.own), channel_id=1, source_target_pairs={{0,1},{1,2},{2,3},{3,4},{4,5},{5,6},{6,7},{7,8},{8,9},{9,10},{10,1... | collective-permute-start | bytes 393224 | tf_op jit(solution)/shard_map/ppermute | solution.py:144

commit v2 on v1

v2 whole, which is shorter than its diff:
```python
import jax
import jax.numpy as jnp
from jax import lax
from jax.experimental import pallas as pl
from jax.experimental.pallas import tpu as pltpu
from jax.sharding import PartitionSpec as P

LANES = 128


def face_flux(two_below, below, here, above, courant):
    forward = courant >= 0.0
    donor = jnp.where(forward, below, here)
    slope = jnp.where(forward, here - two_below, below - above)
    return donor_flux(forward, donor, slope, courant)


def donor_flux(forward, donor, slope, courant):
    reach = jnp.abs(courant)
    least = jnp.minimum(donor, reach)
    most = jnp.maximum(0.0, reach - 1.0 + donor)
    tilt = jnp.tanh(10.0 * slope)
    return jnp.where(forward, 0.5, -0.5) * ((least + most) + tilt * (least - most))


def updated(here, flux, next_flux, courant, next_courant, start):
    spread = jnp.where(start > 0.5, next_courant - courant, 0.0)
    return here - (next_flux - flux) + spread


def x_sweep_row(here, courant):
    length = here.shape[1]
    below = pltpu.roll(here, 1, 1)
    two_below = pltpu.roll(here, 2, 1)
    above = pltpu.roll(here, length - 1, 1)
    flux = face_flux(two_below, below, here, above, courant)
    from_below = flux - jnp.where(below > 0.5, courant, 0.0)
    to_above = flux - jnp.where(here > 0.5, courant, 0.0)
    return here + (to_above - pltpu.roll(from_below, length - 1, 1))


def x_far(fraction, flow_x, flow_y, flow_z, far, courant_y, courant_z, cells, flows, sems):
    far_row = lax.rem(lax.axis_index("row"), 2) * (fraction.shape[0] - 2)
    at = pl.ds(far_row, 2)
    loads = [
        pltpu.make_async_copy(source, into, sems.at[n])
        for n, (source, into) in enumerate(
            (
                (fraction.at[at], cells),
                (flow_x.at[at], flows),
                (flow_y.at[0], courant_y),
                (flow_z.at[:, 0], courant_z),
            )
        )
    ]
    for load in loads:
        load.start()
    loads[0].wait()
    loads[1].wait()
    for i in range(2):
        far[i] = x_sweep_row(cells[i], flows[i])
    loads[2].wait()
    loads[3].wait()


def x_near(fraction, flow_x, far, near):
    del far
    near_row = lax.rem(lax.axis_index("row") + 1, 2) * (fraction.shape[0] - 2)
    for i in range(2):
        near[i] = x_sweep_row(fraction[near_row + i], flow_x[near_row + i])


def x_middle(fraction, flow_x, near, flow_z, middle, inner_z, sems):
    del near
    loads = [
        pltpu.make_async_copy(flow_z.at[:, column], inner_z.at[n], sems.at[n])
        for n, column in enumerate((1, flow_z.shape[1] - 1))
    ]
    for load in loads:
        load.start()
    for i in range(middle.shape[0]):
        middle[i] = x_sweep_row(fraction[i + 2], flow_x[i + 2])
    for load in loads:
        load.wait()


def y_sweep(
    near, near_side, far, far_side, courant_y, middle, flow_y, fraction,
    second, core, chip,
):
    rows, columns, length = second.shape
    odd = lax.rem(lax.axis_index("row"), 2) == 1
    odd_core = lax.rem(lax.axis_index("col"), 2) == 1

    def tile(t, _):
        at = pl.ds(pl.multiple_of(t * LANES, LANES), LANES)

        def ordered(a, b):
            return lax.select(odd, a, b), lax.select(odd, b, a)

        below, above = zip(*(ordered(near_side[i, :, at], far_side[i, :, at]) for i in range(2)))
        low, high = zip(*(ordered(near[i, :, at], far[i, :, at]) for i in range(2)))
        cells = [*below, *low, *(middle[i, :, at] for i in range(rows - 4)), *high, *above]
        flows = [flow_y[i, :, at] for i in range(rows)] + [courant_y[:, at]]
        flux = face_flux(*cells[:4], flows[0])
        for i in range(rows):
            next_flux = face_flux(*cells[i + 1 : i + 5], flows[i + 1])
            result = updated(
                cells[i + 2], flux, next_flux, flows[i], flows[i + 1], fraction[i, :, at]
            )
            flux = next_flux
            second[i, :, at] = result
            for m in range(2):
                up, down = result[columns - 2 + m : columns - 1 + m], result[m : m + 1]
                core[m, i : i + 1, at] = lax.select(odd_core, down, up)
                chip[m, i : i + 1, at] = lax.select(odd_core, up, down)
        return _

    lax.fori_loop(0, length // LANES, tile, None, unroll=2)


CHUNK = 512


def z_inner(second, flow_z, fraction, courant_z, base, inner_cells):
    rows, columns, length = second.shape
    place = lax.broadcasted_iota(jnp.int32, (columns, CHUNK), 0)
    top = place == columns - 1
    inner = (place >= 2) & (place <= columns - 2)
    for i in range(rows):
        for j in range(length // CHUNK):
            at = slice(j * CHUNK, (j + 1) * CHUNK)
            here = second[i, :, at]
            courant = flow_z[i, :, at]
            flux = face_flux(
                pltpu.roll(here, 2, 0),
                pltpu.roll(here, 1, 0),
                here,
                pltpu.roll(here, columns - 1, 0),
                courant,
            )
            flux = jnp.where(inner, flux, 0.0)
            next_courant = jnp.where(
                top, courant_z[i : i + 1, at], pltpu.roll(courant, columns - 1, 0)
            )
            base[i, :, at] = updated(
                here, flux, pltpu.roll(flux, columns - 1, 0), courant, next_courant,
                fraction[i, :, at],
            )
            inner_cells[0, i : i + 1, at] = here[2:3]
            inner_cells[1, i : i + 1, at] = here[columns - 3 : columns - 2]


def z_outer(
    chip, chip_side, core, core_side, base, inner_cells, inner_z, own_z, courant_z, out,
    part, change, sems,
):
    rows, columns, length = base.shape
    odd_core = lax.rem(lax.axis_index("col"), 2) == 1
    place = lax.broadcasted_iota(jnp.int32, (columns, CHUNK), 0)
    pieces = [slice(j * CHUNK, (j + 1) * CHUNK) for j in range(length // CHUNK)]

    for at in pieces:

        def ordered(a, b, at=at):
            pairs = [(a[m, :, at], b[m, :, at]) for m in range(2)]
            return [lax.select(odd_core, x, y) for x, y in pairs], [
                lax.select(odd_core, y, x) for x, y in pairs
            ]

        below, above = ordered(core_side, chip_side)
        low, high = ordered(core, chip)
        after_low, before_high = inner_cells[0, :, at], inner_cells[1, :, at]
        flux = [
            face_flux(*below, *low, own_z[:, at]),
            face_flux(below[1], *low, after_low, inner_z[0, :, at]),
            face_flux(before_high, *high, above[0], inner_z[1, :, at]),
            face_flux(*high, *above, courant_z[:, at]),
        ]
        change[0, :, at] = flux[0] - flux[1]
        change[1, :, at] = flux[1]
        change[2, :, at] = -flux[2]
        change[3, :, at] = flux[2] - flux[3]

    stores = []
    for i in range(rows):
        for at in pieces:
            value = jnp.zeros((columns, CHUNK), base.dtype)
            for n, column in enumerate((0, 1, columns - 2, columns - 1)):
                value = jnp.where(place == column, change[n, i : i + 1, at], value)
            part[i, :, at] = base[i, :, at] + value
        stores.append(pltpu.make_async_copy(part.at[i], out.at[i], sems.at[i]))
        stores[-1].start()
    for store in stores:
        store.wait()


def per_device(n_row, n_col, fraction, flow_x, flow_y, flow_z):
    block, dtype = fraction.shape, fraction.dtype
    rows, columns, length = block
    vmem = pl.BlockSpec(memory_space=pltpu.VMEM)
    hbm = pl.BlockSpec(memory_space=pltpu.HBM)
    params = pltpu.CompilerParams(vmem_limit_bytes=16 * 1024 * 1024)
    dma = pltpu.SemaphoreType.DMA

    def array(*shape):
        return jax.ShapeDtypeStruct(shape, dtype)

    def with_above(n):
        return [(i, i ^ 1) for i in range(n)]

    def down(n):
        return [(i, (i - 1) % n) for i in range(n)]

    def with_below(n):
        return [(i, ((i + 1 ^ 1) - 1) % n) for i in range(n)]

    inputs = [
        pltpu.with_memory_space_constraint(x, pltpu.HBM) for x in (fraction, flow_x, flow_y, flow_z)
    ]
    far, own_y, own_z = pl.pallas_call(
        x_far,
        out_shape=(array(2, columns, length), array(columns, length), array(rows, length)),
        in_specs=[hbm] * 4,
        out_specs=[vmem] * 3,
        scratch_shapes=[
            pltpu.VMEM((2, columns, length), dtype),
            pltpu.VMEM((2, columns, length), dtype),
            dma((4,)),
        ],
        compiler_params=params,
        name="x_far",
    )(*inputs)
    far_side = lax.ppermute(far, "row", with_below(n_row))
    near = pl.pallas_call(
        x_near,
        out_shape=array(2, columns, length),
        in_specs=[vmem] * 3,
        out_specs=vmem,
        compiler_params=params,
        name="x_near",
    )(fraction, flow_x, far)
    near_side = lax.ppermute(near, "row", with_above(n_row))
    courant_y = lax.ppermute(own_y, "row", down(n_row))
    courant_z = lax.ppermute(own_z, "col", down(n_col))
    middle, inner_z = pl.pallas_call(
        x_middle,
        out_shape=(array(rows - 4, columns, length), array(2, rows, length)),
        in_specs=[vmem] * 3 + [hbm],
        out_specs=[vmem] * 2,
        scratch_shapes=[dma((2,))],
        compiler_params=params,
        name="x_middle",
    )(fraction, flow_x, near, inputs[3])
    second, core, chip = pl.pallas_call(
        y_sweep,
        out_shape=(array(*block), array(2, rows, length), array(2, rows, length)),
        in_specs=[vmem] * 8,
        out_specs=[vmem] * 3,
        compiler_params=params,
        cost_estimate=pl.CostEstimate(flops=10**10, bytes_accessed=10**7, transcendentals=0),
        name="y_sweep",
    )(near, near_side, far, far_side, courant_y, middle, flow_y, fraction)
    chip_side = lax.ppermute(chip, "col", with_below(n_col))
    core_side = lax.ppermute(core, "col", with_above(n_col))
    base, inner_cells = pl.pallas_call(
        z_inner,
        out_shape=(array(*block), array(2, rows, length)),
        in_specs=[vmem] * 4,
        out_specs=[vmem] * 2,
        compiler_params=params,
        cost_estimate=pl.CostEstimate(flops=10**10, bytes_accessed=10**7, transcendentals=0),
        name="z_inner",
    )(second, flow_z, fraction, courant_z)
    return pl.pallas_call(
        z_outer,
        out_shape=array(*block),
        in_specs=[vmem] * 9,
        out_specs=hbm,
        scratch_shapes=[
            pltpu.VMEM(block, dtype),
            pltpu.VMEM((4, rows, length), dtype),
            dma((rows,)),
        ],
        compiler_params=params,
        name="z_outer",
    )(chip, chip_side, core, core_side, base, inner_cells, inner_z, own_z, courant_z)


def solution(mesh):
    spec = P("row", "col", None)

    def step(fraction, flow_x, flow_y, flow_z):
        return per_device(
            mesh.shape["row"], mesh.shape["col"], fraction, flow_x, flow_y, flow_z
        )

    return jax.shard_map(
        step, mesh=mesh, in_specs=(spec,) * 4, out_specs=spec, check_vma=False
    )
```

time: 30.7 us -> 24.1 us (0.79)
  the two profiles are of different devices: /device:TPU:0 before, /device:TPU:2 now
where the time goes in v2:
time: 24.1 us; the launch traced here: 23.9 us
  starting transfers between devices  13.4 us (56%)
  waiting for transfers between devices  5.53 us (23%)
  Pallas kernels  4.88 us (20%)
    ppermute x1, waiting for transfers between devices, per_device(): chip_side = lax.ppermute(chip, 'col', with_below(n_col))  5.51 us
    ppermute x1, starting transfers between devices, per_device(): courant_y = lax.ppermute(own_y, 'row', down(n_row))  4.47 us
    ppermute x1, starting transfers between devices, per_device(): courant_z = lax.ppermute(own_z, 'col', down(n_col))  3.47 us
    ppermute x1, starting transfers between devices, per_device(): near_side = lax.ppermute(near, 'row', with_above(n_row))  2.36 us
    ppermute x1, starting transfers between devices, per_device(): chip_side = lax.ppermute(chip, 'col', with_below(n_col))  1.98 us
    pallas_call x1, Pallas kernels, per_device(): pl.pallas_call(x_far, out_shape=(array(2, columns, length), array(columns...  1.36 us
    ppermute x1, starting transfers between devices, per_device(): far_side = lax.ppermute(far, 'row', with_below(n_row))  1.11 us
    pallas_call x1, Pallas kernels, per_device(): pl.pallas_call(z_outer, out_shape=array(*block), in_specs=[vmem] * 9, out...  1.05 us
  transfers between devices with their start and end apart: 6, of which 1 were waited for; matrix products, arithmetic and copies ran while one was open for 0% of the time, Pallas kernels for 9%

profile of v2, /device:TPU:2, one launch (start us, length us, event | category | flops | bytes accessed | tf_op | source)
XLA Modules:
  0.0 23.9 jit_solution(9878748150641428412)
XLA Ops:
  0.0 0.0 copy-start.1
  0.0 0.0 copy-start
  0.0 1.4 %x_far.1 = (f32[2,8,2048]{2,1,0:T(8,128)S(1)}, f32[8,2048]{1,0:T(8,128)S(1)}, f32[8,2048]{1,0:T(8,128)S(1)}) custom-call(f32[8,8,2048]{2,1,0:T(8,128)} %fraction.9, f32[8,8,2048]{2,1,0:T(8,128)} %flow_x.5, f32[8,8,2048]{2,1,0:T(8,128)} %flow_y.3, f32[8,8,2048]{2,1,0:T(8,128)} %flow_z.5), custom_call_target="tpu_custom_call" | custom-call | tf_op jit(solution)/shard_map/x_far/pallas_call | solution.py:221
  1.4 0.0 copy-done.1
  1.4 0.0 copy-done
  1.4 0.3 %x_near.1.near = f32[2,8,2048]{2,1,0:T(8,128)S(1)} custom-call(f32[8,8,2048]{2,1,0:T(8,128)S(1)} %copy-done.1, f32[8,8,2048]{2,1,0:T(8,128)S(1)} %copy-done, f32[2,8,2048]{2,1,0:T(8,128)S(1)} %get-tuple-element.15.far), custom_call_target="tpu_custom_call" | custom-call | tf_op jit(solution)/shard_map/x_near/pallas_call | solution.py:235
  1.7 2.4 %collective-permute-start = (f32[2,8,2048]{2,1,0:T(8,128)S(1)}, f32[2,8,2048]{2,1,0:T(8,128)S(1)}, u32[]{:S(2)}, u32[]{:S(2)}) collective-permute-start(f32[2,8,2048]{2,1,0:T(8,128)S(1)} %x_near.1.near), channel_id=1, source_target_pairs={{0,16},{16,0},{32,48},{48,32},{64,80},{80,64},{96,112},{112,96},{1... | collective-permute-start | bytes 393224 | tf_op jit(solution)/shard_map/ppermute | solution.py:243
  4.0 1.1 %collective-permute-start.1 = (f32[2,8,2048]{2,1,0:T(8,128)S(1)}, f32[2,8,2048]{2,1,0:T(8,128)S(1)}, u32[]{:S(2)}, u32[]{:S(2)}) collective-permute-start(f32[2,8,2048]{2,1,0:T(8,128)S(1)} %get-tuple-element.15.far), channel_id=1, source_target_pairs={{0,240},{16,32},{32,16},{48,64},{64,48},{80,96},{96,80},{112,128},... | collective-permute-start | bytes 393224 | tf_op jit(solution)/shard_map/ppermute | solution.py:234
  5.1 4.5 %collective-permute-start.2 = (f32[8,2048]{1,0:T(8,128)S(1)}, f32[8,2048]{1,0:T(8,128)S(1)}, u32[]{:S(2)}, u32[]{:S(2)}) collective-permute-start(f32[8,2048]{1,0:T(8,128)S(1)} %get-tuple-element.16), channel_id=1, source_target_pairs={{0,240},{16,0},{32,16},{48,32},{64,48},{80,64},{96,80},{112,96},{1... | collective-permute-start | bytes 196616 | tf_op jit(solution)/shard_map/ppermute | solution.py:244
  9.6 0.0 copy-start.3
  9.6 3.5 %collective-permute-start.5 = (f32[8,2048]{1,0:T(8,128)S(1)}, f32[8,2048]{1,0:T(8,128)S(1)}, u32[]{:S(2)}, u32[]{:S(2)}) collective-permute-start(f32[8,2048]{1,0:T(8,128)S(1)} %get-tuple-element.21.own_z), channel_id=1, source_target_pairs={{0,15},{1,0},{2,1},{3,2},{4,3},{5,4},{6,5},{7,6},{8,7},{9,8},{10,9... | collective-permute-start | bytes 196616 | tf_op jit(solution)/shard_map/ppermute | solution.py:245
  13.1 0.9 %x_middle.1 = (f32[4,8,2048]{2,1,0:T(8,128)S(1)}, f32[2,8,2048]{2,1,0:T(8,128)S(1)}) custom-call(f32[8,8,2048]{2,1,0:T(8,128)S(1)} %copy-done.1, f32[8,8,2048]{2,1,0:T(8,128)S(1)} %copy-done, f32[2,8,2048]{2,1,0:T(8,128)S(1)} %x_near.1.near, f32[8,8,2048]{2,1,0:T(8,128)} %flow_z.5), custom_call_target="tpu_custom_call" | custom-call | tf_op jit(solution)/shard_map/x_middle/pallas_call | solution.py:246
  14.0 0.0 collective-permute-done.2.courant_y
  14.0 0.0 collective-permute-done.near_side
  14.0 0.0 collective-permute-done.1.far_side
  14.0 0.0 copy-done.3
  14.0 0.0 copy-start.2
  14.1 0.7 %y_sweep.1 = (f32[8,8,2048]{2,1,0:T(8,128)S(1)}, f32[2,8,2048]{2,1,0:T(8,128)S(1)}, f32[2,8,2048]{2,1,0:T(8,128)S(1)}) custom-call(f32[2,8,2048]{2,1,0:T(8,128)S(1)} %x_near.1.near, f32[2,8,2048]{2,1,0:T(8,128)S(1)} %collective-permute-done.near_side, f32[2,8,2048]{2,1,0:T(8,128)S(1)} %get-tuple-element.15.far, ...), custom_call_target="tpu_custom_call" | custom-call | flops 10000000000 | bytes 10000000 | tf_op jit(solution)/shard_map/y_sweep/pallas_call | solution.py:255
  14.8 2.0 %collective-permute-start.3 = (f32[2,8,2048]{2,1,0:T(8,128)S(1)}, f32[2,8,2048]{2,1,0:T(8,128)S(1)}, u32[]{:S(2)}, u32[]{:S(2)}) collective-permute-start(f32[2,8,2048]{2,1,0:T(8,128)S(1)} %get-tuple-element.18.chip), channel_id=1, source_target_pairs={{0,15},{1,2},{2,1},{3,4},{4,3},{5,6},{6,5},{7,8},{8,7},{9,10},{10,... | collective-permute-start | bytes 393224 | tf_op jit(solution)/shard_map/ppermute | solution.py:264
  16.7 0.0 collective-permute-start.4
  16.7 0.0 collective-permute-done.5.courant_z
  16.7 0.0 copy-done.2
  16.8 0.6 %z_inner.1 = (f32[8,8,2048]{2,1,0:T(8,128)S(1)}, f32[2,8,2048]{2,1,0:T(8,128)S(1)}) custom-call(f32[8,8,2048]{2,1,0:T(8,128)S(1)} %get-tuple-element.20.second, f32[8,8,2048]{2,1,0:T(8,128)S(1)} %copy-done.2, f32[8,8,2048]{2,1,0:T(8,128)S(1)} %copy-done.1, f32[8,2048]{1,0:T(8,128)S(1)} %collective-permute-done.5.courant_z), custom_call_target="tpu_custom_call" | custom-call | flops 10000000000 | bytes 10000000 | tf_op jit(solution)/shard_map/z_inner/pallas_call | solution.py:266
  17.3 5.5 %collective-permute-done.3.chip_side = f32[2,8,2048]{2,1,0:T(8,128)S(1)} collective-permute-done((f32[2,8,2048]{2,1,0:T(8,128)S(1)}, f32[2,8,2048]{2,1,0:T(8,128)S(1)}, u32[]{:S(2)}, u32[]{:S(2)}) %collective-permute-start.3) | collective-permute-done | bytes 131104 | tf_op jit(solution)/shard_map/ppermute | solution.py:264
  22.9 0.0 collective-permute-done.4.core_side
  22.9 1.0 %z_outer.1 = f32[8,8,2048]{2,1,0:T(8,128)} custom-call(f32[2,8,2048]{2,1,0:T(8,128)S(1)} %get-tuple-element.18.chip, f32[2,8,2048]{2,1,0:T(8,128)S(1)} %collective-permute-done.3.chip_side, f32[2,8,2048]{2,1,0:T(8,128)S(1)} %get-tuple-element.19.core, f32[2,8,2048]{2,1,0:T(8,128)S(1)} %collective-permute-done.4.core_side, ...), custom_call_target="tpu_custom_call" | custom-call | tf_op jit(solution)/shard_map/z_outer/pallas_call | solution.py:275
Async XLA Ops:
  0.0 1.4 %copy-start.1 = (f32[8,8,2048]{2,1,0:T(8,128)S(1)}, f32[8,8,2048]{2,1,0:T(8,128)}, u32[]{:S(2)}) copy-start(f32[8,8,2048]{2,1,0:T(8,128)} %fraction.9) | copy-start | bytes 1572868
  0.0 1.4 %copy-start = (f32[8,8,2048]{2,1,0:T(8,128)S(1)}, f32[8,8,2048]{2,1,0:T(8,128)}, u32[]{:S(2)}) copy-start(f32[8,8,2048]{2,1,0:T(8,128)} %flow_x.5) | copy-start | bytes 1572868
  1.7 12.3 %collective-permute-start = (f32[2,8,2048]{2,1,0:T(8,128)S(1)}, f32[2,8,2048]{2,1,0:T(8,128)S(1)}, u32[]{:S(2)}, u32[]{:S(2)}) collective-permute-start(f32[2,8,2048]{2,1,0:T(8,128)S(1)} %x_near.1.near), channel_id=1, source_target_pairs={{0,16},{16,0},{32,48},{48,32},{64,80},{80,64},{96,112},{112,96},{1... | collective-permute-start | bytes 393224 | tf_op jit(solution)/shard_map/ppermute | solution.py:243
  4.0 10.0 %collective-permute-start.1 = (f32[2,8,2048]{2,1,0:T(8,128)S(1)}, f32[2,8,2048]{2,1,0:T(8,128)S(1)}, u32[]{:S(2)}, u32[]{:S(2)}) collective-permute-start(f32[2,8,2048]{2,1,0:T(8,128)S(1)} %get-tuple-element.15.far), channel_id=1, source_target_pairs={{0,240},{16,32},{32,16},{48,64},{64,48},{80,96},{96,80},{112,128},... | collective-permute-start | bytes 393224 | tf_op jit(solution)/shard_map/ppermute | solution.py:234
  5.1 8.9 %collective-permute-start.2 = (f32[8,2048]{1,0:T(8,128)S(1)}, f32[8,2048]{1,0:T(8,128)S(1)}, u32[]{:S(2)}, u32[]{:S(2)}) collective-permute-start(f32[8,2048]{1,0:T(8,128)S(1)} %get-tuple-element.16), channel_id=1, source_target_pairs={{0,240},{16,0},{32,16},{48,32},{64,48},{80,64},{96,80},{112,96},{1... | collective-permute-start | bytes 196616 | tf_op jit(solution)/shard_map/ppermute | solution.py:244
  9.6 4.4 %copy-start.3 = (f32[8,8,2048]{2,1,0:T(8,128)S(1)}, f32[8,8,2048]{2,1,0:T(8,128)}, u32[]{:S(2)}) copy-start(f32[8,8,2048]{2,1,0:T(8,128)} %flow_y.3) | copy-start | bytes 1572868
  9.6 7.1 %collective-permute-start.5 = (f32[8,2048]{1,0:T(8,128)S(1)}, f32[8,2048]{1,0:T(8,128)S(1)}, u32[]{:S(2)}, u32[]{:S(2)}) collective-permute-start(f32[8,2048]{1,0:T(8,128)S(1)} %get-tuple-element.21.own_z), channel_id=1, source_target_pairs={{0,15},{1,0},{2,1},{3,2},{4,3},{5,4},{6,5},{7,6},{8,7},{9,8},{10,9... | collective-permute-start | bytes 196616 | tf_op jit(solution)/shard_map/ppermute | solution.py:245
  14.0 2.7 %copy-start.2 = (f32[8,8,2048]{2,1,0:T(8,128)S(1)}, f32[8,8,2048]{2,1,0:T(8,128)}, u32[]{:S(2)}) copy-start(f32[8,8,2048]{2,1,0:T(8,128)} %flow_z.5) | copy-start | bytes 1572868
  14.8 8.1 %collective-permute-start.3 = (f32[2,8,2048]{2,1,0:T(8,128)S(1)}, f32[2,8,2048]{2,1,0:T(8,128)S(1)}, u32[]{:S(2)}, u32[]{:S(2)}) collective-permute-start(f32[2,8,2048]{2,1,0:T(8,128)S(1)} %get-tuple-element.18.chip), channel_id=1, source_target_pairs={{0,15},{1,2},{2,1},{3,4},{4,3},{5,6},{6,5},{7,8},{8,7},{9,10},{10,... | collective-permute-start | bytes 393224 | tf_op jit(solution)/shard_map/ppermute | solution.py:264
  16.7 6.1 %collective-permute-start.4 = (f32[2,8,2048]{2,1,0:T(8,128)S(1)}, f32[2,8,2048]{2,1,0:T(8,128)S(1)}, u32[]{:S(2)}, u32[]{:S(2)}) collective-permute-start(f32[2,8,2048]{2,1,0:T(8,128)S(1)} %get-tuple-element.19.core), channel_id=1, source_target_pairs={{0,1},{1,0},{2,3},{3,2},{4,5},{5,4},{6,7},{7,6},{8,9},{9,8},{10,11... | collective-permute-start | bytes 393224 | tf_op jit(solution)/shard_map/ppermute | solution.py:265

commit v3 on v2

v3 whole, which is shorter than its diff:
```python
import jax
import jax.numpy as jnp
from jax import lax
from jax.experimental import pallas as pl
from jax.experimental.pallas import tpu as pltpu
from jax.sharding import PartitionSpec as P

LANES = 128
CHUNK = 512


def face_flux(two_below, below, here, above, courant):
    forward = courant >= 0.0
    donor = jnp.where(forward, below, here)
    slope = jnp.where(forward, here - two_below, below - above)
    return donor_flux(forward, donor, slope, courant)


def donor_flux(forward, donor, slope, courant):
    reach = jnp.abs(courant)
    least = jnp.minimum(donor, reach)
    most = jnp.maximum(0.0, reach - 1.0 + donor)
    tilt = jnp.tanh(10.0 * slope)
    return jnp.where(forward, 0.5, -0.5) * ((least + most) + tilt * (least - most))


def updated(here, flux, next_flux, courant, next_courant, start):
    spread = jnp.where(start > 0.5, next_courant - courant, 0.0)
    return here - (next_flux - flux) + spread


def x_sweep_row(here, courant):
    length = here.shape[1]
    below = pltpu.roll(here, 1, 1)
    two_below = pltpu.roll(here, 2, 1)
    above = pltpu.roll(here, length - 1, 1)
    flux = face_flux(two_below, below, here, above, courant)
    from_below = flux - jnp.where(below > 0.5, courant, 0.0)
    to_above = flux - jnp.where(here > 0.5, courant, 0.0)
    return here + (to_above - pltpu.roll(from_below, length - 1, 1))


def x_columns(
    fraction, flow_x, flow_y, flow_z, first, start, courant, upward, downward, own_y, own_z,
    flows, sems,
):
    rows, columns, _ = fraction.shape
    column = lax.rem(lax.axis_index("col"), 2) * (columns - 2)
    loads = [
        pltpu.make_async_copy(source.at[:, column + m], into.at[m], sems.at[2 * n + m])
        for n, (source, into) in enumerate(((fraction, start), (flow_x, flows), (flow_y, courant)))
        for m in range(2)
    ]
    loads.append(pltpu.make_async_copy(flow_y.at[0], own_y, sems.at[6]))
    loads.append(pltpu.make_async_copy(flow_z.at[:, 0], own_z, sems.at[7]))
    for load in loads:
        load.start()
    for load in loads[:4]:
        load.wait()
    for m in range(2):
        result = x_sweep_row(start[m], flows[m])
        first[m] = result
        for i in range(2):
            upward[i, m : m + 1] = result[rows - 2 + i : rows - 1 + i]
            downward[i, m : m + 1] = result[i : i + 1]
    for load in loads[4:]:
        load.wait()
    for m in range(2):
        downward[2, m : m + 1] = courant[m, :1]


def x_rows(fraction, flow_x, own_y, high, low, upward, downward):
    rows, columns, _ = fraction.shape
    odd_core = lax.rem(lax.axis_index("col"), 2) == 1
    pairs = columns // 2 - 1

    def put(message, i, row):
        for p in range(pairs):
            message[i * pairs + p] = lax.select(
                odd_core, row[2 * p : 2 * p + 2], row[2 * p + 2 : 2 * p + 4]
            )

    put(downward, 2, own_y[...])
    for mine, message, start in ((low, downward, 0), (high, upward, rows - 2)):
        for i in range(2):
            mine[i] = x_sweep_row(fraction[start + i], flow_x[start + i])
            put(message, i, mine[i])


def x_middle(fraction, flow_x, chip, middle):
    del chip
    for i in range(middle.shape[0]):
        middle[i] = x_sweep_row(fraction[i + 2], flow_x[i + 2])


def y_columns(first, start, courant, high, lower, upper, own_z, chip, own_z_out):
    _, rows, length = first.shape
    own_z_out[...] = own_z[...]
    place = lax.broadcasted_iota(jnp.int32, (rows, CHUNK), 0)
    bottom = place == 0
    top = place == rows - 1
    for j in range(length // CHUNK):
        at = slice(j * CHUNK, (j + 1) * CHUNK)
        last_flux = face_flux(
            high[0, :, at], high[1, :, at], upper[0, :, at], upper[1, :, at], upper[2, :, at]
        )
        for m in range(2):
            one = slice(m, m + 1)
            here, flow = first[m, :, at], courant[m, :, at]
            below = jnp.where(bottom, lower[1, one, at], pltpu.roll(here, 1, 0))
            two_below = jnp.where(bottom, lower[0, one, at], pltpu.roll(below, 1, 0))
            above = jnp.where(top, upper[0, one, at], pltpu.roll(here, rows - 1, 0))
            flux = face_flux(two_below, below, here, above, flow)
            next_flux = jnp.where(top, last_flux[one], pltpu.roll(flux, rows - 1, 0))
            next_flow = jnp.where(top, upper[2, one, at], pltpu.roll(flow, rows - 1, 0))
            chip[m, :, at] = updated(here, flux, next_flux, flow, next_flow, start[m, :, at])


def y_sweep(
    high, lower_pairs, low, upper_pairs, lower_edge, upper_edge, middle, flow_y, fraction,
    second, core, halo,
):
    rows, columns, length = second.shape
    odd_core = lax.rem(lax.axis_index("col"), 2) == 1
    pairs = columns // 2 - 1
    for edge, rest, slabs in ((lower_edge, lower_pairs, (0, 1)), (upper_edge, upper_pairs, (2, 3, 4))):
        for m, slab in enumerate(slabs):
            others = [rest[m * pairs + p] for p in range(pairs)]
            ends = [edge[m], *others], [*others, edge[m]]
            for p in range(pairs + 1):
                halo[slab, 2 * p : 2 * p + 2] = lax.select(odd_core, ends[1][p], ends[0][p])

    def tile(t, _):
        at = pl.ds(pl.multiple_of(t * LANES, LANES), LANES)

        def pair(ref, start=0):
            return [ref[start + i, :, at] for i in range(2)]

        inner = [middle[i, :, at] for i in range(rows - 4)]
        cells = pair(halo) + pair(low) + inner + pair(high) + pair(halo, 2)
        flows = [flow_y[i, :, at] for i in range(rows)] + [halo[4, :, at]]
        flux = face_flux(*cells[:4], flows[0])
        for i in range(rows):
            next_flux = face_flux(*cells[i + 1 : i + 5], flows[i + 1])
            result = updated(
                cells[i + 2], flux, next_flux, flows[i], flows[i + 1], fraction[i, :, at]
            )
            flux = next_flux
            second[i, :, at] = result
            for m in range(2):
                up, down = result[columns - 2 + m : columns - 1 + m], result[m : m + 1]
                core[m, i : i + 1, at] = lax.select(odd_core, down, up)
        return _

    lax.fori_loop(0, length // LANES, tile, None, unroll=2)


def z_inner(second, flow_z, fraction, base, inside):
    rows, columns, length = second.shape
    place = lax.broadcasted_iota(jnp.int32, (columns, CHUNK), 0)
    top = place == columns - 1
    inner = (place >= 2) & (place <= columns - 2)
    for i in range(rows):
        for j in range(length // CHUNK):
            at = slice(j * CHUNK, (j + 1) * CHUNK)
            here = second[i, :, at]
            courant = flow_z[i, :, at]
            flux = face_flux(
                pltpu.roll(here, 2, 0),
                pltpu.roll(here, 1, 0),
                here,
                pltpu.roll(here, columns - 1, 0),
                courant,
            )
            flux = jnp.where(inner, flux, 0.0)
            next_courant = jnp.where(top, 0.0, pltpu.roll(courant, columns - 1, 0))
            start = fraction[i, :, at]
            base[i, :, at] = updated(
                here, flux, pltpu.roll(flux, columns - 1, 0), courant, next_courant, start
            )
            inside[4, i : i + 1, at] = start[columns - 1 :]
            inside[0, i : i + 1, at] = here[2:3]
            inside[1, i : i + 1, at] = here[columns - 3 : columns - 2]
            inside[2, i : i + 1, at] = courant[1:2]
            inside[3, i : i + 1, at] = courant[columns - 1 :]


def z_outer(
    chip, chip_side, core, core_side, base, inside, own_z, courant_z, out,
    part, change, sems,
):
    rows, columns, length = base.shape
    odd_core = lax.rem(lax.axis_index("col"), 2) == 1
    place = lax.broadcasted_iota(jnp.int32, (columns, CHUNK), 0)
    pieces = [slice(j * CHUNK, (j + 1) * CHUNK) for j in range(length // CHUNK)]

    for at in pieces:

        def ordered(a, b, at=at):
            pairs = [(a[m, :, at], b[m, :, at]) for m in range(a.shape[0])]
            return [lax.select(odd_core, x, y) for x, y in pairs], [
                lax.select(odd_core, y, x) for x, y in pairs
            ]

        below, above = ordered(core_side, chip_side)
        low, high = ordered(core, chip)
        after_low, before_high = inside[0, :, at], inside[1, :, at]
        flux = [
            face_flux(*below, *low, own_z[:, at]),
            face_flux(below[1], *low, after_low, inside[2, :, at]),
            face_flux(before_high, *high, above[0], inside[3, :, at]),
            face_flux(*high, *above, courant_z[:, at]),
        ]
        change[0, :, at] = flux[0] - flux[1]
        change[1, :, at] = flux[1]
        change[2, :, at] = -flux[2]
        spread = jnp.where(inside[4, :, at] > 0.5, courant_z[:, at], 0.0)
        change[3, :, at] = flux[2] - flux[3] + spread

    stores = []
    for i in range(rows):
        for at in pieces:
            value = jnp.zeros((columns, CHUNK), base.dtype)
            for n, column in enumerate((0, 1, columns - 2, columns - 1)):
                value = jnp.where(place == column, change[n, i : i + 1, at], value)
            part[i, :, at] = base[i, :, at] + value
        stores.append(pltpu.make_async_copy(part.at[i], out.at[i], sems.at[i]))
        stores[-1].start()
    for store in stores:
        store.wait()


def per_device(n_row, n_col, fraction, flow_x, flow_y, flow_z):
    block, dtype = fraction.shape, fraction.dtype
    rows, columns, length = block
    vmem = pl.BlockSpec(memory_space=pltpu.VMEM)
    hbm = pl.BlockSpec(memory_space=pltpu.HBM)
    params = pltpu.CompilerParams(vmem_limit_bytes=16 * 1024 * 1024)
    dma = pltpu.SemaphoreType.DMA
    busy = pl.CostEstimate(flops=10**10, bytes_accessed=10**7, transcendentals=0)

    def array(*shape):
        return jax.ShapeDtypeStruct(shape, dtype)

    def with_above(n):
        return [(i, i ^ 1) for i in range(n)]

    def up(n):
        return [(i, (i + 1) % n) for i in range(n)]

    def down(n):
        return [(i, (i - 1) % n) for i in range(n)]

    def with_below(n):
        return [(i, ((i + 1 ^ 1) - 1) % n) for i in range(n)]

    inputs = [
        pltpu.with_memory_space_constraint(x, pltpu.HBM) for x in (fraction, flow_x, flow_y, flow_z)
    ]
    edge, side = array(2, rows, length), array(2, 2, length)
    first, start, courant, upward, downward, own_y, own_z = pl.pallas_call(
        x_columns,
        out_shape=(
            edge, edge, edge, side, array(3, 2, length), array(columns, length), array(rows, length)
        ),
        in_specs=[hbm] * 4,
        out_specs=[vmem] * 7,
        scratch_shapes=[pltpu.VMEM((2, rows, length), dtype), dma((8,))],
        compiler_params=params,
        name="x_columns",
    )(*inputs)
    column_lower = lax.ppermute(upward, "row", up(n_row))
    column_upper = lax.ppermute(downward, "row", down(n_row))
    pairs = columns // 2 - 1
    high, low, upward_pairs, downward_pairs = pl.pallas_call(
        x_rows,
        out_shape=(
            array(2, columns, length),
            array(2, columns, length),
            array(2 * pairs, 2, length),
            array(3 * pairs, 2, length),
        ),
        in_specs=[vmem] * 3,
        out_specs=[vmem] * 4,
        compiler_params=params,
        cost_estimate=busy,
        name="x_rows",
    )(fraction, flow_x, own_y)
    lower_pairs = lax.ppermute(upward_pairs, "row", up(n_row))
    upper_pairs = lax.ppermute(downward_pairs, "row", down(n_row))
    chip, own_z = pl.pallas_call(
        y_columns,
        out_shape=(edge, array(rows, length)),
        in_specs=[vmem] * 7,
        out_specs=[vmem] * 2,
        compiler_params=params,
        cost_estimate=busy,
        name="y_columns",
    )(first, start, courant, upward, column_lower, column_upper, own_z)
    chip_side = lax.ppermute(chip, "col", with_below(n_col))
    courant_z = lax.ppermute(own_z, "col", down(n_col))
    middle = pl.pallas_call(
        x_middle,
        out_shape=array(rows - 4, columns, length),
        in_specs=[vmem] * 3,
        out_specs=vmem,
        compiler_params=params,
        name="x_middle",
    )(fraction, flow_x, chip)
    second, core = pl.pallas_call(
        y_sweep,
        out_shape=(array(*block), edge),
        in_specs=[vmem] * 9,
        out_specs=[vmem] * 2,
        scratch_shapes=[pltpu.VMEM((5, columns, length), dtype)],
        compiler_params=params,
        cost_estimate=busy,
        name="y_sweep",
    )(
        high, lower_pairs, low, upper_pairs, column_lower, column_upper, middle, flow_y, fraction
    )
    core_side = lax.ppermute(core, "col", with_above(n_col))
    base, inside = pl.pallas_call(
        z_inner,
        out_shape=(array(*block), array(5, rows, length)),
        in_specs=[vmem] * 3,
        out_specs=[vmem] * 2,
        compiler_params=params,
        cost_estimate=busy,
        name="z_inner",
    )(second, flow_z, fraction)
    return pl.pallas_call(
        z_outer,
        out_shape=array(*block),
        in_specs=[vmem] * 8,
        out_specs=hbm,
        scratch_shapes=[
            pltpu.VMEM(block, dtype),
            pltpu.VMEM((4, rows, length), dtype),
            dma((rows,)),
        ],
        compiler_params=params,
        name="z_outer",
    )(chip, chip_side, core, core_side, base, inside, own_z, courant_z)


def solution(mesh):
    spec = P("row", "col", None)

    def step(fraction, flow_x, flow_y, flow_z):
        return per_device(
            mesh.shape["row"], mesh.shape["col"], fraction, flow_x, flow_y, flow_z
        )

    return jax.shard_map(
        step, mesh=mesh, in_specs=(spec,) * 4, out_specs=spec, check_vma=False
    )
```

time: 24.1 us -> 23.1 us (0.959)
  waiting for transfers between devices: 5.53 us -> 4.48 us
  starting transfers between devices: 13.4 us -> 13.1 us
    ppermute x1, waiting for transfers between devices: 5.51 us -> 3.6 us  [per_device(): chip_side = lax.ppermute(chip, 'col', with_below(n_col))]
    ppermute x1, starting transfers between devices: 1.98 us -> 3.54 us  [per_device(): chip_side = lax.ppermute(chip, 'col', with_below(n_col))]
    ppermute x1, starting transfers between devices: 3.47 us -> 1.9 us  [per_device(): courant_z = lax.ppermute(own_z, 'col', down(n_col))]
    ppermute x1, waiting for transfers between devices: 0.01 us -> 0.86 us  [per_device(): courant_z = lax.ppermute(own_z, 'col', down(n_col))]
    ppermute x3 -> x4, starting transfers between devices: 7.94 us -> 7.56 us  [the longest x1 5.12 us: per_device(): upper_pairs = lax.ppermute(downward_pairs, 'row', down(n_row))]
    pallas_call x6 -> x7, Pallas kernels: 4.88 us -> 5.08 us  [the longest x1 1.42 us: per_device(): pl.pallas_call(x_columns, out_shape=(edge, edge, edge, side, array(3, 2,...]
  transfers between devices with their start and end apart: 6 -> 7, of which waited for: 1 -> 2; matrix products, arithmetic and copies ran while one was open for 0% -> 0% of each run, Pallas kernels for 9% -> 11%
where the time goes in v3:
time: 23.1 us; the launch traced here: 23 us
  starting transfers between devices  13.1 us (57%)
  Pallas kernels  5.08 us (22%)
  waiting for transfers between devices  4.48 us (19%)
  local copies, waits for them, and re-layouts  0.24 us (1%)
    ppermute x1, starting transfers between devices, per_device(): upper_pairs = lax.ppermute(downward_pairs, 'row', down(n_row))  5.12 us
    ppermute x1, waiting for transfers between devices, per_device(): chip_side = lax.ppermute(chip, 'col', with_below(n_col))  3.6 us
    ppermute x1, starting transfers between devices, per_device(): chip_side = lax.ppermute(chip, 'col', with_below(n_col))  3.54 us
    ppermute x1, starting transfers between devices, per_device(): column_lower = lax.ppermute(upward, 'row', up(n_row))  1.97 us
    ppermute x1, starting transfers between devices, per_device(): courant_z = lax.ppermute(own_z, 'col', down(n_col))  1.9 us
    pallas_call x1, Pallas kernels, per_device(): pl.pallas_call(x_columns, out_shape=(edge, edge, edge, side, array(3, 2,...  1.42 us
    pallas_call x1, Pallas kernels, per_device(): pl.pallas_call(z_outer, out_shape=array(*block), in_specs=[vmem] * 8, out...  1.06 us
    ppermute x1, waiting for transfers between devices, per_device(): courant_z = lax.ppermute(own_z, 'col', down(n_col))  0.86 us
  transfers between devices with their start and end apart: 7, of which 2 were waited for; matrix products, arithmetic and copies ran while one was open for 0% of the time, Pallas kernels for 11%

profile of v3, /device:TPU:2, one launch (start us, length us, event | category | flops | bytes accessed | tf_op | source)
XLA Modules:
  0.0 23.0 jit_solution(1403393377134196726)
XLA Ops:
  0.0 0.0 copy-start.1
  0.0 0.0 copy-start
  0.0 1.4 %x_columns.1 = (f32[2,8,2048]{2,1,0:T(8,128)S(1)}, f32[2,8,2048]{2,1,0:T(8,128)S(1)}, f32[2,8,2048]{2,1,0:T(8,128)S(1)}, f32[2,2,2048]{2,1,0:T(2,128)S(1)}, f32[...) custom-call(f32[8,8,2048]{2,1,0:T(8,128)} %fraction.9, f32[8,8,2048]{2,1,0:T(8,128)} %flow_x.5, ...), custom_call_target="tpu_custom_call" | custom-call | tf_op jit(solution)/shard_map/x_columns/pallas_call | solution.py:261
  1.4 2.0 %collective-permute-start = (f32[2,2,2048]{2,1,0:T(2,128)S(1)}, f32[2,2,2048]{2,1,0:T(2,128)S(1)}, u32[]{:S(2)}, u32[]{:S(2)}) collective-permute-start(f32[2,2,2048]{2,1,0:T(2,128)S(1)} %get-tuple-element.25.high), channel_id=1, source_target_pairs={{0,16},{16,32},{32,48},{48,64},{64,80},{80,96},{96,112},{112,128},... | collective-permute-start | bytes 98312 | tf_op jit(solution)/shard_map/ppermute | solution.py:272
  3.4 0.5 %collective-permute-start.1 = (f32[3,2,2048]{2,1,0:T(2,128)S(1)}, f32[3,2,2048]{2,1,0:T(2,128)S(1)}, u32[]{:S(2)}, u32[]{:S(2)}) collective-permute-start(f32[3,2,2048]{2,1,0:T(2,128)S(1)} %get-tuple-element.26), channel_id=1, source_target_pairs={{0,240},{16,0},{32,16},{48,32},{64,48},{80,64},{96,80},{112,96},{1... | collective-permute-start | bytes 147464 | tf_op jit(solution)/shard_map/ppermute | solution.py:273
  3.9 0.0 copy-done.1
  3.9 0.0 copy-done
  3.9 0.5 %x_rows.1 = (f32[2,8,2048]{2,1,0:T(8,128)S(1)}, f32[2,8,2048]{2,1,0:T(8,128)S(1)}, f32[6,2,2048]{2,1,0:T(2,128)S(1)}, f32[9,2,2048]{2,1,0:T(2,128)S(1)}) custom-call(f32[8,8,2048]{2,1,0:T(8,128)S(1)} %copy-done.1, f32[8,8,2048]{2,1,0:T(8,128)S(1)} %copy-done, f32[8,2048]{1,0:T(8,128)S(1)} %get-tuple-element.29.own_y), custom_call_target="tpu_custom_call" | custom-call | flops 10000000000 | bytes 10000000 | tf_op jit(solution)/shard_map/x_rows/pallas_call | solution.py:275
  4.4 5.1 %collective-permute-start.4 = (f32[9,2,2048]{2,1,0:T(2,128)S(1)}, f32[9,2,2048]{2,1,0:T(2,128)S(1)}, u32[]{:S(2)}, u32[]{:S(2)}) collective-permute-start(f32[9,2,2048]{2,1,0:T(2,128)S(1)} %get-tuple-element.33), channel_id=1, source_target_pairs={{0,240},{16,0},{32,16},{48,32},{64,48},{80,64},{96,80},{112,96},{1... | collective-permute-start | bytes 442376 | tf_op jit(solution)/shard_map/ppermute | solution.py:290
  9.5 0.0 collective-permute-start.3
  9.5 0.0 collective-permute-done.lower.lower_edge
  9.5 0.0 collective-permute-done.1.upper.upper_edge
  9.6 0.2 y_columns.1
  9.7 0.0 copy-start.2
  9.7 0.5 %x_middle.1.middle = f32[4,8,2048]{2,1,0:T(8,128)S(1)} custom-call(f32[8,8,2048]{2,1,0:T(8,128)S(1)} %copy-done.1, f32[8,8,2048]{2,1,0:T(8,128)S(1)} %copy-done, f32[2,8,2048]{2,1,0:T(8,128)S(1)} %get-tuple-element.28.chip), custom_call_target="tpu_custom_call" | custom-call | tf_op jit(solution)/shard_map/x_middle/pallas_call | solution.py:302
  10.3 3.5 %collective-permute-start.2 = (f32[2,8,2048]{2,1,0:T(8,128)S(1)}, f32[2,8,2048]{2,1,0:T(8,128)S(1)}, u32[]{:S(2)}, u32[]{:S(2)}) collective-permute-start(f32[2,8,2048]{2,1,0:T(8,128)S(1)} %get-tuple-element.28.chip), channel_id=1, source_target_pairs={{0,15},{1,2},{2,1},{3,4},{4,3},{5,6},{6,5},{7,8},{8,7},{9,10},{10,... | collective-permute-start | bytes 393224 | tf_op jit(solution)/shard_map/ppermute | solution.py:300
  13.8 1.9 %collective-permute-start.6 = (f32[8,2048]{1,0:T(8,128)S(1)}, f32[8,2048]{1,0:T(8,128)S(1)}, u32[]{:S(2)}, u32[]{:S(2)}) collective-permute-start(f32[8,2048]{1,0:T(8,128)S(1)} %get-tuple-element.38.own_z), channel_id=1, source_target_pairs={{0,15},{1,0},{2,1},{3,2},{4,3},{5,4},{6,5},{7,6},{8,7},{9,8},{10,9... | collective-permute-start | bytes 196616 | tf_op jit(solution)/shard_map/ppermute | solution.py:301
  15.7 0.0 collective-permute-done.3.lower_pairs
  15.7 0.0 collective-permute-done.4.upper_pairs
  15.7 0.0 copy-done.2
  15.7 0.0 copy-start.3
  15.7 0.7 %y_sweep.1 = (f32[8,8,2048]{2,1,0:T(8,128)S(1)}, f32[2,8,2048]{2,1,0:T(8,128)S(1)}) custom-call(f32[2,8,2048]{2,1,0:T(8,128)S(1)} %get-tuple-element.30.high, f32[6,2,2048]{2,1,0:T(2,128)S(1)} %collective-permute-done.3.lower_pairs, f32[2,8,2048]{2,1,0:T(8,128)S(1)} %get-tuple-element.32.low, f32[9,2,2048]{2,1,0:T(2,128)S(1)} %collective-permute-done.4.upper_pairs, ...), custom_call_target="tpu_custom_call" | custom-call | flops 10000000000 | bytes 10000000 | tf_op jit(solution)/shard_map/y_sweep/pallas_call | solution.py:310
  16.4 0.1 collective-permute-start.5
  16.5 0.2 copy-done.3
  16.8 0.7 %z_inner.1 = (f32[8,8,2048]{2,1,0:T(8,128)S(1)}, f32[5,8,2048]{2,1,0:T(8,128)S(1)}) custom-call(f32[8,8,2048]{2,1,0:T(8,128)S(1)} %get-tuple-element.35.second, f32[8,8,2048]{2,1,0:T(8,128)S(1)} %copy-done.3, f32[8,8,2048]{2,1,0:T(8,128)S(1)} %copy-done.1), custom_call_target="tpu_custom_call" | custom-call | flops 10000000000 | bytes 10000000 | tf_op jit(solution)/shard_map/z_inner/pallas_call | solution.py:323
  17.4 0.9 %collective-permute-done.6.courant_z = f32[8,2048]{1,0:T(8,128)S(1)} collective-permute-done((f32[8,2048]{1,0:T(8,128)S(1)}, f32[8,2048]{1,0:T(8,128)S(1)}, u32[]{:S(2)}, u32[]{:S(2)}) %collective-permute-start.6) | collective-permute-done | bytes 65568 | tf_op jit(solution)/shard_map/ppermute | solution.py:301
  18.3 3.6 %collective-permute-done.2.chip_side = f32[2,8,2048]{2,1,0:T(8,128)S(1)} collective-permute-done((f32[2,8,2048]{2,1,0:T(8,128)S(1)}, f32[2,8,2048]{2,1,0:T(8,128)S(1)}, u32[]{:S(2)}, u32[]{:S(2)}) %collective-permute-start.2) | collective-permute-done | bytes 131104 | tf_op jit(solution)/shard_map/ppermute | solution.py:300
  21.9 0.0 collective-permute-done.5.core_side
  21.9 1.1 %z_outer.1 = f32[8,8,2048]{2,1,0:T(8,128)} custom-call(f32[2,8,2048]{2,1,0:T(8,128)S(1)} %get-tuple-element.28.chip, f32[2,8,2048]{2,1,0:T(8,128)S(1)} %collective-permute-done.2.chip_side, f32[2,8,2048]{2,1,0:T(8,128)S(1)} %get-tuple-element.34.core, f32[2,8,2048]{2,1,0:T(8,128)S(1)} %collective-permute-done.5.core_side, ...), custom_call_target="tpu_custom_call" | custom-call | tf_op jit(solution)/shard_map/z_outer/pallas_call | solution.py:332
Async XLA Ops:
  0.0 3.9 %copy-start.1 = (f32[8,8,2048]{2,1,0:T(8,128)S(1)}, f32[8,8,2048]{2,1,0:T(8,128)}, u32[]{:S(2)}) copy-start(f32[8,8,2048]{2,1,0:T(8,128)} %fraction.9) | copy-start | bytes 1572868
  0.0 3.9 %copy-start = (f32[8,8,2048]{2,1,0:T(8,128)S(1)}, f32[8,8,2048]{2,1,0:T(8,128)}, u32[]{:S(2)}) copy-start(f32[8,8,2048]{2,1,0:T(8,128)} %flow_x.5) | copy-start | bytes 1572868
  1.4 8.1 %collective-permute-start = (f32[2,2,2048]{2,1,0:T(2,128)S(1)}, f32[2,2,2048]{2,1,0:T(2,128)S(1)}, u32[]{:S(2)}, u32[]{:S(2)}) collective-permute-start(f32[2,2,2048]{2,1,0:T(2,128)S(1)} %get-tuple-element.25.high), channel_id=1, source_target_pairs={{0,16},{16,32},{32,48},{48,64},{64,80},{80,96},{96,112},{112,128},... | collective-permute-start | bytes 98312 | tf_op jit(solution)/shard_map/ppermute | solution.py:272
  3.4 6.1 %collective-permute-start.1 = (f32[3,2,2048]{2,1,0:T(2,128)S(1)}, f32[3,2,2048]{2,1,0:T(2,128)S(1)}, u32[]{:S(2)}, u32[]{:S(2)}) collective-permute-start(f32[3,2,2048]{2,1,0:T(2,128)S(1)} %get-tuple-element.26), channel_id=1, source_target_pairs={{0,240},{16,0},{32,16},{48,32},{64,48},{80,64},{96,80},{112,96},{1... | collective-permute-start | bytes 147464 | tf_op jit(solution)/shard_map/ppermute | solution.py:273
  4.4 11.3 %collective-permute-start.4 = (f32[9,2,2048]{2,1,0:T(2,128)S(1)}, f32[9,2,2048]{2,1,0:T(2,128)S(1)}, u32[]{:S(2)}, u32[]{:S(2)}) collective-permute-start(f32[9,2,2048]{2,1,0:T(2,128)S(1)} %get-tuple-element.33), channel_id=1, source_target_pairs={{0,240},{16,0},{32,16},{48,32},{64,48},{80,64},{96,80},{112,96},{1... | collective-permute-start | bytes 442376 | tf_op jit(solution)/shard_map/ppermute | solution.py:290
  9.5 6.2 %collective-permute-start.3 = (f32[6,2,2048]{2,1,0:T(2,128)S(1)}, f32[6,2,2048]{2,1,0:T(2,128)S(1)}, u32[]{:S(2)}, u32[]{:S(2)}) collective-permute-start(f32[6,2,2048]{2,1,0:T(2,128)S(1)} %get-tuple-element.31), channel_id=1, source_target_pairs={{0,16},{16,32},{32,48},{48,64},{64,80},{80,96},{96,112},{112,128},... | collective-permute-start | bytes 294920 | tf_op jit(solution)/shard_map/ppermute | solution.py:289
  9.7 6.0 %copy-start.2 = (f32[8,8,2048]{2,1,0:T(8,128)S(1)}, f32[8,8,2048]{2,1,0:T(8,128)}, u32[]{:S(2)}) copy-start(f32[8,8,2048]{2,1,0:T(8,128)} %flow_y.3) | copy-start | bytes 1572868
  10.3 11.6 %collective-permute-start.2 = (f32[2,8,2048]{2,1,0:T(8,128)S(1)}, f32[2,8,2048]{2,1,0:T(8,128)S(1)}, u32[]{:S(2)}, u32[]{:S(2)}) collective-permute-start(f32[2,8,2048]{2,1,0:T(8,128)S(1)} %get-tuple-element.28.chip), channel_id=1, source_target_pairs={{0,15},{1,2},{2,1},{3,4},{4,3},{5,6},{6,5},{7,8},{8,7},{9,10},{10,... | collective-permute-start | bytes 393224 | tf_op jit(solution)/shard_map/ppermute | solution.py:300
  13.8 4.5 %collective-permute-start.6 = (f32[8,2048]{1,0:T(8,128)S(1)}, f32[8,2048]{1,0:T(8,128)S(1)}, u32[]{:S(2)}, u32[]{:S(2)}) collective-permute-start(f32[8,2048]{1,0:T(8,128)S(1)} %get-tuple-element.38.own_z), channel_id=1, source_target_pairs={{0,15},{1,0},{2,1},{3,2},{4,3},{5,4},{6,5},{7,6},{8,7},{9,8},{10,9... | collective-permute-start | bytes 196616 | tf_op jit(solution)/shard_map/ppermute | solution.py:301
  15.7 1.0 %copy-start.3 = (f32[8,8,2048]{2,1,0:T(8,128)S(1)}, f32[8,8,2048]{2,1,0:T(8,128)}, u32[]{:S(2)}) copy-start(f32[8,8,2048]{2,1,0:T(8,128)} %flow_z.3) | copy-start | bytes 1572868
  16.4 5.5 %collective-permute-start.5 = (f32[2,8,2048]{2,1,0:T(8,128)S(1)}, f32[2,8,2048]{2,1,0:T(8,128)S(1)}, u32[]{:S(2)}, u32[]{:S(2)}) collective-permute-start(f32[2,8,2048]{2,1,0:T(8,128)S(1)} %get-tuple-element.34.core), channel_id=1, source_target_pairs={{0,1},{1,0},{2,3},{3,2},{4,5},{5,4},{6,7},{7,6},{8,9},{9,8},{10,11... | collective-permute-start | bytes 393224 | tf_op jit(solution)/shard_map/ppermute | solution.py:322

commit v4 on v3

--- a/solution.py
+++ b/solution.py
@@ -41,8 +41,7 @@
 
 
 def x_columns(
-    fraction, flow_x, flow_y, flow_z, first, start, courant, upward, downward, own_y, own_z,
-    flows, sems,
+    fraction, flow_x, flow_y, flow_z, first, start, courant, near, far, own_y, own_z, flows, sems,
 ):
     rows, columns, _ = fraction.shape
     column = lax.rem(lax.axis_index("col"), 2) * (columns - 2)
@@ -57,16 +56,18 @@
         load.start()
     for load in loads[:4]:
         load.wait()
+    odd = lax.rem(lax.axis_index("row"), 2) == 1
     for m in range(2):
-        result = x_sweep_row(start[m], flows[m])
-        first[m] = result
+        first[m] = x_sweep_row(start[m], flows[m])
         for i in range(2):
-            upward[i, m : m + 1] = result[rows - 2 + i : rows - 1 + i]
-            downward[i, m : m + 1] = result[i : i + 1]
+            up, down = first[m, rows - 2 + i : rows - 1 + i], first[m, i : i + 1]
+            near[i, m : m + 1] = lax.select(odd, down, up)
+            far[i, m : m + 1] = lax.select(odd, up, down)
     for load in loads[4:]:
         load.wait()
     for m in range(2):
-        downward[2, m : m + 1] = courant[m, :1]
+        near[2, m : m + 1] = courant[m, :1]
+        far[2, m : m + 1] = courant[m, :1]
 
 
 def x_rows(fraction, flow_x, own_y, high, low, upward, downward):
@@ -93,16 +94,22 @@
         middle[i] = x_sweep_row(fraction[i + 2], flow_x[i + 2])
 
 
-def y_columns(first, start, courant, high, lower, upper, own_z, chip, own_z_out):
+def y_columns(
+    first, start, courant, near, near_side, far, far_side, own_z, chip, own_z_out, lower, upper
+):
     _, rows, length = first.shape
     own_z_out[...] = own_z[...]
+    odd = lax.rem(lax.axis_index("row"), 2) == 1
+    lower[...] = lax.select(odd, near_side[...], far_side[...])
+    upper[...] = lax.select(odd, far_side[...], near_side[...])
     place = lax.broadcasted_iota(jnp.int32, (rows, CHUNK), 0)
     bottom = place == 0
     top = place == rows - 1
     for j in range(length // CHUNK):
         at = slice(j * CHUNK, (j + 1) * CHUNK)
+        high = [lax.select(odd, far[i, :, at], near[i, :, at]) for i in range(2)]
         last_flux = face_flux(
-            high[0, :, at], high[1, :, at], upper[0, :, at], upper[1, :, at], upper[2, :, at]
+            *high, upper[0, :, at], upper[1, :, at], upper[2, :, at]
         )
         for m in range(2):
             one = slice(m, m + 1)
@@ -257,11 +264,11 @@
     inputs = [
         pltpu.with_memory_space_constraint(x, pltpu.HBM) for x in (fraction, flow_x, flow_y, flow_z)
     ]
-    edge, side = array(2, rows, length), array(2, 2, length)
-    first, start, courant, upward, downward, own_y, own_z = pl.pallas_call(
+    edge, side = array(2, rows, length), array(3, 2, length)
+    first, start, courant, near, far, own_y, own_z = pl.pallas_call(
         x_columns,
         out_shape=(
-            edge, edge, edge, side, array(3, 2, length), array(columns, length), array(rows, length)
+            edge, edge, edge, side, side, array(columns, length), array(rows, length)
         ),
         in_specs=[hbm] * 4,
         out_specs=[vmem] * 7,
@@ -269,8 +276,8 @@
         compiler_params=params,
         name="x_columns",
     )(*inputs)
-    column_lower = lax.ppermute(upward, "row", up(n_row))
-    column_upper = lax.ppermute(downward, "row", down(n_row))
+    near_side = lax.ppermute(near, "row", with_above(n_row))
+    far_side = lax.ppermute(far, "row", with_below(n_row))
     pairs = columns // 2 - 1
     high, low, upward_pairs, downward_pairs = pl.pallas_call(
         x_rows,
@@ -288,15 +295,15 @@
     )(fraction, flow_x, own_y)
     lower_pairs = lax.ppermute(upward_pairs, "row", up(n_row))
     upper_pairs = lax.ppermute(downward_pairs, "row", down(n_row))
-    chip, own_z = pl.pallas_call(
+    chip, own_z, column_lower, column_upper = pl.pallas_call(
         y_columns,
-        out_shape=(edge, array(rows, length)),
-        in_specs=[vmem] * 7,
-        out_specs=[vmem] * 2,
+        out_shape=(edge, array(rows, length), side, side),
+        in_specs=[vmem] * 8,
+        out_specs=[vmem] * 4,
         compiler_params=params,
         cost_estimate=busy,
         name="y_columns",
-    )(first, start, courant, upward, column_lower, column_upper, own_z)
+    )(first, start, courant, near, near_side, far, far_side, own_z)
     chip_side = lax.ppermute(chip, "col", with_below(n_col))
     courant_z = lax.ppermute(own_z, "col", down(n_col))
     middle = pl.pallas_call(
@@ -306,7 +313,7 @@
         out_specs=vmem,
         compiler_params=params,
         name="x_middle",
-    )(fraction, flow_x, chip)
+    )(fraction, flow_x, upper_pairs)
     second, core = pl.pallas_call(
         y_sweep,
         out_shape=(array(*block), edge),

time: 23.1 us -> 22.9 us (level)
  waiting for transfers between devices: 4.48 us -> 3.83 us
  starting transfers between devices: 13.1 us -> 13.6 us
    ppermute x2, starting transfers between devices: 2.44 us -> 3.47 us  [the longest x1 2.36 us: per_device(): near_side = lax.ppermute(near, 'row', with_above(n_row))]
    ppermute x1, starting transfers between devices: 5.12 us -> 4.55 us  [per_device(): upper_pairs = lax.ppermute(downward_pairs, 'row', down(n_row))]
    ppermute x1, waiting for transfers between devices: 0.86 us -> 0.36 us  [per_device(): courant_z = lax.ppermute(own_z, 'col', down(n_col))]
where the time goes in v4:
time: 22.9 us; the launch traced here: 22.8 us
  starting transfers between devices  13.6 us (59%)
  Pallas kernels  5.09 us (22%)
  waiting for transfers between devices  3.83 us (17%)
  local copies, waits for them, and re-layouts  0.24 us (1%)
    ppermute x1, starting transfers between devices, per_device(): upper_pairs = lax.ppermute(downward_pairs, 'row', down(n_row))  4.55 us
    ppermute x1, starting transfers between devices, per_device(): chip_side = lax.ppermute(chip, 'col', with_below(n_col))  3.56 us
    ppermute x1, waiting for transfers between devices, per_device(): chip_side = lax.ppermute(chip, 'col', with_below(n_col))  3.46 us
    ppermute x1, starting transfers between devices, per_device(): near_side = lax.ppermute(near, 'row', with_above(n_row))  2.36 us
    ppermute x1, starting transfers between devices, per_device(): courant_z = lax.ppermute(own_z, 'col', down(n_col))  1.89 us
    pallas_call x1, Pallas kernels, per_device(): pl.pallas_call(x_columns, out_shape=(edge, edge, edge, side, side, array(...  1.43 us
    ppermute x1, starting transfers between devices, per_device(): far_side = lax.ppermute(far, 'row', with_below(n_row))  1.11 us
    pallas_call x1, Pallas kernels, per_device(): pl.pallas_call(z_outer, out_shape=array(*block), in_specs=[vmem] * 8, out...  1.06 us
  transfers between devices with their start and end apart: 7, of which 2 were waited for; matrix products, arithmetic and copies ran while one was open for 0% of the time, Pallas kernels for 11%

profile of v4, /device:TPU:2, one launch (start us, length us, event | category | flops | bytes accessed | tf_op | source)
XLA Modules:
  0.0 22.8 jit_solution(13114472710322112316)
XLA Ops:
  0.0 0.0 copy-start.1
  0.0 0.0 copy-start
  0.0 1.4 %x_columns.1 = (f32[2,8,2048]{2,1,0:T(8,128)S(1)}, f32[2,8,2048]{2,1,0:T(8,128)S(1)}, f32[2,8,2048]{2,1,0:T(8,128)S(1)}, f32[3,2,2048]{2,1,0:T(2,128)S(1)}, f32[...) custom-call(f32[8,8,2048]{2,1,0:T(8,128)} %fraction.9, f32[8,8,2048]{2,1,0:T(8,128)} %flow_x.5, ...), custom_call_target="tpu_custom_call" | custom-call | tf_op jit(solution)/shard_map/x_columns/pallas_call | solution.py:268
  1.4 2.4 %collective-permute-start = (f32[3,2,2048]{2,1,0:T(2,128)S(1)}, f32[3,2,2048]{2,1,0:T(2,128)S(1)}, u32[]{:S(2)}, u32[]{:S(2)}) collective-permute-start(f32[3,2,2048]{2,1,0:T(2,128)S(1)} %get-tuple-element.27.near), channel_id=1, source_target_pairs={{0,16},{16,0},{32,48},{48,32},{64,80},{80,64},{96,112},{112,96},{1... | collective-permute-start | bytes 147464 | tf_op jit(solution)/shard_map/ppermute | solution.py:279
  3.8 1.1 %collective-permute-start.1 = (f32[3,2,2048]{2,1,0:T(2,128)S(1)}, f32[3,2,2048]{2,1,0:T(2,128)S(1)}, u32[]{:S(2)}, u32[]{:S(2)}) collective-permute-start(f32[3,2,2048]{2,1,0:T(2,128)S(1)} %get-tuple-element.28.far), channel_id=1, source_target_pairs={{0,240},{16,32},{32,16},{48,64},{64,48},{80,96},{96,80},{112,128},... | collective-permute-start | bytes 147464 | tf_op jit(solution)/shard_map/ppermute | solution.py:280
  4.9 0.0 copy-done.1
  4.9 0.0 copy-done
  4.9 0.5 %x_rows.1 = (f32[2,8,2048]{2,1,0:T(8,128)S(1)}, f32[2,8,2048]{2,1,0:T(8,128)S(1)}, f32[6,2,2048]{2,1,0:T(2,128)S(1)}, f32[9,2,2048]{2,1,0:T(2,128)S(1)}) custom-call(f32[8,8,2048]{2,1,0:T(8,128)S(1)} %copy-done.1, f32[8,8,2048]{2,1,0:T(8,128)S(1)} %copy-done, f32[8,2048]{1,0:T(8,128)S(1)} %get-tuple-element.31.own_y), custom_call_target="tpu_custom_call" | custom-call | flops 10000000000 | bytes 10000000 | tf_op jit(solution)/shard_map/x_rows/pallas_call | solution.py:282
  5.4 4.5 %collective-permute-start.4 = (f32[9,2,2048]{2,1,0:T(2,128)S(1)}, f32[9,2,2048]{2,1,0:T(2,128)S(1)}, u32[]{:S(2)}, u32[]{:S(2)}) collective-permute-start(f32[9,2,2048]{2,1,0:T(2,128)S(1)} %get-tuple-element.35), channel_id=1, source_target_pairs={{0,240},{16,0},{32,16},{48,32},{64,48},{80,64},{96,80},{112,96},{1... | collective-permute-start | bytes 442376 | tf_op jit(solution)/shard_map/ppermute | solution.py:297
  10.0 0.0 collective-permute-start.3
  10.0 0.0 collective-permute-done.near_side
  10.0 0.0 collective-permute-done.1.far_side
  10.0 0.2 y_columns.1
  10.2 3.6 %collective-permute-start.2 = (f32[2,8,2048]{2,1,0:T(8,128)S(1)}, f32[2,8,2048]{2,1,0:T(8,128)S(1)}, u32[]{:S(2)}, u32[]{:S(2)}) collective-permute-start(f32[2,8,2048]{2,1,0:T(8,128)S(1)} %get-tuple-element.30.chip), channel_id=1, source_target_pairs={{0,15},{1,2},{2,1},{3,4},{4,3},{5,6},{6,5},{7,8},{8,7},{9,10},{10,... | collective-permute-start | bytes 393224 | tf_op jit(solution)/shard_map/ppermute | solution.py:307
  13.8 0.0 copy-start.2
  13.8 1.9 %collective-permute-start.6 = (f32[8,2048]{1,0:T(8,128)S(1)}, f32[8,2048]{1,0:T(8,128)S(1)}, u32[]{:S(2)}, u32[]{:S(2)}) collective-permute-start(f32[8,2048]{1,0:T(8,128)S(1)} %get-tuple-element.42.own_z), channel_id=1, source_target_pairs={{0,15},{1,0},{2,1},{3,2},{4,3},{5,4},{6,5},{7,6},{8,7},{9,8},{10,9... | collective-permute-start | bytes 196616 | tf_op jit(solution)/shard_map/ppermute | solution.py:308
  15.7 0.0 collective-permute-done.4.chip.upper_pairs
  15.7 0.5 %x_middle.1.middle = f32[4,8,2048]{2,1,0:T(8,128)S(1)} custom-call(f32[8,8,2048]{2,1,0:T(8,128)S(1)} %copy-done.1, f32[8,8,2048]{2,1,0:T(8,128)S(1)} %copy-done, f32[9,2,2048]{2,1,0:T(2,128)S(1)} %collective-permute-done.4.chip.upper_pairs), custom_call_target="tpu_custom_call" | custom-call | tf_op jit(solution)/shard_map/x_middle/pallas_call | solution.py:309
  16.2 0.0 collective-permute-done.3.lower_pairs
  16.2 0.0 copy-done.2
  16.2 0.0 copy-start.3
  16.2 0.7 %y_sweep.1 = (f32[8,8,2048]{2,1,0:T(8,128)S(1)}, f32[2,8,2048]{2,1,0:T(8,128)S(1)}) custom-call(f32[2,8,2048]{2,1,0:T(8,128)S(1)} %get-tuple-element.32.high, f32[6,2,2048]{2,1,0:T(2,128)S(1)} %collective-permute-done.3.lower_pairs, f32[2,8,2048]{2,1,0:T(8,128)S(1)} %get-tuple-element.34.low, f32[9,2,2048]{2,1,0:T(2,128)S(1)} %collective-permute-done.4.chip.upper_pairs, ...), custom_call_target="tpu_custom_call" | custom-call | flops 10000000000 | bytes 10000000 | tf_op jit(solution)/shard_map/y_sweep/pallas_call | solution.py:317
  16.9 0.1 collective-permute-start.5
  17.0 0.2 copy-done.3
  17.2 0.7 %z_inner.1 = (f32[8,8,2048]{2,1,0:T(8,128)S(1)}, f32[5,8,2048]{2,1,0:T(8,128)S(1)}) custom-call(f32[8,8,2048]{2,1,0:T(8,128)S(1)} %get-tuple-element.39.second, f32[8,8,2048]{2,1,0:T(8,128)S(1)} %copy-done.3, f32[8,8,2048]{2,1,0:T(8,128)S(1)} %copy-done.1), custom_call_target="tpu_custom_call" | custom-call | flops 10000000000 | bytes 10000000 | tf_op jit(solution)/shard_map/z_inner/pallas_call | solution.py:330
  17.9 0.4 %collective-permute-done.6.courant_z = f32[8,2048]{1,0:T(8,128)S(1)} collective-permute-done((f32[8,2048]{1,0:T(8,128)S(1)}, f32[8,2048]{1,0:T(8,128)S(1)}, u32[]{:S(2)}, u32[]{:S(2)}) %collective-permute-start.6) | collective-permute-done | bytes 65568 | tf_op jit(solution)/shard_map/ppermute | solution.py:308
  18.3 3.5 %collective-permute-done.2.chip_side = f32[2,8,2048]{2,1,0:T(8,128)S(1)} collective-permute-done((f32[2,8,2048]{2,1,0:T(8,128)S(1)}, f32[2,8,2048]{2,1,0:T(8,128)S(1)}, u32[]{:S(2)}, u32[]{:S(2)}) %collective-permute-start.2) | collective-permute-done | bytes 131104 | tf_op jit(solution)/shard_map/ppermute | solution.py:307
  21.7 0.0 collective-permute-done.5.core_side
  21.7 1.1 %z_outer.1 = f32[8,8,2048]{2,1,0:T(8,128)} custom-call(f32[2,8,2048]{2,1,0:T(8,128)S(1)} %get-tuple-element.30.chip, f32[2,8,2048]{2,1,0:T(8,128)S(1)} %collective-permute-done.2.chip_side, f32[2,8,2048]{2,1,0:T(8,128)S(1)} %get-tuple-element.38.core, f32[2,8,2048]{2,1,0:T(8,128)S(1)} %collective-permute-done.5.core_side, ...), custom_call_target="tpu_custom_call" | custom-call | tf_op jit(solution)/shard_map/z_outer/pallas_call | solution.py:339
Async XLA Ops:
  0.0 4.9 %copy-start.1 = (f32[8,8,2048]{2,1,0:T(8,128)S(1)}, f32[8,8,2048]{2,1,0:T(8,128)}, u32[]{:S(2)}) copy-start(f32[8,8,2048]{2,1,0:T(8,128)} %fraction.9) | copy-start | bytes 1572868
  0.0 4.9 %copy-start = (f32[8,8,2048]{2,1,0:T(8,128)S(1)}, f32[8,8,2048]{2,1,0:T(8,128)}, u32[]{:S(2)}) copy-start(f32[8,8,2048]{2,1,0:T(8,128)} %flow_x.5) | copy-start | bytes 1572868
  1.4 8.6 %collective-permute-start = (f32[3,2,2048]{2,1,0:T(2,128)S(1)}, f32[3,2,2048]{2,1,0:T(2,128)S(1)}, u32[]{:S(2)}, u32[]{:S(2)}) collective-permute-start(f32[3,2,2048]{2,1,0:T(2,128)S(1)} %get-tuple-element.27.near), channel_id=1, source_target_pairs={{0,16},{16,0},{32,48},{48,32},{64,80},{80,64},{96,112},{112,96},{1... | collective-permute-start | bytes 147464 | tf_op jit(solution)/shard_map/ppermute | solution.py:279
  3.8 6.2 %collective-permute-start.1 = (f32[3,2,2048]{2,1,0:T(2,128)S(1)}, f32[3,2,2048]{2,1,0:T(2,128)S(1)}, u32[]{:S(2)}, u32[]{:S(2)}) collective-permute-start(f32[3,2,2048]{2,1,0:T(2,128)S(1)} %get-tuple-element.28.far), channel_id=1, source_target_pairs={{0,240},{16,32},{32,16},{48,64},{64,48},{80,96},{96,80},{112,128},... | collective-permute-start | bytes 147464 | tf_op jit(solution)/shard_map/ppermute | solution.py:280
  5.4 10.2 %collective-permute-start.4 = (f32[9,2,2048]{2,1,0:T(2,128)S(1)}, f32[9,2,2048]{2,1,0:T(2,128)S(1)}, u32[]{:S(2)}, u32[]{:S(2)}) collective-permute-start(f32[9,2,2048]{2,1,0:T(2,128)S(1)} %get-tuple-element.35), channel_id=1, source_target_pairs={{0,240},{16,0},{32,16},{48,32},{64,48},{80,64},{96,80},{112,96},{1... | collective-permute-start | bytes 442376 | tf_op jit(solution)/shard_map/ppermute | solution.py:297
  10.0 6.2 %collective-permute-start.3 = (f32[6,2,2048]{2,1,0:T(2,128)S(1)}, f32[6,2,2048]{2,1,0:T(2,128)S(1)}, u32[]{:S(2)}, u32[]{:S(2)}) collective-permute-start(f32[6,2,2048]{2,1,0:T(2,128)S(1)} %get-tuple-element.33), channel_id=1, source_target_pairs={{0,16},{16,32},{32,48},{48,64},{64,80},{80,96},{96,112},{112,128},... | collective-permute-start | bytes 294920 | tf_op jit(solution)/shard_map/ppermute | solution.py:296
  10.2 11.5 %collective-permute-start.2 = (f32[2,8,2048]{2,1,0:T(8,128)S(1)}, f32[2,8,2048]{2,1,0:T(8,128)S(1)}, u32[]{:S(2)}, u32[]{:S(2)}) collective-permute-start(f32[2,8,2048]{2,1,0:T(8,128)S(1)} %get-tuple-element.30.chip), channel_id=1, source_target_pairs={{0,15},{1,2},{2,1},{3,4},{4,3},{5,6},{6,5},{7,8},{8,7},{9,10},{10,... | collective-permute-start | bytes 393224 | tf_op jit(solution)/shard_map/ppermute | solution.py:307
  13.8 2.4 %copy-start.2 = (f32[8,8,2048]{2,1,0:T(8,128)S(1)}, f32[8,8,2048]{2,1,0:T(8,128)}, u32[]{:S(2)}) copy-start(f32[8,8,2048]{2,1,0:T(8,128)} %flow_y.3) | copy-start | bytes 1572868
  13.8 4.5 %collective-permute-start.6 = (f32[8,2048]{1,0:T(8,128)S(1)}, f32[8,2048]{1,0:T(8,128)S(1)}, u32[]{:S(2)}, u32[]{:S(2)}) collective-permute-start(f32[8,2048]{1,0:T(8,128)S(1)} %get-tuple-element.42.own_z), channel_id=1, source_target_pairs={{0,15},{1,0},{2,1},{3,2},{4,3},{5,4},{6,5},{7,6},{8,7},{9,8},{10,9... | collective-permute-start | bytes 196616 | tf_op jit(solution)/shard_map/ppermute | solution.py:308
  16.2 1.0 %copy-start.3 = (f32[8,8,2048]{2,1,0:T(8,128)S(1)}, f32[8,8,2048]{2,1,0:T(8,128)}, u32[]{:S(2)}) copy-start(f32[8,8,2048]{2,1,0:T(8,128)} %flow_z.3) | copy-start | bytes 1572868
  16.9 4.8 %collective-permute-start.5 = (f32[2,8,2048]{2,1,0:T(8,128)S(1)}, f32[2,8,2048]{2,1,0:T(8,128)S(1)}, u32[]{:S(2)}, u32[]{:S(2)}) collective-permute-start(f32[2,8,2048]{2,1,0:T(8,128)S(1)} %get-tuple-element.38.core), channel_id=1, source_target_pairs={{0,1},{1,0},{2,3},{3,2},{4,5},{5,4},{6,7},{7,6},{8,9},{9,8},{10,11... | collective-permute-start | bytes 393224 | tf_op jit(solution)/shard_map/ppermute | solution.py:329

commit v5 on v4

--- a/solution.py
+++ b/solution.py
@@ -125,10 +125,11 @@
 
 def y_sweep(
     high, lower_pairs, low, upper_pairs, lower_edge, upper_edge, middle, flow_y, fraction,
-    second, core, halo,
+    own_z, second, core, halo,
 ):
     rows, columns, length = second.shape
     odd_core = lax.rem(lax.axis_index("col"), 2) == 1
+    core[2] = own_z[...]
     pairs = columns // 2 - 1
     for edge, rest, slabs in ((lower_edge, lower_pairs, (0, 1)), (upper_edge, upper_pairs, (2, 3, 4))):
         for m, slab in enumerate(slabs):
@@ -162,11 +163,13 @@
     lax.fori_loop(0, length // LANES, tile, None, unroll=2)
 
 
-def z_inner(second, flow_z, fraction, base, inside):
+def z_inner(second, flow_z, fraction, out, inside, base, sems):
     rows, columns, length = second.shape
+    odd_core = lax.rem(lax.axis_index("col"), 2) == 1
     place = lax.broadcasted_iota(jnp.int32, (columns, CHUNK), 0)
     top = place == columns - 1
     inner = (place >= 2) & (place <= columns - 2)
+    stores = []
     for i in range(rows):
         for j in range(length // CHUNK):
             at = slice(j * CHUNK, (j + 1) * CHUNK)
@@ -182,56 +185,71 @@
             flux = jnp.where(inner, flux, 0.0)
             next_courant = jnp.where(top, 0.0, pltpu.roll(courant, columns - 1, 0))
             start = fraction[i, :, at]
-            base[i, :, at] = updated(
+            result = updated(
                 here, flux, pltpu.roll(flux, columns - 1, 0), courant, next_courant, start
             )
+            base[i, :, at] = result
             inside[4, i : i + 1, at] = start[columns - 1 :]
+            for m in range(2):
+                upper, lower = result[columns - 2 + m : columns - 1 + m], result[m : m + 1]
+                inside[5 + m, i : i + 1, at] = lax.select(odd_core, upper, lower)
+                inside[7 + m, i : i + 1, at] = lax.select(odd_core, lower, upper)
             inside[0, i : i + 1, at] = here[2:3]
             inside[1, i : i + 1, at] = here[columns - 3 : columns - 2]
             inside[2, i : i + 1, at] = courant[1:2]
             inside[3, i : i + 1, at] = courant[columns - 1 :]
-
-
-def z_outer(
-    chip, chip_side, core, core_side, base, inside, own_z, courant_z, out,
-    part, change, sems,
-):
-    rows, columns, length = base.shape
+        stores.append(pltpu.make_async_copy(base.at[i], out.at[i], sems.at[i]))
+        stores[-1].start()
+    for store in stores:
+        store.wait()
+
+
+def side_change(is_lower, own, side, inside, own_z, last_flow, at):
+    mine = [own[m, :, at] for m in range(2)]
+    theirs = [side[m, :, at] for m in range(2)]
+
+    def pick(lower, upper):
+        return [lax.select(is_lower, x, y) for x, y in zip(lower, upper)]
+
+    outer = face_flux(
+        *pick([*theirs, *mine, own_z[:, at]], [inside[1, :, at], *mine, theirs[0], inside[3, :, at]])
+    )
+    inner = face_flux(
+        *pick([theirs[1], *mine, inside[0, :, at], inside[2, :, at]], [*mine, *theirs, last_flow])
+    )
+    spread = jnp.where(inside[4, :, at] > 0.5, last_flow, 0.0)
+    return pick([outer - inner, inner], [-outer, outer - inner + spread])
+
+
+def z_core(core, core_side, inside, own_z, values):
     odd_core = lax.rem(lax.axis_index("col"), 2) == 1
-    place = lax.broadcasted_iota(jnp.int32, (columns, CHUNK), 0)
-    pieces = [slice(j * CHUNK, (j + 1) * CHUNK) for j in range(length // CHUNK)]
-
-    for at in pieces:
-
-        def ordered(a, b, at=at):
-            pairs = [(a[m, :, at], b[m, :, at]) for m in range(a.shape[0])]
-            return [lax.select(odd_core, x, y) for x, y in pairs], [
-                lax.select(odd_core, y, x) for x, y in pairs
-            ]
-
-        below, above = ordered(core_side, chip_side)
-        low, high = ordered(core, chip)
-        after_low, before_high = inside[0, :, at], inside[1, :, at]
-        flux = [
-            face_flux(*below, *low, own_z[:, at]),
-            face_flux(below[1], *low, after_low, inside[2, :, at]),
-            face_flux(before_high, *high, above[0], inside[3, :, at]),
-            face_flux(*high, *above, courant_z[:, at]),
-        ]
-        change[0, :, at] = flux[0] - flux[1]
-        change[1, :, at] = flux[1]
-        change[2, :, at] = -flux[2]
-        spread = jnp.where(inside[4, :, at] > 0.5, courant_z[:, at], 0.0)
-        change[3, :, at] = flux[2] - flux[3] + spread
-
-    stores = []
-    for i in range(rows):
-        for at in pieces:
-            value = jnp.zeros((columns, CHUNK), base.dtype)
-            for n, column in enumerate((0, 1, columns - 2, columns - 1)):
-                value = jnp.where(place == column, change[n, i : i + 1, at], value)
-            part[i, :, at] = base[i, :, at] + value
-        stores.append(pltpu.make_async_copy(part.at[i], out.at[i], sems.at[i]))
+    for j in range(values.shape[2] // CHUNK):
+        at = slice(j * CHUNK, (j + 1) * CHUNK)
+        change = side_change(odd_core, core, core_side, inside, own_z, core_side[2, :, at], at)
+        for m in range(2):
+            values[m, :, at] = inside[7 + m, :, at] + change[m]
+
+
+def z_chip(chip, chip_side, inside, own_z, courant_z, values, result, out, part, sems):
+    del result
+    columns, length = out.shape[1:]
+    upper_side = lax.rem(lax.axis_index("col"), 2)
+    column = upper_side * (columns - 2)
+    other = (1 - upper_side) * (columns - 2)
+    stores = [
+        pltpu.make_async_copy(values.at[m], out.at[:, other + m], sems.at[m]) for m in range(2)
+    ]
+    for store in stores:
+        store.start()
+    for j in range(length // CHUNK):
+        at = slice(j * CHUNK, (j + 1) * CHUNK)
+        change = side_change(
+            upper_side == 0, chip, chip_side, inside, own_z, courant_z[:, at], at
+        )
+        for m in range(2):
+            part[m, :, at] = inside[5 + m, :, at] + change[m]
+    for m in range(2):
+        stores.append(pltpu.make_async_copy(part.at[m], out.at[:, column + m], sems.at[2 + m]))
         stores[-1].start()
     for store in stores:
         store.wait()
@@ -316,39 +334,46 @@
     )(fraction, flow_x, upper_pairs)
     second, core = pl.pallas_call(
         y_sweep,
-        out_shape=(array(*block), edge),
-        in_specs=[vmem] * 9,
+        out_shape=(array(*block), array(3, rows, length)),
+        in_specs=[vmem] * 10,
         out_specs=[vmem] * 2,
         scratch_shapes=[pltpu.VMEM((5, columns, length), dtype)],
         compiler_params=params,
         cost_estimate=busy,
         name="y_sweep",
     )(
-        high, lower_pairs, low, upper_pairs, column_lower, column_upper, middle, flow_y, fraction
+        high, lower_pairs, low, upper_pairs, column_lower, column_upper, middle, flow_y, fraction,
+        own_z,
     )
     core_side = lax.ppermute(core, "col", with_above(n_col))
-    base, inside = pl.pallas_call(
+    result, inside = pl.pallas_call(
         z_inner,
-        out_shape=(array(*block), array(5, rows, length)),
+        out_shape=(array(*block), array(9, rows, length)),
         in_specs=[vmem] * 3,
-        out_specs=[vmem] * 2,
+        out_specs=[hbm, vmem],
+        scratch_shapes=[pltpu.VMEM(block, dtype), dma((rows,))],
         compiler_params=params,
         cost_estimate=busy,
         name="z_inner",
     )(second, flow_z, fraction)
+    values = pl.pallas_call(
+        z_core,
+        out_shape=edge,
+        in_specs=[vmem] * 4,
+        out_specs=vmem,
+        compiler_params=params,
+        name="z_core",
+    )(core, core_side, inside, own_z)
     return pl.pallas_call(
-        z_outer,
+        z_chip,
         out_shape=array(*block),
-        in_specs=[vmem] * 8,
+        in_specs=[vmem] * 6 + [hbm],
         out_specs=hbm,
-        scratch_shapes=[
-            pltpu.VMEM(block, dtype),
-            pltpu.VMEM((4, rows, length), dtype),
-            dma((rows,)),
-        ],
-        compiler_params=params,
-        name="z_outer",
-    )(chip, chip_side, core, core_side, base, inside, own_z, courant_z)
+        scratch_shapes=[pltpu.VMEM((2, rows, length), dtype), dma((4,))],
+        input_output_aliases={6: 0},
+        compiler_params=params,
+        name="z_chip",
+    )(chip, chip_side, inside, own_z, courant_z, values, result)
 
 
 def solution(mesh):

time: 22.9 us -> 22.7 us (level)
  waiting for transfers between devices: 3.83 us -> 3.1 us
  Pallas kernels: 5.09 us -> 5.53 us
    pallas_call x3 -> x4, Pallas kernels: 2.43 us -> 2.87 us  [the longest x1 1.23 us: per_device(): pl.pallas_call(z_inner, out_shape=(array(*block), array(9, rows, length))...]
    ppermute x1, waiting for transfers between devices: 3.46 us -> 3.09 us  [per_device(): chip_side = lax.ppermute(chip, 'col', with_below(n_col))]
    ppermute x1, waiting for transfers between devices: 0.36 us -> 0.01 us  [per_device(): courant_z = lax.ppermute(own_z, 'col', down(n_col))]
  transfers between devices with their start and end apart: 7 -> 7, of which waited for: 2 -> 1; matrix products, arithmetic and copies ran while one was open for 0% -> 0% of each run, Pallas kernels for 11% -> 15%
where the time goes in v5:
time: 22.7 us; the launch traced here: 22.5 us
  starting transfers between devices  13.6 us (60%)
  Pallas kernels  5.53 us (24%)
  waiting for transfers between devices  3.1 us (14%)
  local copies, waits for them, and re-layouts  0.24 us (1%)
    ppermute x1, starting transfers between devices, per_device(): upper_pairs = lax.ppermute(downward_pairs, 'row', down(n_row))  4.55 us
    ppermute x1, starting transfers between devices, per_device(): chip_side = lax.ppermute(chip, 'col', with_below(n_col))  3.56 us
    ppermute x1, waiting for transfers between devices, per_device(): chip_side = lax.ppermute(chip, 'col', with_below(n_col))  3.09 us
    ppermute x1, starting transfers between devices, per_device(): near_side = lax.ppermute(near, 'row', with_above(n_row))  2.36 us
    ppermute x1, starting transfers between devices, per_device(): courant_z = lax.ppermute(own_z, 'col', down(n_col))  1.89 us
    pallas_call x1, Pallas kernels, per_device(): pl.pallas_call(x_columns, out_shape=(edge, edge, edge, side, side, array(...  1.43 us
    pallas_call x1, Pallas kernels, per_device(): pl.pallas_call(z_inner, out_shape=(array(*block), array(9, rows, length))...  1.23 us
    ppermute x1, starting transfers between devices, per_device(): far_side = lax.ppermute(far, 'row', with_below(n_row))  1.11 us
  transfers between devices with their start and end apart: 7, of which 1 were waited for; matrix products, arithmetic and copies ran while one was open for 0% of the time, Pallas kernels for 15%

profile of v5, /device:TPU:2, one launch (start us, length us, event | category | flops | bytes accessed | tf_op | source)
XLA Modules:
  0.0 22.5 jit_solution(3301985010907439116)
XLA Ops:
  0.0 0.0 copy-start.1
  0.0 0.0 copy-start
  0.0 1.4 %x_columns.1 = (f32[2,8,2048]{2,1,0:T(8,128)S(1)}, f32[2,8,2048]{2,1,0:T(8,128)S(1)}, f32[2,8,2048]{2,1,0:T(8,128)S(1)}, f32[3,2,2048]{2,1,0:T(2,128)S(1)}, f32[...) custom-call(f32[8,8,2048]{2,1,0:T(8,128)} %fraction.9, f32[8,8,2048]{2,1,0:T(8,128)} %flow_x.5, ...), custom_call_target="tpu_custom_call" | custom-call | tf_op jit(solution)/shard_map/x_columns/pallas_call | solution.py:286
  1.4 2.4 %collective-permute-start = (f32[3,2,2048]{2,1,0:T(2,128)S(1)}, f32[3,2,2048]{2,1,0:T(2,128)S(1)}, u32[]{:S(2)}, u32[]{:S(2)}) collective-permute-start(f32[3,2,2048]{2,1,0:T(2,128)S(1)} %get-tuple-element.27.near), channel_id=1, source_target_pairs={{0,16},{16,0},{32,48},{48,32},{64,80},{80,64},{96,112},{112,96},{1... | collective-permute-start | bytes 147464 | tf_op jit(solution)/shard_map/ppermute | solution.py:297
  3.8 1.1 %collective-permute-start.1 = (f32[3,2,2048]{2,1,0:T(2,128)S(1)}, f32[3,2,2048]{2,1,0:T(2,128)S(1)}, u32[]{:S(2)}, u32[]{:S(2)}) collective-permute-start(f32[3,2,2048]{2,1,0:T(2,128)S(1)} %get-tuple-element.28.far), channel_id=1, source_target_pairs={{0,240},{16,32},{32,16},{48,64},{64,48},{80,96},{96,80},{112,128},... | collective-permute-start | bytes 147464 | tf_op jit(solution)/shard_map/ppermute | solution.py:298
  4.9 0.0 copy-done.1
  4.9 0.0 copy-done
  4.9 0.5 %x_rows.1 = (f32[2,8,2048]{2,1,0:T(8,128)S(1)}, f32[2,8,2048]{2,1,0:T(8,128)S(1)}, f32[6,2,2048]{2,1,0:T(2,128)S(1)}, f32[9,2,2048]{2,1,0:T(2,128)S(1)}) custom-call(f32[8,8,2048]{2,1,0:T(8,128)S(1)} %copy-done.1, f32[8,8,2048]{2,1,0:T(8,128)S(1)} %copy-done, f32[8,2048]{1,0:T(8,128)S(1)} %get-tuple-element.31.own_y), custom_call_target="tpu_custom_call" | custom-call | flops 10000000000 | bytes 10000000 | tf_op jit(solution)/shard_map/x_rows/pallas_call | solution.py:300
  5.4 4.5 %collective-permute-start.4 = (f32[9,2,2048]{2,1,0:T(2,128)S(1)}, f32[9,2,2048]{2,1,0:T(2,128)S(1)}, u32[]{:S(2)}, u32[]{:S(2)}) collective-permute-start(f32[9,2,2048]{2,1,0:T(2,128)S(1)} %get-tuple-element.35), channel_id=1, source_target_pairs={{0,240},{16,0},{32,16},{48,32},{64,48},{80,64},{96,80},{112,96},{1... | collective-permute-start | bytes 442376 | tf_op jit(solution)/shard_map/ppermute | solution.py:315
  10.0 0.0 collective-permute-start.3
  10.0 0.0 collective-permute-done.near_side
  10.0 0.0 collective-permute-done.1.far_side
  10.0 0.2 y_columns.1
  10.2 3.6 %collective-permute-start.2 = (f32[2,8,2048]{2,1,0:T(8,128)S(1)}, f32[2,8,2048]{2,1,0:T(8,128)S(1)}, u32[]{:S(2)}, u32[]{:S(2)}) collective-permute-start(f32[2,8,2048]{2,1,0:T(8,128)S(1)} %get-tuple-element.30.chip), channel_id=1, source_target_pairs={{0,15},{1,2},{2,1},{3,4},{4,3},{5,6},{6,5},{7,8},{8,7},{9,10},{10,... | collective-permute-start | bytes 393224 | tf_op jit(solution)/shard_map/ppermute | solution.py:325
  13.8 0.0 copy-start.2
  13.8 1.9 %collective-permute-start.5 = (f32[8,2048]{1,0:T(8,128)S(1)}, f32[8,2048]{1,0:T(8,128)S(1)}, u32[]{:S(2)}, u32[]{:S(2)}) collective-permute-start(f32[8,2048]{1,0:T(8,128)S(1)} %get-tuple-element.38.own_z), channel_id=1, source_target_pairs={{0,15},{1,0},{2,1},{3,2},{4,3},{5,4},{6,5},{7,6},{8,7},{9,8},{10,9... | collective-permute-start | bytes 196616 | tf_op jit(solution)/shard_map/ppermute | solution.py:326
  15.7 0.0 collective-permute-done.4.chip.upper_pairs
  15.7 0.5 %x_middle.1.middle = f32[4,8,2048]{2,1,0:T(8,128)S(1)} custom-call(f32[8,8,2048]{2,1,0:T(8,128)S(1)} %copy-done.1, f32[8,8,2048]{2,1,0:T(8,128)S(1)} %copy-done, f32[9,2,2048]{2,1,0:T(2,128)S(1)} %collective-permute-done.4.chip.upper_pairs), custom_call_target="tpu_custom_call" | custom-call | tf_op jit(solution)/shard_map/x_middle/pallas_call | solution.py:327
  16.2 0.0 collective-permute-done.3.lower_pairs
  16.2 0.0 copy-done.2
  16.2 0.0 copy-start.3
  16.2 0.7 %y_sweep.1 = (f32[8,8,2048]{2,1,0:T(8,128)S(1)}, f32[3,8,2048]{2,1,0:T(8,128)S(1)}) custom-call(f32[2,8,2048]{2,1,0:T(8,128)S(1)} %get-tuple-element.32.high, f32[6,2,2048]{2,1,0:T(2,128)S(1)} %collective-permute-done.3.lower_pairs, f32[2,8,2048]{2,1,0:T(8,128)S(1)} %get-tuple-element.34.low, f32[9,2,2048]{2,1,0:T(2,128)S(1)} %collective-permute-done.4.chip.upper_pairs, ...), custom_call_target="tpu_custom_call" | custom-call | flops 10000000000 | bytes 10000000 | tf_op jit(solution)/shard_map/y_sweep/pallas_call | solution.py:335
  16.9 0.1 collective-permute-start.6
  17.0 0.2 %copy-done.3 = f32[8,8,2048]{2,1,0:T(8,128)S(1)} copy-done((f32[8,8,2048]{2,1,0:T(8,128)S(1)}, f32[8,8,2048]{2,1,0:T(8,128)}, u32[]{:S(2)}) %copy-start.3) | copy-done | bytes 524312
  17.2 1.2 %z_inner.1 = (f32[8,8,2048]{2,1,0:T(8,128)}, f32[9,8,2048]{2,1,0:T(8,128)S(1)}) custom-call(f32[8,8,2048]{2,1,0:T(8,128)S(1)} %get-tuple-element.39.second, f32[8,8,2048]{2,1,0:T(8,128)S(1)} %copy-done.3, f32[8,8,2048]{2,1,0:T(8,128)S(1)} %copy-done.1), custom_call_target="tpu_custom_call" | custom-call | flops 10000000000 | bytes 10000000 | tf_op jit(solution)/shard_map/z_inner/pallas_call | solution.py:349
  18.5 0.0 collective-permute-done.6.core_side
  18.5 0.1 z_core.1.values
  18.6 0.0 collective-permute-done.5.courant_z
  18.6 3.1 %collective-permute-done.2.chip_side = f32[2,8,2048]{2,1,0:T(8,128)S(1)} collective-permute-done((f32[2,8,2048]{2,1,0:T(8,128)S(1)}, f32[2,8,2048]{2,1,0:T(8,128)S(1)}, u32[]{:S(2)}, u32[]{:S(2)}) %collective-permute-start.2) | collective-permute-done | bytes 131104 | tf_op jit(solution)/shard_map/ppermute | solution.py:325
  21.7 0.8 %z_chip.1 = f32[8,8,2048]{2,1,0:T(8,128)} custom-call(f32[2,8,2048]{2,1,0:T(8,128)S(1)} %get-tuple-element.30.chip, f32[2,8,2048]{2,1,0:T(8,128)S(1)} %collective-permute-done.2.chip_side, f32[9,8,2048]{2,1,0:T(8,128)S(1)} %get-tuple-element.40.inside, f32[8,2048]{1,0:T(8,128)S(1)} %get-tuple-element.38.own_z, ...), custom_call_target="tpu_custom_call", output_to_operand_aliasing={{}: (6, {})} | custom-call | tf_op jit(solution)/shard_map/z_chip/pallas_call | solution.py:367
Async XLA Ops:
  0.0 4.9 %copy-start.1 = (f32[8,8,2048]{2,1,0:T(8,128)S(1)}, f32[8,8,2048]{2,1,0:T(8,128)}, u32[]{:S(2)}) copy-start(f32[8,8,2048]{2,1,0:T(8,128)} %fraction.9) | copy-start | bytes 1572868
  0.0 4.9 %copy-start = (f32[8,8,2048]{2,1,0:T(8,128)S(1)}, f32[8,8,2048]{2,1,0:T(8,128)}, u32[]{:S(2)}) copy-start(f32[8,8,2048]{2,1,0:T(8,128)} %flow_x.5) | copy-start | bytes 1572868
  1.4 8.6 %collective-permute-start = (f32[3,2,2048]{2,1,0:T(2,128)S(1)}, f32[3,2,2048]{2,1,0:T(2,128)S(1)}, u32[]{:S(2)}, u32[]{:S(2)}) collective-permute-start(f32[3,2,2048]{2,1,0:T(2,128)S(1)} %get-tuple-element.27.near), channel_id=1, source_target_pairs={{0,16},{16,0},{32,48},{48,32},{64,80},{80,64},{96,112},{112,96},{1... | collective-permute-start | bytes 147464 | tf_op jit(solution)/shard_map/ppermute | solution.py:297
  3.8 6.2 %collective-permute-start.1 = (f32[3,2,2048]{2,1,0:T(2,128)S(1)}, f32[3,2,2048]{2,1,0:T(2,128)S(1)}, u32[]{:S(2)}, u32[]{:S(2)}) collective-permute-start(f32[3,2,2048]{2,1,0:T(2,128)S(1)} %get-tuple-element.28.far), channel_id=1, source_target_pairs={{0,240},{16,32},{32,16},{48,64},{64,48},{80,96},{96,80},{112,128},... | collective-permute-start | bytes 147464 | tf_op jit(solution)/shard_map/ppermute | solution.py:298
  5.4 10.2 %collective-permute-start.4 = (f32[9,2,2048]{2,1,0:T(2,128)S(1)}, f32[9,2,2048]{2,1,0:T(2,128)S(1)}, u32[]{:S(2)}, u32[]{:S(2)}) collective-permute-start(f32[9,2,2048]{2,1,0:T(2,128)S(1)} %get-tuple-element.35), channel_id=1, source_target_pairs={{0,240},{16,0},{32,16},{48,32},{64,48},{80,64},{96,80},{112,96},{1... | collective-permute-start | bytes 442376 | tf_op jit(solution)/shard_map/ppermute | solution.py:315
  10.0 6.2 %collective-permute-start.3 = (f32[6,2,2048]{2,1,0:T(2,128)S(1)}, f32[6,2,2048]{2,1,0:T(2,128)S(1)}, u32[]{:S(2)}, u32[]{:S(2)}) collective-permute-start(f32[6,2,2048]{2,1,0:T(2,128)S(1)} %get-tuple-element.33), channel_id=1, source_target_pairs={{0,16},{16,32},{32,48},{48,64},{64,80},{80,96},{96,112},{112,128},... | collective-permute-start | bytes 294920 | tf_op jit(solution)/shard_map/ppermute | solution.py:314
  10.2 11.5 %collective-permute-start.2 = (f32[2,8,2048]{2,1,0:T(8,128)S(1)}, f32[2,8,2048]{2,1,0:T(8,128)S(1)}, u32[]{:S(2)}, u32[]{:S(2)}) collective-permute-start(f32[2,8,2048]{2,1,0:T(8,128)S(1)} %get-tuple-element.30.chip), channel_id=1, source_target_pairs={{0,15},{1,2},{2,1},{3,4},{4,3},{5,6},{6,5},{7,8},{8,7},{9,10},{10,... | collective-permute-start | bytes 393224 | tf_op jit(solution)/shard_map/ppermute | solution.py:325
  13.8 2.4 %copy-start.2 = (f32[8,8,2048]{2,1,0:T(8,128)S(1)}, f32[8,8,2048]{2,1,0:T(8,128)}, u32[]{:S(2)}) copy-start(f32[8,8,2048]{2,1,0:T(8,128)} %flow_y.3) | copy-start | bytes 1572868
  13.8 4.9 %collective-permute-start.5 = (f32[8,2048]{1,0:T(8,128)S(1)}, f32[8,2048]{1,0:T(8,128)S(1)}, u32[]{:S(2)}, u32[]{:S(2)}) collective-permute-start(f32[8,2048]{1,0:T(8,128)S(1)} %get-tuple-element.38.own_z), channel_id=1, source_target_pairs={{0,15},{1,0},{2,1},{3,2},{4,3},{5,4},{6,5},{7,6},{8,7},{9,8},{10,9... | collective-permute-start | bytes 196616 | tf_op jit(solution)/shard_map/ppermute | solution.py:326
  16.2 1.0 %copy-start.3 = (f32[8,8,2048]{2,1,0:T(8,128)S(1)}, f32[8,8,2048]{2,1,0:T(8,128)}, u32[]{:S(2)}) copy-start(f32[8,8,2048]{2,1,0:T(8,128)} %flow_z.3) | copy-start | bytes 1572868
  16.9 1.6 %collective-permute-start.6 = (f32[3,8,2048]{2,1,0:T(8,128)S(1)}, f32[3,8,2048]{2,1,0:T(8,128)S(1)}, u32[]{:S(2)}, u32[]{:S(2)}) collective-permute-start(f32[3,8,2048]{2,1,0:T(8,128)S(1)} %get-tuple-element.41.core), channel_id=1, source_target_pairs={{0,1},{1,0},{2,3},{3,2},{4,5},{5,4},{6,7},{7,6},{8,9},{9,8},{10,11... | collective-permute-start | bytes 589832 | tf_op jit(solution)/shard_map/ppermute | solution.py:348

commit v6 on v5

--- a/solution.py
+++ b/solution.py
@@ -160,7 +160,7 @@
                 core[m, i : i + 1, at] = lax.select(odd_core, down, up)
         return _
 
-    lax.fori_loop(0, length // LANES, tile, None, unroll=2)
+    lax.fori_loop(0, length // LANES, tile, None, unroll=4)
 
 
 def z_inner(second, flow_z, fraction, out, inside, base, sems):

time: 22.7 us -> 22.7 us (level)
  no operation moved by 1% of the time
where the time goes in v6:
time: 22.7 us; the launch traced here: 22.5 us
  starting transfers between devices  13.6 us (60%)
  Pallas kernels  5.5 us (24%)
  waiting for transfers between devices  3.1 us (14%)
  local copies, waits for them, and re-layouts  0.27 us (1%)
    ppermute x1, starting transfers between devices, per_device(): upper_pairs = lax.ppermute(downward_pairs, 'row', down(n_row))  4.55 us
    ppermute x1, starting transfers between devices, per_device(): chip_side = lax.ppermute(chip, 'col', with_below(n_col))  3.56 us
    ppermute x1, waiting for transfers between devices, per_device(): chip_side = lax.ppermute(chip, 'col', with_below(n_col))  3.09 us
    ppermute x1, starting transfers between devices, per_device(): near_side = lax.ppermute(near, 'row', with_above(n_row))  2.36 us
    ppermute x1, starting transfers between devices, per_device(): courant_z = lax.ppermute(own_z, 'col', down(n_col))  1.89 us
    pallas_call x1, Pallas kernels, per_device(): pl.pallas_call(x_columns, out_shape=(edge, edge, edge, side, side, array(...  1.43 us
    pallas_call x1, Pallas kernels, per_device(): pl.pallas_call(z_inner, out_shape=(array(*block), array(9, rows, length))...  1.23 us
    ppermute x1, starting transfers between devices, per_device(): far_side = lax.ppermute(far, 'row', with_below(n_row))  1.11 us
  transfers between devices with their start and end apart: 7, of which 1 were waited for; matrix products, arithmetic and copies ran while one was open for 0% of the time, Pallas kernels for 15%

profile of v6, /device:TPU:2, one launch (start us, length us, event | category | flops | bytes accessed | tf_op | source)
XLA Modules:
  0.0 22.5 jit_solution(10963328583967737028)
XLA Ops:
  0.0 0.0 copy-start.1
  0.0 0.0 copy-start
  0.0 1.4 %x_columns.1 = (f32[2,8,2048]{2,1,0:T(8,128)S(1)}, f32[2,8,2048]{2,1,0:T(8,128)S(1)}, f32[2,8,2048]{2,1,0:T(8,128)S(1)}, f32[3,2,2048]{2,1,0:T(2,128)S(1)}, f32[...) custom-call(f32[8,8,2048]{2,1,0:T(8,128)} %fraction.9, f32[8,8,2048]{2,1,0:T(8,128)} %flow_x.5, ...), custom_call_target="tpu_custom_call" | custom-call | tf_op jit(solution)/shard_map/x_columns/pallas_call | solution.py:286
  1.4 2.4 %collective-permute-start = (f32[3,2,2048]{2,1,0:T(2,128)S(1)}, f32[3,2,2048]{2,1,0:T(2,128)S(1)}, u32[]{:S(2)}, u32[]{:S(2)}) collective-permute-start(f32[3,2,2048]{2,1,0:T(2,128)S(1)} %get-tuple-element.27.near), channel_id=1, source_target_pairs={{0,16},{16,0},{32,48},{48,32},{64,80},{80,64},{96,112},{112,96},{1... | collective-permute-start | bytes 147464 | tf_op jit(solution)/shard_map/ppermute | solution.py:297
  3.8 1.1 %collective-permute-start.1 = (f32[3,2,2048]{2,1,0:T(2,128)S(1)}, f32[3,2,2048]{2,1,0:T(2,128)S(1)}, u32[]{:S(2)}, u32[]{:S(2)}) collective-permute-start(f32[3,2,2048]{2,1,0:T(2,128)S(1)} %get-tuple-element.28.far), channel_id=1, source_target_pairs={{0,240},{16,32},{32,16},{48,64},{64,48},{80,96},{96,80},{112,128},... | collective-permute-start | bytes 147464 | tf_op jit(solution)/shard_map/ppermute | solution.py:298
  4.9 0.0 copy-done.1
  4.9 0.0 copy-done
  4.9 0.5 %x_rows.1 = (f32[2,8,2048]{2,1,0:T(8,128)S(1)}, f32[2,8,2048]{2,1,0:T(8,128)S(1)}, f32[6,2,2048]{2,1,0:T(2,128)S(1)}, f32[9,2,2048]{2,1,0:T(2,128)S(1)}) custom-call(f32[8,8,2048]{2,1,0:T(8,128)S(1)} %copy-done.1, f32[8,8,2048]{2,1,0:T(8,128)S(1)} %copy-done, f32[8,2048]{1,0:T(8,128)S(1)} %get-tuple-element.31.own_y), custom_call_target="tpu_custom_call" | custom-call | flops 10000000000 | bytes 10000000 | tf_op jit(solution)/shard_map/x_rows/pallas_call | solution.py:300
  5.4 4.5 %collective-permute-start.4 = (f32[9,2,2048]{2,1,0:T(2,128)S(1)}, f32[9,2,2048]{2,1,0:T(2,128)S(1)}, u32[]{:S(2)}, u32[]{:S(2)}) collective-permute-start(f32[9,2,2048]{2,1,0:T(2,128)S(1)} %get-tuple-element.35), channel_id=1, source_target_pairs={{0,240},{16,0},{32,16},{48,32},{64,48},{80,64},{96,80},{112,96},{1... | collective-permute-start | bytes 442376 | tf_op jit(solution)/shard_map/ppermute | solution.py:315
  10.0 0.0 collective-permute-start.3
  10.0 0.0 collective-permute-done.near_side
  10.0 0.0 collective-permute-done.1.far_side
  10.0 0.2 y_columns.1
  10.2 3.6 %collective-permute-start.2 = (f32[2,8,2048]{2,1,0:T(8,128)S(1)}, f32[2,8,2048]{2,1,0:T(8,128)S(1)}, u32[]{:S(2)}, u32[]{:S(2)}) collective-permute-start(f32[2,8,2048]{2,1,0:T(8,128)S(1)} %get-tuple-element.30.chip), channel_id=1, source_target_pairs={{0,15},{1,2},{2,1},{3,4},{4,3},{5,6},{6,5},{7,8},{8,7},{9,10},{10,... | collective-permute-start | bytes 393224 | tf_op jit(solution)/shard_map/ppermute | solution.py:325
  13.8 0.0 copy-start.2
  13.8 1.9 %collective-permute-start.5 = (f32[8,2048]{1,0:T(8,128)S(1)}, f32[8,2048]{1,0:T(8,128)S(1)}, u32[]{:S(2)}, u32[]{:S(2)}) collective-permute-start(f32[8,2048]{1,0:T(8,128)S(1)} %get-tuple-element.38.own_z), channel_id=1, source_target_pairs={{0,15},{1,0},{2,1},{3,2},{4,3},{5,4},{6,5},{7,6},{8,7},{9,8},{10,9... | collective-permute-start | bytes 196616 | tf_op jit(solution)/shard_map/ppermute | solution.py:326
  15.7 0.0 collective-permute-done.4.chip.upper_pairs
  15.7 0.5 %x_middle.1.middle = f32[4,8,2048]{2,1,0:T(8,128)S(1)} custom-call(f32[8,8,2048]{2,1,0:T(8,128)S(1)} %copy-done.1, f32[8,8,2048]{2,1,0:T(8,128)S(1)} %copy-done, f32[9,2,2048]{2,1,0:T(2,128)S(1)} %collective-permute-done.4.chip.upper_pairs), custom_call_target="tpu_custom_call" | custom-call | tf_op jit(solution)/shard_map/x_middle/pallas_call | solution.py:327
  16.2 0.0 collective-permute-done.3.lower_pairs
  16.2 0.0 copy-done.2
  16.2 0.0 copy-start.3
  16.2 0.7 %y_sweep.1 = (f32[8,8,2048]{2,1,0:T(8,128)S(1)}, f32[3,8,2048]{2,1,0:T(8,128)S(1)}) custom-call(f32[2,8,2048]{2,1,0:T(8,128)S(1)} %get-tuple-element.32.high, f32[6,2,2048]{2,1,0:T(2,128)S(1)} %collective-permute-done.3.lower_pairs, f32[2,8,2048]{2,1,0:T(8,128)S(1)} %get-tuple-element.34.low, f32[9,2,2048]{2,1,0:T(2,128)S(1)} %collective-permute-done.4.chip.upper_pairs, ...), custom_call_target="tpu_custom_call" | custom-call | flops 10000000000 | bytes 10000000 | tf_op jit(solution)/shard_map/y_sweep/pallas_call | solution.py:335
  16.9 0.1 collective-permute-start.6
  17.0 0.3 %copy-done.3 = f32[8,8,2048]{2,1,0:T(8,128)S(1)} copy-done((f32[8,8,2048]{2,1,0:T(8,128)S(1)}, f32[8,8,2048]{2,1,0:T(8,128)}, u32[]{:S(2)}) %copy-start.3) | copy-done | bytes 524312
  17.2 1.2 %z_inner.1 = (f32[8,8,2048]{2,1,0:T(8,128)}, f32[9,8,2048]{2,1,0:T(8,128)S(1)}) custom-call(f32[8,8,2048]{2,1,0:T(8,128)S(1)} %get-tuple-element.39.second, f32[8,8,2048]{2,1,0:T(8,128)S(1)} %copy-done.3, f32[8,8,2048]{2,1,0:T(8,128)S(1)} %copy-done.1), custom_call_target="tpu_custom_call" | custom-call | flops 10000000000 | bytes 10000000 | tf_op jit(solution)/shard_map/z_inner/pallas_call | solution.py:349
  18.5 0.0 collective-permute-done.6.core_side
  18.5 0.1 z_core.1.values
  18.6 0.0 collective-permute-done.5.courant_z
  18.6 3.1 %collective-permute-done.2.chip_side = f32[2,8,2048]{2,1,0:T(8,128)S(1)} collective-permute-done((f32[2,8,2048]{2,1,0:T(8,128)S(1)}, f32[2,8,2048]{2,1,0:T(8,128)S(1)}, u32[]{:S(2)}, u32[]{:S(2)}) %collective-permute-start.2) | collective-permute-done | bytes 131104 | tf_op jit(solution)/shard_map/ppermute | solution.py:325
  21.7 0.8 %z_chip.1 = f32[8,8,2048]{2,1,0:T(8,128)} custom-call(f32[2,8,2048]{2,1,0:T(8,128)S(1)} %get-tuple-element.30.chip, f32[2,8,2048]{2,1,0:T(8,128)S(1)} %collective-permute-done.2.chip_side, f32[9,8,2048]{2,1,0:T(8,128)S(1)} %get-tuple-element.40.inside, f32[8,2048]{1,0:T(8,128)S(1)} %get-tuple-element.38.own_z, ...), custom_call_target="tpu_custom_call", output_to_operand_aliasing={{}: (6, {})} | custom-call | tf_op jit(solution)/shard_map/z_chip/pallas_call | solution.py:367
Async XLA Ops:
  0.0 4.9 %copy-start.1 = (f32[8,8,2048]{2,1,0:T(8,128)S(1)}, f32[8,8,2048]{2,1,0:T(8,128)}, u32[]{:S(2)}) copy-start(f32[8,8,2048]{2,1,0:T(8,128)} %fraction.9) | copy-start | bytes 1572868
  0.0 4.9 %copy-start = (f32[8,8,2048]{2,1,0:T(8,128)S(1)}, f32[8,8,2048]{2,1,0:T(8,128)}, u32[]{:S(2)}) copy-start(f32[8,8,2048]{2,1,0:T(8,128)} %flow_x.5) | copy-start | bytes 1572868
  1.4 8.6 %collective-permute-start = (f32[3,2,2048]{2,1,0:T(2,128)S(1)}, f32[3,2,2048]{2,1,0:T(2,128)S(1)}, u32[]{:S(2)}, u32[]{:S(2)}) collective-permute-start(f32[3,2,2048]{2,1,0:T(2,128)S(1)} %get-tuple-element.27.near), channel_id=1, source_target_pairs={{0,16},{16,0},{32,48},{48,32},{64,80},{80,64},{96,112},{112,96},{1... | collective-permute-start | bytes 147464 | tf_op jit(solution)/shard_map/ppermute | solution.py:297
  3.8 6.2 %collective-permute-start.1 = (f32[3,2,2048]{2,1,0:T(2,128)S(1)}, f32[3,2,2048]{2,1,0:T(2,128)S(1)}, u32[]{:S(2)}, u32[]{:S(2)}) collective-permute-start(f32[3,2,2048]{2,1,0:T(2,128)S(1)} %get-tuple-element.28.far), channel_id=1, source_target_pairs={{0,240},{16,32},{32,16},{48,64},{64,48},{80,96},{96,80},{112,128},... | collective-permute-start | bytes 147464 | tf_op jit(solution)/shard_map/ppermute | solution.py:298
  5.4 10.2 %collective-permute-start.4 = (f32[9,2,2048]{2,1,0:T(2,128)S(1)}, f32[9,2,2048]{2,1,0:T(2,128)S(1)}, u32[]{:S(2)}, u32[]{:S(2)}) collective-permute-start(f32[9,2,2048]{2,1,0:T(2,128)S(1)} %get-tuple-element.35), channel_id=1, source_target_pairs={{0,240},{16,0},{32,16},{48,32},{64,48},{80,64},{96,80},{112,96},{1... | collective-permute-start | bytes 442376 | tf_op jit(solution)/shard_map/ppermute | solution.py:315
  10.0 6.2 %collective-permute-start.3 = (f32[6,2,2048]{2,1,0:T(2,128)S(1)}, f32[6,2,2048]{2,1,0:T(2,128)S(1)}, u32[]{:S(2)}, u32[]{:S(2)}) collective-permute-start(f32[6,2,2048]{2,1,0:T(2,128)S(1)} %get-tuple-element.33), channel_id=1, source_target_pairs={{0,16},{16,32},{32,48},{48,64},{64,80},{80,96},{96,112},{112,128},... | collective-permute-start | bytes 294920 | tf_op jit(solution)/shard_map/ppermute | solution.py:314
  10.2 11.5 %collective-permute-start.2 = (f32[2,8,2048]{2,1,0:T(8,128)S(1)}, f32[2,8,2048]{2,1,0:T(8,128)S(1)}, u32[]{:S(2)}, u32[]{:S(2)}) collective-permute-start(f32[2,8,2048]{2,1,0:T(8,128)S(1)} %get-tuple-element.30.chip), channel_id=1, source_target_pairs={{0,15},{1,2},{2,1},{3,4},{4,3},{5,6},{6,5},{7,8},{8,7},{9,10},{10,... | collective-permute-start | bytes 393224 | tf_op jit(solution)/shard_map/ppermute | solution.py:325
  13.8 2.4 %copy-start.2 = (f32[8,8,2048]{2,1,0:T(8,128)S(1)}, f32[8,8,2048]{2,1,0:T(8,128)}, u32[]{:S(2)}) copy-start(f32[8,8,2048]{2,1,0:T(8,128)} %flow_y.3) | copy-start | bytes 1572868
  13.8 4.9 %collective-permute-start.5 = (f32[8,2048]{1,0:T(8,128)S(1)}, f32[8,2048]{1,0:T(8,128)S(1)}, u32[]{:S(2)}, u32[]{:S(2)}) collective-permute-start(f32[8,2048]{1,0:T(8,128)S(1)} %get-tuple-element.38.own_z), channel_id=1, source_target_pairs={{0,15},{1,0},{2,1},{3,2},{4,3},{5,4},{6,5},{7,6},{8,7},{9,8},{10,9... | collective-permute-start | bytes 196616 | tf_op jit(solution)/shard_map/ppermute | solution.py:326
  16.2 1.0 %copy-start.3 = (f32[8,8,2048]{2,1,0:T(8,128)S(1)}, f32[8,8,2048]{2,1,0:T(8,128)}, u32[]{:S(2)}) copy-start(f32[8,8,2048]{2,1,0:T(8,128)} %flow_z.3) | copy-start | bytes 1572868
  16.9 1.6 %collective-permute-start.6 = (f32[3,8,2048]{2,1,0:T(8,128)S(1)}, f32[3,8,2048]{2,1,0:T(8,128)S(1)}, u32[]{:S(2)}, u32[]{:S(2)}) collective-permute-start(f32[3,8,2048]{2,1,0:T(8,128)S(1)} %get-tuple-element.41.core), channel_id=1, source_target_pairs={{0,1},{1,0},{2,3},{3,2},{4,5},{5,4},{6,7},{7,6},{8,9},{9,8},{10,11... | collective-permute-start | bytes 589832 | tf_op jit(solution)/shard_map/ppermute | solution.py:348

commit v7 on v5

--- a/solution.py
+++ b/solution.py
@@ -70,22 +70,32 @@
         far[2, m : m + 1] = courant[m, :1]
 
 
-def x_rows(fraction, flow_x, own_y, high, low, upward, downward):
-    rows, columns, _ = fraction.shape
+def other_pairs(row):
     odd_core = lax.rem(lax.axis_index("col"), 2) == 1
-    pairs = columns // 2 - 1
-
-    def put(message, i, row):
-        for p in range(pairs):
-            message[i * pairs + p] = lax.select(
-                odd_core, row[2 * p : 2 * p + 2], row[2 * p + 2 : 2 * p + 4]
-            )
-
-    put(downward, 2, own_y[...])
-    for mine, message, start in ((low, downward, 0), (high, upward, rows - 2)):
-        for i in range(2):
-            mine[i] = x_sweep_row(fraction[start + i], flow_x[start + i])
-            put(message, i, mine[i])
+    return [
+        lax.select(odd_core, row[2 * p : 2 * p + 2], row[2 * p + 2 : 2 * p + 4])
+        for p in range(row.shape[0] // 2 - 1)
+    ]
+
+
+def x_two_rows(fraction, flow_x, row, mine, message):
+    pairs = fraction.shape[1] // 2 - 1
+    for i in range(2):
+        mine[i] = x_sweep_row(fraction[row + i], flow_x[row + i])
+        for p, values in enumerate(other_pairs(mine[i])):
+            message[i * pairs + p] = values
+
+
+def x_high(fraction, flow_x, near_side, high, upward):
+    del near_side
+    x_two_rows(fraction, flow_x, fraction.shape[0] - 2, high, upward)
+
+
+def x_low(fraction, flow_x, own_y, low, downward):
+    pairs = fraction.shape[1] // 2 - 1
+    for p, values in enumerate(other_pairs(own_y[...])):
+        downward[2 * pairs + p] = values
+    x_two_rows(fraction, flow_x, 0, low, downward)
 
 
 def x_middle(fraction, flow_x, chip, middle):
@@ -297,22 +307,26 @@
     near_side = lax.ppermute(near, "row", with_above(n_row))
     far_side = lax.ppermute(far, "row", with_below(n_row))
     pairs = columns // 2 - 1
-    high, low, upward_pairs, downward_pairs = pl.pallas_call(
-        x_rows,
-        out_shape=(
-            array(2, columns, length),
-            array(2, columns, length),
-            array(2 * pairs, 2, length),
-            array(3 * pairs, 2, length),
-        ),
+    low, downward_pairs = pl.pallas_call(
+        x_low,
+        out_shape=(array(2, columns, length), array(3 * pairs, 2, length)),
         in_specs=[vmem] * 3,
-        out_specs=[vmem] * 4,
+        out_specs=[vmem] * 2,
         compiler_params=params,
         cost_estimate=busy,
-        name="x_rows",
+        name="x_low",
     )(fraction, flow_x, own_y)
+    upper_pairs = lax.ppermute(downward_pairs, "row", down(n_row))
+    high, upward_pairs = pl.pallas_call(
+        x_high,
+        out_shape=(array(2, columns, length), array(2 * pairs, 2, length)),
+        in_specs=[vmem] * 3,
+        out_specs=[vmem] * 2,
+        compiler_params=params,
+        cost_estimate=busy,
+        name="x_high",
+    )(fraction, flow_x, near_side)
     lower_pairs = lax.ppermute(upward_pairs, "row", up(n_row))
-    upper_pairs = lax.ppermute(downward_pairs, "row", down(n_row))
     chip, own_z, column_lower, column_upper = pl.pallas_call(
         y_columns,
         out_shape=(edge, array(rows, length), side, side),

time: 22.7 us -> 22.8 us (level)
    pallas_call x1 -> x2, Pallas kernels: 0.53 us -> 0.54 us  [the longest x1 0.27 us: per_device(): pl.pallas_call(x_low, out_shape=(array(2, columns, length), array(3 * pai...]
where the time goes in v7:
time: 22.8 us; the launch traced here: 22.7 us
  starting transfers between devices  13.6 us (60%)
  Pallas kernels  5.54 us (24%)
  waiting for transfers between devices  3.14 us (14%)
  local copies, waits for them, and re-layouts  0.24 us (1%)
    ppermute x1, starting transfers between devices, per_device(): upper_pairs = lax.ppermute(downward_pairs, 'row', down(n_row))  4.55 us
    ppermute x1, starting transfers between devices, per_device(): chip_side = lax.ppermute(chip, 'col', with_below(n_col))  3.56 us
    ppermute x1, waiting for transfers between devices, per_device(): chip_side = lax.ppermute(chip, 'col', with_below(n_col))  3.13 us
    ppermute x1, starting transfers between devices, per_device(): near_side = lax.ppermute(near, 'row', with_above(n_row))  2.36 us
    ppermute x1, starting transfers between devices, per_device(): courant_z = lax.ppermute(own_z, 'col', down(n_col))  1.89 us
    pallas_call x1, Pallas kernels, per_device(): pl.pallas_call(x_columns, out_shape=(edge, edge, edge, side, side, array(...  1.43 us
    pallas_call x1, Pallas kernels, per_device(): pl.pallas_call(z_inner, out_shape=(array(*block), array(9, rows, length))...  1.23 us
    ppermute x1, starting transfers between devices, per_device(): far_side = lax.ppermute(far, 'row', with_below(n_row))  1.11 us
  transfers between devices with their start and end apart: 7, of which 1 were waited for; matrix products, arithmetic and copies ran while one was open for 0% of the time, Pallas kernels for 15%

profile of v7, /device:TPU:2, one launch (start us, length us, event | category | flops | bytes accessed | tf_op | source)
XLA Modules:
  0.0 22.7 jit_solution(7032118871156687311)
XLA Ops:
  0.0 0.0 copy-start.1
  0.0 0.0 copy-start
  0.0 1.4 %x_columns.1 = (f32[2,8,2048]{2,1,0:T(8,128)S(1)}, f32[2,8,2048]{2,1,0:T(8,128)S(1)}, f32[2,8,2048]{2,1,0:T(8,128)S(1)}, f32[3,2,2048]{2,1,0:T(2,128)S(1)}, f32[...) custom-call(f32[8,8,2048]{2,1,0:T(8,128)} %fraction.11, f32[8,8,2048]{2,1,0:T(8,128)} %flow_x.7, ...), custom_call_target="tpu_custom_call" | custom-call | tf_op jit(solution)/shard_map/x_columns/pallas_call | solution.py:296
  1.4 2.4 %collective-permute-start = (f32[3,2,2048]{2,1,0:T(2,128)S(1)}, f32[3,2,2048]{2,1,0:T(2,128)S(1)}, u32[]{:S(2)}, u32[]{:S(2)}) collective-permute-start(f32[3,2,2048]{2,1,0:T(2,128)S(1)} %get-tuple-element.27.near), channel_id=1, source_target_pairs={{0,16},{16,0},{32,48},{48,32},{64,80},{80,64},{96,112},{112,96},{1... | collective-permute-start | bytes 147464 | tf_op jit(solution)/shard_map/ppermute | solution.py:307
  3.8 1.1 %collective-permute-start.1 = (f32[3,2,2048]{2,1,0:T(2,128)S(1)}, f32[3,2,2048]{2,1,0:T(2,128)S(1)}, u32[]{:S(2)}, u32[]{:S(2)}) collective-permute-start(f32[3,2,2048]{2,1,0:T(2,128)S(1)} %get-tuple-element.28.far), channel_id=1, source_target_pairs={{0,240},{16,32},{32,16},{48,64},{64,48},{80,96},{96,80},{112,128},... | collective-permute-start | bytes 147464 | tf_op jit(solution)/shard_map/ppermute | solution.py:308
  4.9 0.0 copy-done.1
  4.9 0.0 copy-done
  4.9 0.3 %x_low.1 = (f32[2,8,2048]{2,1,0:T(8,128)S(1)}, f32[9,2,2048]{2,1,0:T(2,128)S(1)}) custom-call(f32[8,8,2048]{2,1,0:T(8,128)S(1)} %copy-done.1, f32[8,8,2048]{2,1,0:T(8,128)S(1)} %copy-done, f32[8,2048]{1,0:T(8,128)S(1)} %get-tuple-element.33.own_y), custom_call_target="tpu_custom_call" | custom-call | flops 10000000000 | bytes 10000000 | tf_op jit(solution)/shard_map/x_low/pallas_call | solution.py:310
  5.2 4.5 %collective-permute-start.4 = (f32[9,2,2048]{2,1,0:T(2,128)S(1)}, f32[9,2,2048]{2,1,0:T(2,128)S(1)}, u32[]{:S(2)}, u32[]{:S(2)}) collective-permute-start(f32[9,2,2048]{2,1,0:T(2,128)S(1)} %get-tuple-element.35), channel_id=1, source_target_pairs={{0,240},{16,0},{32,16},{48,32},{64,48},{80,64},{96,80},{112,96},{1... | collective-permute-start | bytes 442376 | tf_op jit(solution)/shard_map/ppermute | solution.py:319
  9.7 0.0 collective-permute-done.near_side
  9.7 0.3 %x_high.1 = (f32[2,8,2048]{2,1,0:T(8,128)S(1)}, f32[6,2,2048]{2,1,0:T(2,128)S(1)}) custom-call(f32[8,8,2048]{2,1,0:T(8,128)S(1)} %copy-done.1, f32[8,8,2048]{2,1,0:T(8,128)S(1)} %copy-done, f32[3,2,2048]{2,1,0:T(2,128)S(1)} %collective-permute-done.near_side), custom_call_target="tpu_custom_call" | custom-call | flops 10000000000 | bytes 10000000 | tf_op jit(solution)/shard_map/x_high/pallas_call | solution.py:320
  10.0 0.1 collective-permute-start.3
  10.1 0.0 collective-permute-done.1.far_side
  10.1 0.2 y_columns.1
  10.3 3.6 %collective-permute-start.2 = (f32[2,8,2048]{2,1,0:T(8,128)S(1)}, f32[2,8,2048]{2,1,0:T(8,128)S(1)}, u32[]{:S(2)}, u32[]{:S(2)}) collective-permute-start(f32[2,8,2048]{2,1,0:T(8,128)S(1)} %get-tuple-element.30.chip), channel_id=1, source_target_pairs={{0,15},{1,2},{2,1},{3,4},{4,3},{5,6},{6,5},{7,8},{8,7},{9,10},{10,... | collective-permute-start | bytes 393224 | tf_op jit(solution)/shard_map/ppermute | solution.py:339
  13.9 0.0 copy-start.2
  13.9 1.9 %collective-permute-start.5 = (f32[8,2048]{1,0:T(8,128)S(1)}, f32[8,2048]{1,0:T(8,128)S(1)}, u32[]{:S(2)}, u32[]{:S(2)}) collective-permute-start(f32[8,2048]{1,0:T(8,128)S(1)} %get-tuple-element.38.own_z), channel_id=1, source_target_pairs={{0,15},{1,0},{2,1},{3,2},{4,3},{5,4},{6,5},{7,6},{8,7},{9,8},{10,9... | collective-permute-start | bytes 196616 | tf_op jit(solution)/shard_map/ppermute | solution.py:340
  15.8 0.0 collective-permute-done.4.chip.upper_pairs
  15.8 0.5 %x_middle.1.middle = f32[4,8,2048]{2,1,0:T(8,128)S(1)} custom-call(f32[8,8,2048]{2,1,0:T(8,128)S(1)} %copy-done.1, f32[8,8,2048]{2,1,0:T(8,128)S(1)} %copy-done, f32[9,2,2048]{2,1,0:T(2,128)S(1)} %collective-permute-done.4.chip.upper_pairs), custom_call_target="tpu_custom_call" | custom-call | tf_op jit(solution)/shard_map/x_middle/pallas_call | solution.py:341
  16.3 0.0 collective-permute-done.3.lower_pairs
  16.3 0.0 copy-done.2
  16.3 0.0 copy-start.3
  16.3 0.7 %y_sweep.1 = (f32[8,8,2048]{2,1,0:T(8,128)S(1)}, f32[3,8,2048]{2,1,0:T(8,128)S(1)}) custom-call(f32[2,8,2048]{2,1,0:T(8,128)S(1)} %get-tuple-element.31.high, f32[6,2,2048]{2,1,0:T(2,128)S(1)} %collective-permute-done.3.lower_pairs, f32[2,8,2048]{2,1,0:T(8,128)S(1)} %get-tuple-element.34.low, f32[9,2,2048]{2,1,0:T(2,128)S(1)} %collective-permute-done.4.chip.upper_pairs, ...), custom_call_target="tpu_custom_call" | custom-call | flops 10000000000 | bytes 10000000 | tf_op jit(solution)/shard_map/y_sweep/pallas_call | solution.py:349
  17.0 0.1 collective-permute-start.6
  17.1 0.2 copy-done.3
  17.4 1.2 %z_inner.1 = (f32[8,8,2048]{2,1,0:T(8,128)}, f32[9,8,2048]{2,1,0:T(8,128)S(1)}) custom-call(f32[8,8,2048]{2,1,0:T(8,128)S(1)} %get-tuple-element.39.second, f32[8,8,2048]{2,1,0:T(8,128)S(1)} %copy-done.3, f32[8,8,2048]{2,1,0:T(8,128)S(1)} %copy-done.1), custom_call_target="tpu_custom_call" | custom-call | flops 10000000000 | bytes 10000000 | tf_op jit(solution)/shard_map/z_inner/pallas_call | solution.py:363
  18.6 0.0 collective-permute-done.6.core_side
  18.6 0.1 z_core.1.values
  18.7 0.0 collective-permute-done.5.courant_z
  18.8 3.1 %collective-permute-done.2.chip_side = f32[2,8,2048]{2,1,0:T(8,128)S(1)} collective-permute-done((f32[2,8,2048]{2,1,0:T(8,128)S(1)}, f32[2,8,2048]{2,1,0:T(8,128)S(1)}, u32[]{:S(2)}, u32[]{:S(2)}) %collective-permute-start.2) | collective-permute-done | bytes 131104 | tf_op jit(solution)/shard_map/ppermute | solution.py:339
  21.9 0.8 %z_chip.1 = f32[8,8,2048]{2,1,0:T(8,128)} custom-call(f32[2,8,2048]{2,1,0:T(8,128)S(1)} %get-tuple-element.30.chip, f32[2,8,2048]{2,1,0:T(8,128)S(1)} %collective-permute-done.2.chip_side, f32[9,8,2048]{2,1,0:T(8,128)S(1)} %get-tuple-element.40.inside, f32[8,2048]{1,0:T(8,128)S(1)} %get-tuple-element.38.own_z, ...), custom_call_target="tpu_custom_call", output_to_operand_aliasing={{}: (6, {})} | custom-call | tf_op jit(solution)/shard_map/z_chip/pallas_call | solution.py:381
Async XLA Ops:
  0.0 4.9 %copy-start.1 = (f32[8,8,2048]{2,1,0:T(8,128)S(1)}, f32[8,8,2048]{2,1,0:T(8,128)}, u32[]{:S(2)}) copy-start(f32[8,8,2048]{2,1,0:T(8,128)} %fraction.11) | copy-start | bytes 1572868
  0.0 4.9 %copy-start = (f32[8,8,2048]{2,1,0:T(8,128)S(1)}, f32[8,8,2048]{2,1,0:T(8,128)}, u32[]{:S(2)}) copy-start(f32[8,8,2048]{2,1,0:T(8,128)} %flow_x.7) | copy-start | bytes 1572868
  1.4 8.3 %collective-permute-start = (f32[3,2,2048]{2,1,0:T(2,128)S(1)}, f32[3,2,2048]{2,1,0:T(2,128)S(1)}, u32[]{:S(2)}, u32[]{:S(2)}) collective-permute-start(f32[3,2,2048]{2,1,0:T(2,128)S(1)} %get-tuple-element.27.near), channel_id=1, source_target_pairs={{0,16},{16,0},{32,48},{48,32},{64,80},{80,64},{96,112},{112,96},{1... | collective-permute-start | bytes 147464 | tf_op jit(solution)/shard_map/ppermute | solution.py:307
  3.8 6.3 %collective-permute-start.1 = (f32[3,2,2048]{2,1,0:T(2,128)S(1)}, f32[3,2,2048]{2,1,0:T(2,128)S(1)}, u32[]{:S(2)}, u32[]{:S(2)}) collective-permute-start(f32[3,2,2048]{2,1,0:T(2,128)S(1)} %get-tuple-element.28.far), channel_id=1, source_target_pairs={{0,240},{16,32},{32,16},{48,64},{64,48},{80,96},{96,80},{112,128},... | collective-permute-start | bytes 147464 | tf_op jit(solution)/shard_map/ppermute | solution.py:308
  5.2 10.6 %collective-permute-start.4 = (f32[9,2,2048]{2,1,0:T(2,128)S(1)}, f32[9,2,2048]{2,1,0:T(2,128)S(1)}, u32[]{:S(2)}, u32[]{:S(2)}) collective-permute-start(f32[9,2,2048]{2,1,0:T(2,128)S(1)} %get-tuple-element.35), channel_id=1, source_target_pairs={{0,240},{16,0},{32,16},{48,32},{64,48},{80,64},{96,80},{112,96},{1... | collective-permute-start | bytes 442376 | tf_op jit(solution)/shard_map/ppermute | solution.py:319
  10.0 6.3 %collective-permute-start.3 = (f32[6,2,2048]{2,1,0:T(2,128)S(1)}, f32[6,2,2048]{2,1,0:T(2,128)S(1)}, u32[]{:S(2)}, u32[]{:S(2)}) collective-permute-start(f32[6,2,2048]{2,1,0:T(2,128)S(1)} %get-tuple-element.32), channel_id=1, source_target_pairs={{0,16},{16,32},{32,48},{48,64},{64,80},{80,96},{96,112},{112,128},... | collective-permute-start | bytes 294920 | tf_op jit(solution)/shard_map/ppermute | solution.py:329
  10.3 11.6 %collective-permute-start.2 = (f32[2,8,2048]{2,1,0:T(8,128)S(1)}, f32[2,8,2048]{2,1,0:T(8,128)S(1)}, u32[]{:S(2)}, u32[]{:S(2)}) collective-permute-start(f32[2,8,2048]{2,1,0:T(8,128)S(1)} %get-tuple-element.30.chip), channel_id=1, source_target_pairs={{0,15},{1,2},{2,1},{3,4},{4,3},{5,6},{6,5},{7,8},{8,7},{9,10},{10,... | collective-permute-start | bytes 393224 | tf_op jit(solution)/shard_map/ppermute | solution.py:339
  13.9 2.4 %copy-start.2 = (f32[8,8,2048]{2,1,0:T(8,128)S(1)}, f32[8,8,2048]{2,1,0:T(8,128)}, u32[]{:S(2)}) copy-start(f32[8,8,2048]{2,1,0:T(8,128)} %flow_y.3) | copy-start | bytes 1572868
  13.9 4.9 %collective-permute-start.5 = (f32[8,2048]{1,0:T(8,128)S(1)}, f32[8,2048]{1,0:T(8,128)S(1)}, u32[]{:S(2)}, u32[]{:S(2)}) collective-permute-start(f32[8,2048]{1,0:T(8,128)S(1)} %get-tuple-element.38.own_z), channel_id=1, source_target_pairs={{0,15},{1,0},{2,1},{3,2},{4,3},{5,4},{6,5},{7,6},{8,7},{9,8},{10,9... | collective-permute-start | bytes 196616 | tf_op jit(solution)/shard_map/ppermute | solution.py:340
  16.3 1.0 %copy-start.3 = (f32[8,8,2048]{2,1,0:T(8,128)S(1)}, f32[8,8,2048]{2,1,0:T(8,128)}, u32[]{:S(2)}) copy-start(f32[8,8,2048]{2,1,0:T(8,128)} %flow_z.3) | copy-start | bytes 1572868
  17.0 1.6 %collective-permute-start.6 = (f32[3,8,2048]{2,1,0:T(8,128)S(1)}, f32[3,8,2048]{2,1,0:T(8,128)S(1)}, u32[]{:S(2)}, u32[]{:S(2)}) collective-permute-start(f32[3,8,2048]{2,1,0:T(8,128)S(1)} %get-tuple-element.41.core), channel_id=1, source_target_pairs={{0,1},{1,0},{2,3},{3,2},{4,5},{5,4},{6,7},{7,6},{8,9},{9,8},{10,11... | collective-permute-start | bytes 589832 | tf_op jit(solution)/shard_map/ppermute | solution.py:362

commit v8 on v7

--- a/solution.py
+++ b/solution.py
@@ -170,7 +170,7 @@
                 core[m, i : i + 1, at] = lax.select(odd_core, down, up)
         return _
 
-    lax.fori_loop(0, length // LANES, tile, None, unroll=2)
+    lax.fori_loop(0, length // LANES, tile, None, unroll=4)
 
 
 def z_inner(second, flow_z, fraction, out, inside, base, sems):

time: 22.8 us -> 22.8 us (level)
  transfers between devices with their start and end apart: 7 -> 7, of which waited for: 1 -> 1; matrix products, arithmetic and copies ran while one was open for 0% -> 0% of each run, Pallas kernels for 15% -> 14%
where the time goes in v8:
time: 22.8 us; the launch traced here: 22.7 us
  starting transfers between devices  13.6 us (60%)
  Pallas kernels  5.51 us (24%)
  waiting for transfers between devices  3.14 us (14%)
  local copies, waits for them, and re-layouts  0.27 us (1%)
    ppermute x1, starting transfers between devices, per_device(): upper_pairs = lax.ppermute(downward_pairs, 'row', down(n_row))  4.55 us
    ppermute x1, starting transfers between devices, per_device(): chip_side = lax.ppermute(chip, 'col', with_below(n_col))  3.56 us
    ppermute x1, waiting for transfers between devices, per_device(): chip_side = lax.ppermute(chip, 'col', with_below(n_col))  3.13 us
    ppermute x1, starting transfers between devices, per_device(): near_side = lax.ppermute(near, 'row', with_above(n_row))  2.36 us
    ppermute x1, starting transfers between devices, per_device(): courant_z = lax.ppermute(own_z, 'col', down(n_col))  1.89 us
    pallas_call x1, Pallas kernels, per_device(): pl.pallas_call(x_columns, out_shape=(edge, edge, edge, side, side, array(...  1.43 us
    pallas_call x1, Pallas kernels, per_device(): pl.pallas_call(z_inner, out_shape=(array(*block), array(9, rows, length))...  1.23 us
    ppermute x1, starting transfers between devices, per_device(): far_side = lax.ppermute(far, 'row', with_below(n_row))  1.11 us
  transfers between devices with their start and end apart: 7, of which 1 were waited for; matrix products, arithmetic and copies ran while one was open for 0% of the time, Pallas kernels for 14%

profile of v8, /device:TPU:2, one launch (start us, length us, event | category | flops | bytes accessed | tf_op | source)
XLA Modules:
  0.0 22.7 jit_solution(214997420860245650)
XLA Ops:
  0.0 0.0 copy-start.1
  0.0 0.0 copy-start
  0.0 1.4 %x_columns.1 = (f32[2,8,2048]{2,1,0:T(8,128)S(1)}, f32[2,8,2048]{2,1,0:T(8,128)S(1)}, f32[2,8,2048]{2,1,0:T(8,128)S(1)}, f32[3,2,2048]{2,1,0:T(2,128)S(1)}, f32[...) custom-call(f32[8,8,2048]{2,1,0:T(8,128)} %fraction.11, f32[8,8,2048]{2,1,0:T(8,128)} %flow_x.7, ...), custom_call_target="tpu_custom_call" | custom-call | tf_op jit(solution)/shard_map/x_columns/pallas_call | solution.py:296
  1.4 2.4 %collective-permute-start = (f32[3,2,2048]{2,1,0:T(2,128)S(1)}, f32[3,2,2048]{2,1,0:T(2,128)S(1)}, u32[]{:S(2)}, u32[]{:S(2)}) collective-permute-start(f32[3,2,2048]{2,1,0:T(2,128)S(1)} %get-tuple-element.27.near), channel_id=1, source_target_pairs={{0,16},{16,0},{32,48},{48,32},{64,80},{80,64},{96,112},{112,96},{1... | collective-permute-start | bytes 147464 | tf_op jit(solution)/shard_map/ppermute | solution.py:307
  3.8 1.1 %collective-permute-start.1 = (f32[3,2,2048]{2,1,0:T(2,128)S(1)}, f32[3,2,2048]{2,1,0:T(2,128)S(1)}, u32[]{:S(2)}, u32[]{:S(2)}) collective-permute-start(f32[3,2,2048]{2,1,0:T(2,128)S(1)} %get-tuple-element.28.far), channel_id=1, source_target_pairs={{0,240},{16,32},{32,16},{48,64},{64,48},{80,96},{96,80},{112,128},... | collective-permute-start | bytes 147464 | tf_op jit(solution)/shard_map/ppermute | solution.py:308
  4.9 0.0 copy-done.1
  4.9 0.0 copy-done
  4.9 0.3 %x_low.1 = (f32[2,8,2048]{2,1,0:T(8,128)S(1)}, f32[9,2,2048]{2,1,0:T(2,128)S(1)}) custom-call(f32[8,8,2048]{2,1,0:T(8,128)S(1)} %copy-done.1, f32[8,8,2048]{2,1,0:T(8,128)S(1)} %copy-done, f32[8,2048]{1,0:T(8,128)S(1)} %get-tuple-element.33.own_y), custom_call_target="tpu_custom_call" | custom-call | flops 10000000000 | bytes 10000000 | tf_op jit(solution)/shard_map/x_low/pallas_call | solution.py:310
  5.2 4.5 %collective-permute-start.4 = (f32[9,2,2048]{2,1,0:T(2,128)S(1)}, f32[9,2,2048]{2,1,0:T(2,128)S(1)}, u32[]{:S(2)}, u32[]{:S(2)}) collective-permute-start(f32[9,2,2048]{2,1,0:T(2,128)S(1)} %get-tuple-element.35), channel_id=1, source_target_pairs={{0,240},{16,0},{32,16},{48,32},{64,48},{80,64},{96,80},{112,96},{1... | collective-permute-start | bytes 442376 | tf_op jit(solution)/shard_map/ppermute | solution.py:319
  9.7 0.0 collective-permute-done.near_side
  9.7 0.3 %x_high.1 = (f32[2,8,2048]{2,1,0:T(8,128)S(1)}, f32[6,2,2048]{2,1,0:T(2,128)S(1)}) custom-call(f32[8,8,2048]{2,1,0:T(8,128)S(1)} %copy-done.1, f32[8,8,2048]{2,1,0:T(8,128)S(1)} %copy-done, f32[3,2,2048]{2,1,0:T(2,128)S(1)} %collective-permute-done.near_side), custom_call_target="tpu_custom_call" | custom-call | flops 10000000000 | bytes 10000000 | tf_op jit(solution)/shard_map/x_high/pallas_call | solution.py:320
  10.0 0.1 collective-permute-start.3
  10.1 0.0 collective-permute-done.1.far_side
  10.1 0.2 y_columns.1
  10.3 3.6 %collective-permute-start.2 = (f32[2,8,2048]{2,1,0:T(8,128)S(1)}, f32[2,8,2048]{2,1,0:T(8,128)S(1)}, u32[]{:S(2)}, u32[]{:S(2)}) collective-permute-start(f32[2,8,2048]{2,1,0:T(8,128)S(1)} %get-tuple-element.30.chip), channel_id=1, source_target_pairs={{0,15},{1,2},{2,1},{3,4},{4,3},{5,6},{6,5},{7,8},{8,7},{9,10},{10,... | collective-permute-start | bytes 393224 | tf_op jit(solution)/shard_map/ppermute | solution.py:339
  13.9 0.0 copy-start.2
  13.9 1.9 %collective-permute-start.5 = (f32[8,2048]{1,0:T(8,128)S(1)}, f32[8,2048]{1,0:T(8,128)S(1)}, u32[]{:S(2)}, u32[]{:S(2)}) collective-permute-start(f32[8,2048]{1,0:T(8,128)S(1)} %get-tuple-element.38.own_z), channel_id=1, source_target_pairs={{0,15},{1,0},{2,1},{3,2},{4,3},{5,4},{6,5},{7,6},{8,7},{9,8},{10,9... | collective-permute-start | bytes 196616 | tf_op jit(solution)/shard_map/ppermute | solution.py:340
  15.8 0.0 collective-permute-done.4.chip.upper_pairs
  15.8 0.5 %x_middle.1.middle = f32[4,8,2048]{2,1,0:T(8,128)S(1)} custom-call(f32[8,8,2048]{2,1,0:T(8,128)S(1)} %copy-done.1, f32[8,8,2048]{2,1,0:T(8,128)S(1)} %copy-done, f32[9,2,2048]{2,1,0:T(2,128)S(1)} %collective-permute-done.4.chip.upper_pairs), custom_call_target="tpu_custom_call" | custom-call | tf_op jit(solution)/shard_map/x_middle/pallas_call | solution.py:341
  16.3 0.0 collective-permute-done.3.lower_pairs
  16.3 0.0 copy-done.2
  16.3 0.0 copy-start.3
  16.3 0.7 %y_sweep.1 = (f32[8,8,2048]{2,1,0:T(8,128)S(1)}, f32[3,8,2048]{2,1,0:T(8,128)S(1)}) custom-call(f32[2,8,2048]{2,1,0:T(8,128)S(1)} %get-tuple-element.31.high, f32[6,2,2048]{2,1,0:T(2,128)S(1)} %collective-permute-done.3.lower_pairs, f32[2,8,2048]{2,1,0:T(8,128)S(1)} %get-tuple-element.34.low, f32[9,2,2048]{2,1,0:T(2,128)S(1)} %collective-permute-done.4.chip.upper_pairs, ...), custom_call_target="tpu_custom_call" | custom-call | flops 10000000000 | bytes 10000000 | tf_op jit(solution)/shard_map/y_sweep/pallas_call | solution.py:349
  17.0 0.1 collective-permute-start.6
  17.1 0.3 %copy-done.3 = f32[8,8,2048]{2,1,0:T(8,128)S(1)} copy-done((f32[8,8,2048]{2,1,0:T(8,128)S(1)}, f32[8,8,2048]{2,1,0:T(8,128)}, u32[]{:S(2)}) %copy-start.3) | copy-done | bytes 524312
  17.4 1.2 %z_inner.1 = (f32[8,8,2048]{2,1,0:T(8,128)}, f32[9,8,2048]{2,1,0:T(8,128)S(1)}) custom-call(f32[8,8,2048]{2,1,0:T(8,128)S(1)} %get-tuple-element.39.second, f32[8,8,2048]{2,1,0:T(8,128)S(1)} %copy-done.3, f32[8,8,2048]{2,1,0:T(8,128)S(1)} %copy-done.1), custom_call_target="tpu_custom_call" | custom-call | flops 10000000000 | bytes 10000000 | tf_op jit(solution)/shard_map/z_inner/pallas_call | solution.py:363
  18.6 0.0 collective-permute-done.6.core_side
  18.6 0.1 z_core.1.values
  18.7 0.0 collective-permute-done.5.courant_z
  18.8 3.1 %collective-permute-done.2.chip_side = f32[2,8,2048]{2,1,0:T(8,128)S(1)} collective-permute-done((f32[2,8,2048]{2,1,0:T(8,128)S(1)}, f32[2,8,2048]{2,1,0:T(8,128)S(1)}, u32[]{:S(2)}, u32[]{:S(2)}) %collective-permute-start.2) | collective-permute-done | bytes 131104 | tf_op jit(solution)/shard_map/ppermute | solution.py:339
  21.9 0.8 %z_chip.1 = f32[8,8,2048]{2,1,0:T(8,128)} custom-call(f32[2,8,2048]{2,1,0:T(8,128)S(1)} %get-tuple-element.30.chip, f32[2,8,2048]{2,1,0:T(8,128)S(1)} %collective-permute-done.2.chip_side, f32[9,8,2048]{2,1,0:T(8,128)S(1)} %get-tuple-element.40.inside, f32[8,2048]{1,0:T(8,128)S(1)} %get-tuple-element.38.own_z, ...), custom_call_target="tpu_custom_call", output_to_operand_aliasing={{}: (6, {})} | custom-call | tf_op jit(solution)/shard_map/z_chip/pallas_call | solution.py:381
Async XLA Ops:
  0.0 4.9 %copy-start.1 = (f32[8,8,2048]{2,1,0:T(8,128)S(1)}, f32[8,8,2048]{2,1,0:T(8,128)}, u32[]{:S(2)}) copy-start(f32[8,8,2048]{2,1,0:T(8,128)} %fraction.11) | copy-start | bytes 1572868
  0.0 4.9 %copy-start = (f32[8,8,2048]{2,1,0:T(8,128)S(1)}, f32[8,8,2048]{2,1,0:T(8,128)}, u32[]{:S(2)}) copy-start(f32[8,8,2048]{2,1,0:T(8,128)} %flow_x.7) | copy-start | bytes 1572868
  1.4 8.3 %collective-permute-start = (f32[3,2,2048]{2,1,0:T(2,128)S(1)}, f32[3,2,2048]{2,1,0:T(2,128)S(1)}, u32[]{:S(2)}, u32[]{:S(2)}) collective-permute-start(f32[3,2,2048]{2,1,0:T(2,128)S(1)} %get-tuple-element.27.near), channel_id=1, source_target_pairs={{0,16},{16,0},{32,48},{48,32},{64,80},{80,64},{96,112},{112,96},{1... | collective-permute-start | bytes 147464 | tf_op jit(solution)/shard_map/ppermute | solution.py:307
  3.8 6.3 %collective-permute-start.1 = (f32[3,2,2048]{2,1,0:T(2,128)S(1)}, f32[3,2,2048]{2,1,0:T(2,128)S(1)}, u32[]{:S(2)}, u32[]{:S(2)}) collective-permute-start(f32[3,2,2048]{2,1,0:T(2,128)S(1)} %get-tuple-element.28.far), channel_id=1, source_target_pairs={{0,240},{16,32},{32,16},{48,64},{64,48},{80,96},{96,80},{112,128},... | collective-permute-start | bytes 147464 | tf_op jit(solution)/shard_map/ppermute | solution.py:308
  5.2 10.6 %collective-permute-start.4 = (f32[9,2,2048]{2,1,0:T(2,128)S(1)}, f32[9,2,2048]{2,1,0:T(2,128)S(1)}, u32[]{:S(2)}, u32[]{:S(2)}) collective-permute-start(f32[9,2,2048]{2,1,0:T(2,128)S(1)} %get-tuple-element.35), channel_id=1, source_target_pairs={{0,240},{16,0},{32,16},{48,32},{64,48},{80,64},{96,80},{112,96},{1... | collective-permute-start | bytes 442376 | tf_op jit(solution)/shard_map/ppermute | solution.py:319
  10.0 6.3 %collective-permute-start.3 = (f32[6,2,2048]{2,1,0:T(2,128)S(1)}, f32[6,2,2048]{2,1,0:T(2,128)S(1)}, u32[]{:S(2)}, u32[]{:S(2)}) collective-permute-start(f32[6,2,2048]{2,1,0:T(2,128)S(1)} %get-tuple-element.32), channel_id=1, source_target_pairs={{0,16},{16,32},{32,48},{48,64},{64,80},{80,96},{96,112},{112,128},... | collective-permute-start | bytes 294920 | tf_op jit(solution)/shard_map/ppermute | solution.py:329
  10.3 11.6 %collective-permute-start.2 = (f32[2,8,2048]{2,1,0:T(8,128)S(1)}, f32[2,8,2048]{2,1,0:T(8,128)S(1)}, u32[]{:S(2)}, u32[]{:S(2)}) collective-permute-start(f32[2,8,2048]{2,1,0:T(8,128)S(1)} %get-tuple-element.30.chip), channel_id=1, source_target_pairs={{0,15},{1,2},{2,1},{3,4},{4,3},{5,6},{6,5},{7,8},{8,7},{9,10},{10,... | collective-permute-start | bytes 393224 | tf_op jit(solution)/shard_map/ppermute | solution.py:339
  13.9 2.4 %copy-start.2 = (f32[8,8,2048]{2,1,0:T(8,128)S(1)}, f32[8,8,2048]{2,1,0:T(8,128)}, u32[]{:S(2)}) copy-start(f32[8,8,2048]{2,1,0:T(8,128)} %flow_y.3) | copy-start | bytes 1572868
  13.9 4.9 %collective-permute-start.5 = (f32[8,2048]{1,0:T(8,128)S(1)}, f32[8,2048]{1,0:T(8,128)S(1)}, u32[]{:S(2)}, u32[]{:S(2)}) collective-permute-start(f32[8,2048]{1,0:T(8,128)S(1)} %get-tuple-element.38.own_z), channel_id=1, source_target_pairs={{0,15},{1,0},{2,1},{3,2},{4,3},{5,4},{6,5},{7,6},{8,7},{9,8},{10,9... | collective-permute-start | bytes 196616 | tf_op jit(solution)/shard_map/ppermute | solution.py:340
  16.3 1.0 %copy-start.3 = (f32[8,8,2048]{2,1,0:T(8,128)S(1)}, f32[8,8,2048]{2,1,0:T(8,128)}, u32[]{:S(2)}) copy-start(f32[8,8,2048]{2,1,0:T(8,128)} %flow_z.3) | copy-start | bytes 1572868
  17.0 1.6 %collective-permute-start.6 = (f32[3,8,2048]{2,1,0:T(8,128)S(1)}, f32[3,8,2048]{2,1,0:T(8,128)S(1)}, u32[]{:S(2)}, u32[]{:S(2)}) collective-permute-start(f32[3,8,2048]{2,1,0:T(8,128)S(1)} %get-tuple-element.41.core), channel_id=1, source_target_pairs={{0,1},{1,0},{2,3},{3,2},{4,5},{5,4},{6,7},{7,6},{8,9},{9,8},{10,11... | collective-permute-start | bytes 589832 | tf_op jit(solution)/shard_map/ppermute | solution.py:362
